TPU v7x, 128 devices: a whole 4x4x4 slice. The times are simulated.
128 devices in a mesh: dp: 8 (over x, core), fsdp: 16 (over y, z).
Axes of the slice: x: 4, y: 4, z: 4, core: 2. Of those that a mesh axis runs over, the one named last changes fastest.
Arguments:
- hidden_in: bfloat16 [1024, 128, 5120], P(('dp', 'fsdp')), may hold values from -6 to 6
- kv_weight: bfloat16 [5120, 1024], P('fsdp'), may hold values from -0.078125 to 0.078125
- ln_gain: float32 [5120], replicated, may hold values from 0.1 to 1.9
- k_gain: float32 [128], replicated, may hold values from 0.1 to 1.9
- cost_slots: int32 [128, 8], P(('dp', 'fsdp')), may hold values from 0 to 7, each once within a row
- lengths: int32 [1024], P(('dp', 'fsdp')), may hold values from 16 to 128
- rewards: int32 [1024], P(('dp', 'fsdp')), may hold values from 0 to 3
- group_ids: int32 [1024], P(('dp', 'fsdp')), may hold values from 0 to 63, as said below
- kv_cotangent: bfloat16 [1024, 128, 1024], P(('dp', 'fsdp')), may hold values from -16 to 16
Outputs:
- keys_values: bfloat16 [1024, 128, 1024], P(('dp', 'fsdp'))
- kv_grad: float32 [5120, 1024], P('fsdp')
Inputs may be any that keep to these rules, and one draw needn't show every extreme that they name: `group_ids`: each prompt has exactly 16 completions.
All inputs are finite; a program needn't handle non-finite values.
Results may differ from a plain program's by a relative error of at most 0.0058.
Values may be sent and summed in bfloat16 or wider, within the bound.
No kernel may reach another device: no remote copies, remote signals or barrier semaphores. Data moves between devices by JAX's collectives and lax.ppermute only.
A program may use at most 192 MiB of HBM per device.

v0:
```python
import jax
import jax.numpy as jnp
from jax import lax
from jax.sharding import PartitionSpec as P

HEAD_SIZE = 128
KEY_VALUE_HEADS = 4
GROUP = 16


EPS = 1e-06


def rms_scale(values, gain):
    return values * lax.rsqrt(jnp.mean(values * values, -1, keepdims=True) + EPS) * gain


def on_device(
    hidden_in, kv_weight, ln_gain, k_gain, cost_slots, lengths, rewards, group_ids, kv_cotangent
):
    seqs, rows, width = hidden_in.shape
    n_dp = lax.axis_size("dp")
    n_fsdp = lax.axis_size("fsdp")
    kv_cols = kv_weight.shape[1]
    key_columns = kv_cols // 2
    groups = n_dp * n_fsdp * seqs // GROUP
    row_total_count = seqs * rows
    scores = rewards.astype(jnp.float32)
    member = (group_ids[:, None] == jnp.arange(groups, dtype=jnp.int32)[None, :]).astype(
        jnp.float32
    )
    totals, squares = lax.psum(
        (jnp.sum(member * scores[:, None], 0), jnp.sum(member * (scores * scores)[:, None], 0)),
        ("dp", "fsdp"),
    )
    means = totals / GROUP
    spread = squares / GROUP - means * means
    own_mean = jnp.sum(member * means[None, :], 1)
    own_spread = jnp.sum(member * spread[None, :], 1)
    weight = (
        (scores - own_mean) / jnp.sqrt(jnp.maximum(own_spread, 1.0)) / lengths.astype(jnp.float32)
    )
    positions = jnp.arange(rows, dtype=jnp.int32)
    coef = jnp.where(positions[None, :] < lengths[:, None], weight[:, None], 0.0).astype(
        jnp.bfloat16
    )
    inverse = jnp.argsort(cost_slots[0])
    send_tokens = jnp.take(hidden_in, inverse, axis=0)
    send_coef = jnp.take(coef, inverse, axis=0)
    token_block, coef_block = (
        lax.all_to_all(send_tokens, "dp", split_axis=0, concat_axis=0, tiled=True),
        lax.all_to_all(send_coef, "dp", split_axis=0, concat_axis=0, tiled=True),
    )
    normed = rms_scale(
        token_block.reshape(row_total_count, width).astype(jnp.float32), ln_gain
    ).astype(jnp.bfloat16)
    columns = normed
    key_value_before_norm = jnp.dot(
        columns,
        lax.all_gather(kv_weight, "fsdp", axis=0, tiled=True),
        preferred_element_type=jnp.float32,
    )
    keys_before_norm = key_value_before_norm[:, :key_columns].reshape(
        row_total_count, KEY_VALUE_HEADS, HEAD_SIZE
    )

    def key_norm(values):
        return rms_scale(values, k_gain)

    keys, backward_pass = jax.vjp(key_norm, keys_before_norm)
    local_kv = jnp.concatenate(
        [keys.reshape(row_total_count, key_columns), key_value_before_norm[:, key_columns:]], 1
    ).astype(jnp.bfloat16)
    keys_values = local_kv.reshape(seqs, rows, kv_cols)
    incoming_gradient = kv_cotangent.reshape(row_total_count, kv_cols).astype(jnp.float32)
    (key_gradient,) = backward_pass(
        incoming_gradient[:, :key_columns].reshape(row_total_count, KEY_VALUE_HEADS, HEAD_SIZE)
    )
    row_coef = coef_block.reshape(row_total_count).astype(jnp.float32)
    scaled = (
        jnp.concatenate(
            [
                key_gradient.reshape(row_total_count, key_columns),
                incoming_gradient[:, key_columns:],
            ],
            1,
        )
        * row_coef[:, None]
    ).astype(jnp.bfloat16)
    columns = normed
    grad_local = lax.psum_scatter(
        lax.dot_general(
            columns, scaled, (((0,), (0,)), ((), ())), preferred_element_type=jnp.float32
        ),
        "fsdp",
        scatter_dimension=0,
        tiled=True,
    )
    kv_grad = lax.psum(grad_local, "dp")
    return (keys_values, kv_grad)


def solution(mesh):
    in_specs = (
        P(("dp", "fsdp"), None, None),
        P("fsdp", None),
        P(),
        P(),
        P(("dp", "fsdp"), None),
        P(("dp", "fsdp")),
        P(("dp", "fsdp")),
        P(("dp", "fsdp")),
        P(("dp", "fsdp"), None, None),
    )
    out_specs = (P(("dp", "fsdp"), None, None), P("fsdp", None))
    return jax.shard_map(
        on_device, mesh=mesh, in_specs=in_specs, out_specs=out_specs, check_vma=False
    )
```

profile of v0, /device:TPU:1, one launch (start us, length us, event | category | flops | bytes accessed | tf_op | source)
XLA Modules:
  0.0 494.9 jit_solution(3863205117243874348)
XLA Ops:
  7.2 0.0 all-gather.2.cloned.1.call-start
  7.2 0.7 all-gather.2.cloned.1.call-update
  7.9 0.7 convert_element_type.49
  8.6 1.6 sort.17
  10.2 0.7 convert_multiply_fusion
  10.8 0.7 select_reduce_fusion.3
  11.6 69.9 %all-reduce = (f32[64]{0:T(128)S(1)}, f32[64]{0:T(128)S(1)}) all-reduce(f32[64]{0:T(128)S(1)} %get-tuple-element.8, f32[64]{0:T(128)S(1)} %get-tuple-element.9), channel_id=1, replica_groups=mesh['dp'=8,'fsdp'=16] {'dp','fsdp'}, use_global_device_ids=true, to_apply=%region_5.0 | all-reduce | flops 128 | bytes 1024 | tf_op jit(solution)/shard_map/psum | solution.py:32
  81.5 0.9 select_reduce_fusion.2
  82.4 0.7 convert_divide_fusion
  83.1 0.7 select_convert_fusion
  83.8 0.6 gather_fusion.1
  84.4 0.1 bitcast_select_fusion
  84.5 0.6 copy.20
  85.1 4.3 all-to-all-start.1
  89.3 9.5 %gather_fusion = bf16[8,128,5120]{2,1,0:T(8,128)(2,1)} fusion(bf16[8,128,5120]{2,1,0:T(8,128)(2,1)} %param.9, s32[1024]{0:T(1024)S(1)} %pad_clamp_fusion), kind=kCustom, calls=%fused_computation | custom fusion | bytes 20971552 | tf_op jit(solution)/shard_map/jit(_take)/gather | solution.py:48
  98.8 8.9 %broadcast_select_fusion = bf16[8,128,5120]{2,1,0:T(8,128)(2,1)} fusion(bf16[8,128,5120]{2,1,0:T(8,128)(2,1)} %gather_fusion, pred[8]{0:T(512)(128)(4,1)S(1)} %compare_and_fusion), kind=kLoop, calls=%fused_computation.6 | loop fusion | flops 5242880 | bytes 20971528 | tf_op jit(solution)/shard_map/jit(_take)/select_n | solution.py:48
  107.7 5.3 %all-to-all-start = ((bf16[8,128,5120]{2,1,0:T(8,128)(2,1)}), bf16[8,128,5120]{2,1,0:T(8,128)(2,1)}, u32[]{:S(2)}, u32[]{:S(2)}) async-start(bf16[8,128,5120]{2,1,0:T(8,128)(2,1)} %broadcast_select_fusion), calls=%async_computation | async-start | bytes 20971520 | tf_op jit(solution)/shard_map/all_to_all | solution.py:51
  113.0 0.2 reduce-scatter.2.cloned.1.call-start
  113.2 0.6 bitcast_convert_fusion
  113.8 2.0 copy-done
  115.8 0.2 slice.23
  116.0 1.8 reshape.110
  117.7 0.0 copy-start.4
  117.7 111.5 %all-to-all-done = bf16[8,128,5120]{2,1,0:T(8,128)(2,1)} async-done(((bf16[8,128,5120]{2,1,0:T(8,128)(2,1)}), bf16[8,128,5120]{2,1,0:T(8,128)(2,1)}, u32[]{:S(2)}, u32[]{:S(2)}) %all-to-all-start) | async-done | bytes 10485792 | tf_op jit(solution)/shard_map/all_to_all | solution.py:51
  229.3 6.1 %multiply_reduce_fusion = f32[8,128]{1,0:T(8,128)S(1)} fusion(bf16[8,128,5120]{2,1,0:T(8,128)(2,1)} %all-to-all-done), kind=kLoop, calls=%fused_computation.5 | loop fusion | flops 15727616 | bytes 10489856 | tf_op jit(solution)/shard_map/reduce_sum | solution.py:15
  235.4 10.9 %fusion.1 = bf16[1024,5120]{1,0:T(8,128)(2,1)} fusion(f32[5120]{0:T(1024)S(1)} %copy-done.4, f32[1024]{0:T(1024)S(1)} %rsqrt_bitcast_fusion, bf16[8,128,5120]{2,1,0:T(8,128)(2,1)} %all-to-all-done), kind=kLoop, calls=%fused_computation.4 | loop fusion | flops 20971520 | bytes 20996096 | tf_op jit(solution)/shard_map/convert_element_type | solution.py:56
  246.2 15.4 %fusion.10 = f32[1024,1024]{1,0:T(8,128)S(1)} fusion(bf16[1024,5120]{1,0:T(8,128)(2,1)} %fusion.1, bf16[5120,1024]{1,0:T(8,128)(2,1)} %all-gather.2.cloned.1.call-done), kind=kOutput, calls=%fused_computation.43 | convolution fusion | flops 10737418240 | bytes 25165824 | tf_op jit(solution)/shard_map/dot_general | solution.py:58
  261.6 2.0 copy-done.2
  263.6 0.2 slice.21
  263.8 1.7 reshape.109
  265.5 4.7 multiply_reduce_fusion.1
  270.2 0.2 copy.18
  270.4 0.2 copy.16
  270.6 0.2 copy.19
  270.8 0.2 copy.17
  271.1 0.0 slice-start.1
  271.1 1.2 broadcast_in_dim.56
  272.3 1.5 mul.140
  273.8 4.3 add_add_fusion
  278.1 15.6 %fusion.3 = f32[5120,1024]{1,0:T(8,128)} fusion(bf16[1024,5120]{1,0:T(8,128)(2,1)S(1)} %bitcast.38, f32[1024,512]{1,0:T(8,128)} %get-tuple-element.14, f32[1024,512]{1,0:T(8,128)S(1)} %get-tuple-element.12, f32[1024]{0:T(1024)S(1)} %bitcast.43), kind=kOutput, calls=%fused_computation.10 | convolution fusion | flops 10740563968 | bytes 35655680 | tf_op jit(solution)/shard_map/dot_general | solution.py:92
  293.8 0.0 reduce-scatter.2.cloned.1.call-update
  293.8 0.0 all-reduce.3.cloned.1.call-start
  293.8 128.8 %reduce-scatter.2.cloned.1.call-done = f32[320,1024]{1,0:T(8,128)} async-done(((f32[5120,1024]{1,0:T(8,128)}), f32[320,1024]{1,0:T(8,128)}) %reduce-scatter.2.cloned.1.call-update) | async-done | bytes 1310736 | tf_op jit(solution)/shard_map/reduce_scatter | solution.py:91
  422.6 0.0 all-reduce.3.cloned.1.call-update
  422.6 1.7 slice.29
  424.4 1.6 pad_maximum_fusion
  426.0 59.9 %all-reduce.3.cloned.1.call-done = f32[320,1024]{1,0:T(8,128)} async-done(((f32[320,1024]{1,0:T(8,128)}), f32[320,1024]{1,0:T(8,128)}) %all-reduce.3.cloned.1.call-update) | async-done | bytes 1310736 | tf_op jit(solution)/shard_map/psum | solution.py:99
  485.8 2.5 copy.27
  (26 shorter events, 0.1 us)
Async XLA Ops:
  7.2 239.1 %all-gather.2.cloned.1.call-start = ((), (), s32[]{:S(2)}) async-start(), calls=%async_computation.3 | async-start | bytes 11141120 | tf_op jit(solution)/shard_map/all_gather | solution.py:60
  85.1 22.6 %all-to-all-start.1 = ((bf16[8,1,128]{2,1,0:T(2,128)(2,1)}), bf16[8,1,128]{2,1,0:T(2,128)(2,1)S(1)}, u32[]{:S(2)}, u32[]{:S(2)}) async-start(bf16[8,1,128]{2,1,0:T(2,128)(2,1)} %copy.20), calls=%async_computation.1 | async-start | bytes 8192 | tf_op jit(solution)/shard_map/all_to_all | solution.py:52
  107.7 5.5 %copy-start.3 = (bf16[8,128,1024]{2,1,0:T(8,128)(2,1)S(1)}, bf16[8,128,1024]{2,1,0:T(8,128)(2,1)}, u32[]{:S(2)}) copy-start(bf16[8,128,1024]{2,1,0:T(8,128)(2,1)} %param.17) | copy-start | bytes 6291460
  107.7 121.6 %all-to-all-start = ((bf16[8,128,5120]{2,1,0:T(8,128)(2,1)}), bf16[8,128,5120]{2,1,0:T(8,128)(2,1)}, u32[]{:S(2)}, u32[]{:S(2)}) async-start(bf16[8,128,5120]{2,1,0:T(8,128)(2,1)} %broadcast_select_fusion), calls=%async_computation | async-start | bytes 20971520 | tf_op jit(solution)/shard_map/all_to_all | solution.py:51
  113.0 309.7 %reduce-scatter.2.cloned.1.call-start = ((), (), s32[]{:S(2)}) async-start(), calls=%async_computation.4 | async-start | bytes 22282240 | tf_op jit(solution)/shard_map/reduce_scatter | solution.py:91
  113.8 2.0 copy-start
  115.8 1.9 copy-start.5
  117.7 117.6 %copy-start.4 = (f32[5120]{0:T(1024)S(1)}, f32[5120]{0:T(1024)}, u32[]{:S(2)}) copy-start(f32[5120]{0:T(1024)} %param.11) | copy-start | bytes 61444
  261.6 2.0 copy-start.2
  265.5 12.6 %slice-start = ((s8[10485760]{0:T(1024)(128)(4,1)}), s8[2097152]{0:T(1024)(128)(4,1)S(1)}, s32[]{:S(2)}) async-start(s8[10485760]{0:T(1024)(128)(4,1)} %bitcast.37), calls=%async_computation.6 | async-start | bytes 4194304
  271.1 2.7 copy-start.1
  271.1 7.0 %slice-start.1 = ((s8[10485760]{0:T(1024)(128)(4,1)}), s8[4194304]{0:T(1024)(128)(4,1)S(1)}, s32[]{:S(2)}) async-start(s8[10485760]{0:T(1024)(128)(4,1)} %bitcast.37), calls=%async_computation.7 | async-start | bytes 8388608
  273.8 4.3 slice-start.2
  293.8 192.0 %all-reduce.3.cloned.1.call-start = ((), (), s32[]{:S(2)}) async-start(), calls=%async_computation.5 | async-start | bytes 2621440 | tf_op jit(solution)/shard_map/psum | solution.py:99
Sparse Core Ops, SparseCore 0:
  10.2 84.9 all-gather.1
  293.9 128.6 reduce-scatter.1
  425.0 60.8 all-reduce.2
where the time goes:
time: 497 us; the launch traced here: 495 us
  waiting for transfers between devices  301 us (61%)
  blocking collectives  69.9 us (14%)
  other arithmetic  43 us (9%)
  matrix products  31 us (6%)
  local copies, waits for them, and re-layouts  26.2 us (5%)
  between operations  13.9 us (3%)
  starting transfers between devices  9.83 us (2%)
    reduce_scatter x1, waiting for transfers between devices, on_device(): lax.psum_scatter(lax.dot_general(columns, scaled, (((0,), (0,)), ((), ())...  129 us
    all_to_all x1, waiting for transfers between devices, on_device(): lax.all_to_all(send_tokens, 'dp', split_axis=0, concat_axis=0, tiled=True)  112 us
    psum x1, blocking collectives, on_device(): lax.psum((jnp.sum(member * scores[:, None], 0), jnp.sum(member * (scores...  69.9 us
    psum x1, waiting for transfers between devices, on_device(): kv_grad = lax.psum(grad_local, 'dp')  59.9 us
    dot_general x1, matrix products, on_device(): lax.dot_general(columns, scaled, (((0,), (0,)), ((), ())), preferred_elem...  15.6 us
    dot_general x1, matrix products, on_device(): jnp.dot(columns, lax.all_gather(kv_weight, 'fsdp', axis=0, tiled=True), p...  15.4 us
    convert_element_type x1, other arithmetic, on_device(): normed = rms_scale(token_block.reshape(row_total_count, width).astype(jnp...  10.9 us
  transfers between devices with their start and end apart: 5, of which 3 were waited for; matrix products, arithmetic and copies ran while one was open for 10% of the time, Pallas kernels for 0%

commit v1 on v0

v1 whole, which is shorter than its diff:
```python
import functools

import jax
import jax.numpy as jnp
from jax import lax
from jax.experimental import pallas as pl
from jax.experimental.pallas import tpu as pltpu
from jax.sharding import PartitionSpec as P

HEAD = 128
GROUP = 16
GROUPS = 64
EPS = 1e-06
SEQS = 8
ROWS = 128
WIDTH = 5120
BLOCK = 320
QUARTER = 1280
HALF = 256
TOKENS = SEQS * ROWS
MIB = 1 << 20

bf16, f32 = jnp.bfloat16, jnp.float32


def ring_yz(dy, dz):
    return [
        (y * 4 + z, ((y + dy) % 4) * 4 + (z + dz) % 4) for y in range(4) for z in range(4)
    ]


def ring_x(dx, flip=0):
    return [(x * 2 + c, ((x + dx) % 4) * 2 + (c ^ flip)) for x in range(4) for c in range(2)]


def along_y(value, step):
    return lax.ppermute(value, "fsdp", ring_yz(step, 0))


def along_z(value, step):
    return lax.ppermute(value, "fsdp", ring_yz(0, step))


def along_x(value, step):
    return lax.ppermute(value, "dp", ring_x(step))


def to_partner(value):
    return lax.ppermute(value, "dp", ring_x(0, 1))


def norm_kernel(order_ref, hidden_ref, gain_ref, rows_ref, columns_ref):
    values = hidden_ref[0].astype(f32)
    mean = jnp.sum(values * values, -1, keepdims=True) * (1.0 / WIDTH)
    normed = (values * lax.rsqrt(mean + EPS) * gain_ref[...]).astype(bf16)
    rows_ref[...] = normed
    columns_ref[...] = normed.T


def norm_call(order, hidden_in, ln_gain):
    return pl.pallas_call(
        norm_kernel,
        grid_spec=pltpu.PrefetchScalarGridSpec(
            num_scalar_prefetch=1,
            grid=(SEQS,),
            in_specs=[
                pl.BlockSpec((1, ROWS, WIDTH), lambda i, o: (o[i], 0, 0)),
                pl.BlockSpec((1, WIDTH), lambda i, o: (0, 0)),
            ],
            out_specs=[
                pl.BlockSpec((ROWS, WIDTH), lambda i, o: (i, 0)),
                pl.BlockSpec((WIDTH, ROWS), lambda i, o: (0, i)),
            ],
        ),
        out_shape=[
            jax.ShapeDtypeStruct((TOKENS, WIDTH), bf16),
            jax.ShapeDtypeStruct((WIDTH, TOKENS), bf16),
        ],
        compiler_params=pltpu.CompilerParams(vmem_limit_bytes=40 * MIB),
        cost_estimate=pl.CostEstimate(
            flops=8 * TOKENS * WIDTH, bytes_accessed=6 * TOKENS * WIDTH, transcendentals=0
        ),
        name="input_norm",
    )(order, hidden_in, ln_gain.reshape(1, WIDTH))


STEP = 512
STEPS = 2 * TOKENS // STEP


def project_kernel(
    place_ref, length_ref, weight_ref, gain_ref, cot_ref, own_ref, partner_ref,
    a0, a1, a2, a3, b0, b1, b2, b3,
    kv_ref, scaled_ref, w_ref, buf_ref, acc_ref, w_sem, buf_sem,
):
    i = pl.program_id(0)
    y, z = place_ref[1], place_ref[2]

    def w_copies():
        out = []
        for k, (a, b) in enumerate(zip((a0, a1, a2, a3), (b0, b1, b2, b3))):
            for r in range(4):
                ya, za = lax.rem(y + 4 - k, 4), lax.rem(z + 4 - r, 4)
                yb, zb = lax.rem(y + 4 - r, 4), lax.rem(z + 4 - k, 4)
                for src, yy, zz, col in ((a, ya, za, 0), (b, yb, zb, HALF)):
                    row = pl.multiple_of((yy * 4 + zz) * BLOCK, BLOCK)
                    out.append(
                        pltpu.make_async_copy(
                            src.at[r], w_ref.at[pl.ds(row, BLOCK), pl.ds(col, HALF)], w_sem
                        )
                    )
        return out

    def block_copy(source, j, slot):
        return pltpu.make_async_copy(
            source.at[pl.ds(pl.multiple_of(j * STEP, STEP), STEP)],
            buf_ref.at[slot],
            buf_sem.at[slot],
        )

    def start_block(j, slot):
        @pl.when(j < STEPS // 2)
        def _():
            block_copy(own_ref, j, slot).start()

        @pl.when(j >= STEPS // 2)
        def _():
            block_copy(partner_ref, j - STEPS // 2, slot).start()

    @pl.when(i == 0)
    def _():
        for copy in w_copies():
            copy.start()
        start_block(0, 0)
        start_block(1, 1)
        for copy in w_copies():
            copy.wait()

    slot = lax.rem(i, 2)
    block_copy(own_ref, 0, slot).wait()

    acc_ref[...] = jnp.dot(buf_ref[slot], w_ref[...], preferred_element_type=f32)

    @pl.when(i + 2 < STEPS)
    def _():
        start_block(i + 2, slot)

    gain = gain_ref[...]
    rows = lax.broadcasted_iota(jnp.int32, (ROWS, 1), 0)
    for q in range(STEP // ROWS):
        n = i * (STEP // ROWS) + q
        coef = jnp.where(rows < length_ref[n], weight_ref[n], 0.0)
        coef = coef.astype(bf16).astype(f32)
        span = pl.ds(q * ROWS, ROWS)
        for head in range(HALF // HEAD):
            columns = pl.ds(head * HEAD, HEAD)
            keys = acc_ref[span, columns]
            scale = lax.rsqrt(jnp.mean(keys * keys, -1, keepdims=True) + EPS)
            unit = keys * scale
            kv_ref[q, 0, :, columns] = (unit * gain).astype(bf16)
            slope = cot_ref[q, 0, :, columns].astype(f32) * gain
            inner = jnp.mean(unit * slope, -1, keepdims=True)
            scaled_ref[span, columns] = ((slope - unit * inner) * scale * coef).astype(bf16)
        columns = pl.ds(HALF, HALF)
        kv_ref[q, 0, :, columns] = acc_ref[span, columns].astype(bf16)
        scaled_ref[span, columns] = (cot_ref[q, 0, :, columns].astype(f32) * coef).astype(bf16)


def project_call(place, lengths, weights, k_gain, cotangent, own, partner, a, b):
    per = STEP // ROWS
    spot = lambda i, p, l, w: (lax.rem(i, 2), lax.rem(lax.div(i, 2) + p[0], 2), 0, 0)
    any_spec = pl.BlockSpec(memory_space=pl.ANY)
    return pl.pallas_call(
        project_kernel,
        grid_spec=pltpu.PrefetchScalarGridSpec(
            num_scalar_prefetch=3,
            grid=(STEPS,),
            in_specs=[
                pl.BlockSpec((1, HEAD), lambda i, p, l, w: (0, 0)),
                pl.BlockSpec((per, 1, ROWS, 2 * HALF), spot),
            ]
            + [any_spec] * 10,
            out_specs=[
                pl.BlockSpec((per, 1, ROWS, 2 * HALF), spot),
                pl.BlockSpec((STEP, 2 * HALF), lambda i, p, l, w: (i, 0)),
            ],
            scratch_shapes=[
                pltpu.VMEM((WIDTH, 2 * HALF), bf16),
                pltpu.VMEM((2, STEP, WIDTH), bf16),
                pltpu.VMEM((STEP, 2 * HALF), f32),
                pltpu.SemaphoreType.DMA,
                pltpu.SemaphoreType.DMA((2,)),
            ],
        ),
        out_shape=[
            jax.ShapeDtypeStruct((SEQS, 2, ROWS, 2 * HALF), bf16),
            jax.ShapeDtypeStruct((2 * TOKENS, 2 * HALF), bf16),
        ],
        compiler_params=pltpu.CompilerParams(vmem_limit_bytes=50 * MIB),
        cost_estimate=pl.CostEstimate(
            flops=4 * TOKENS * WIDTH * 2 * HALF,
            bytes_accessed=4 * TOKENS * WIDTH + 12 * MIB,
            transcendentals=0,
        ),
        name="project",
    )(place, lengths, weights, k_gain.reshape(1, HEAD), cotangent, own, partner, *a, *b)


def gradient_kernel(place_ref, ao_ref, ap_ref, bo_ref, bp_ref, scaled_ref, a_ref, b_ref):
    for own, partner, cols, out in (
        (ao_ref, ap_ref, pl.ds(0, HALF), a_ref),
        (bo_ref, bp_ref, pl.ds(HALF, HALF), b_ref),
    ):
        total = jnp.dot(
            own[0, 0], scaled_ref[pl.ds(0, TOKENS), cols], preferred_element_type=f32
        ) + jnp.dot(
            partner[0, 0], scaled_ref[pl.ds(TOKENS, TOKENS), cols], preferred_element_type=f32
        )
        out[0] = total.astype(bf16)


def gradient_call(step, place, own, partner, scaled):
    def a_spot(i, p):
        return (lax.rem(p[1] + step, 4), lax.rem(p[2] + i, 4), 0, 0)

    def b_spot(i, p):
        return (lax.rem(p[1] + i, 4), lax.rem(p[2] + step, 4), 0, 0)

    block = (1, 1, BLOCK, TOKENS)
    out = pl.BlockSpec((1, BLOCK, HALF), lambda i, p: (i, 0, 0))
    return pl.pallas_call(
        gradient_kernel,
        grid_spec=pltpu.PrefetchScalarGridSpec(
            num_scalar_prefetch=1,
            grid=(4,),
            in_specs=[
                pl.BlockSpec(block, a_spot),
                pl.BlockSpec(block, a_spot),
                pl.BlockSpec(block, b_spot),
                pl.BlockSpec(block, b_spot),
                pl.BlockSpec((2 * TOKENS, 2 * HALF), lambda i, p: (0, 0)),
            ],
            out_specs=[out, out],
        ),
        out_shape=[jax.ShapeDtypeStruct((4, BLOCK, HALF), bf16)] * 2,
        compiler_params=pltpu.CompilerParams(vmem_limit_bytes=40 * MIB),
        cost_estimate=pl.CostEstimate(
            flops=TOKENS * WIDTH * 2 * HALF,
            bytes_accessed=2 * TOKENS * WIDTH + 4 * MIB,
            transcendentals=0,
        ),
        name="weight_gradient",
    )(place, own, partner, own, partner, scaled)


def group_statistics(rewards, group_ids):
    scores = rewards.astype(f32)
    member = (group_ids[:, None] == jnp.arange(GROUPS, dtype=jnp.int32)[None, :]).astype(f32)
    sums = jnp.stack(
        [jnp.sum(member * scores[:, None], 0), jnp.sum(member * (scores * scores)[:, None], 0)]
    ).reshape(1, 1, 2 * GROUPS)
    for axis in ("dp", "fsdp"):
        count = lax.axis_size(axis)
        sums = lax.all_to_all(
            jnp.broadcast_to(sums, (count, 1, 2 * GROUPS)), axis, 0, 0, tiled=True
        ).sum(0, keepdims=True)
    totals, squares = sums[0, 0, :GROUPS], sums[0, 0, GROUPS:]
    means = totals / GROUP
    spread = squares / GROUP - means * means
    own_mean = jnp.sum(member * means[None, :], 1)
    own_spread = jnp.sum(member * spread[None, :], 1)
    return (scores - own_mean) / jnp.sqrt(jnp.maximum(own_spread, 1.0))


def gathered(block, first, second):
    stage = jnp.stack([block, first(block, 1), first(block, 2), first(block, 3)])
    return [stage, second(stage, 1), second(stage, 2), second(stage, 3)]


def on_device(
    hidden_in, kv_weight, ln_gain, k_gain, cost_slots, lengths, rewards, group_ids, kv_cotangent
):
    place_f = lax.axis_index("fsdp")
    y, z = lax.div(place_f, 4), lax.rem(place_f, 4)
    core = lax.rem(lax.axis_index("dp"), 2)
    place = jnp.stack([core, y, z]).astype(jnp.int32)

    by_core = kv_weight.reshape(BLOCK, 2, 2, HALF)
    mine = jnp.where(core == 0, by_core[:, :, 0], by_core[:, :, 1])
    weights_a = gathered(mine[:, 0], along_z, along_y)
    weights_b = gathered(mine[:, 1], along_y, along_z)

    cot_send = (
        kv_cotangent.reshape(4, 2, ROWS, 2, 2, HALF)
        .transpose(0, 4, 1, 2, 3, 5)
        .reshape(SEQS, 2, ROWS, 2 * HALF)
    )
    cot = lax.all_to_all(cot_send, "dp", split_axis=0, concat_axis=0, tiled=True)

    slots = cost_slots[0]
    index = jnp.arange(SEQS, dtype=jnp.int32)
    hit = slots[None, :] == index[:, None]
    order = jnp.sum(jnp.where(hit, index[None, :], 0), 1).astype(jnp.int32)

    normed, normed_t = norm_call(order, hidden_in, ln_gain)
    partner, partner_t = to_partner(normed), to_partner(normed_t)

    weight = group_statistics(rewards, group_ids) / lengths.astype(f32)
    sent = jnp.stack([weight, lengths.astype(f32)])
    sent = jnp.sum(jnp.where(hit[None], sent[:, None, :], 0.0), 2)
    both = jnp.concatenate([sent, to_partner(sent)], 1)

    kv_send, scaled = project_call(
        place, both[1].astype(jnp.int32), both[0], k_gain, cot, normed, partner,
        weights_a, weights_b,
    )

    kv = lax.all_to_all(kv_send, "dp", split_axis=0, concat_axis=0, tiled=True)
    keys_values = (
        kv.reshape(4, 2, 2, ROWS, 2, HALF).transpose(0, 2, 3, 4, 1, 5).reshape(SEQS, ROWS, 4 * HALF)
    )

    own_t = normed_t.reshape(4, 4, BLOCK, TOKENS)
    partner_t = partner_t.reshape(4, 4, BLOCK, TOKENS)
    parts = {k: gradient_call(k, place, own_t, partner_t, scaled) for k in (2, 1, 3, 0)}
    sum_a = sum(along_y(parts[k][0], k).astype(f32) for k in (2, 1, 3)) + parts[0][0].astype(f32)
    sum_b = sum(along_z(parts[k][1], k).astype(f32) for k in (2, 1, 3)) + parts[0][1].astype(f32)
    sum_a = sum(along_z(sum_a[k].astype(bf16), k).astype(f32) for k in (2, 1, 3)) + sum_a[0]
    sum_b = sum(along_y(sum_b[k].astype(bf16), k).astype(f32) for k in (2, 1, 3)) + sum_b[0]
    rows = jnp.stack([sum_a, sum_b], 1)
    rows_sent = rows.astype(bf16)
    ahead = [rows_sent.astype(f32)] + [along_x(rows_sent, k).astype(f32) for k in (1, 2, 3)]
    rows = (ahead[0] + ahead[2]) + (ahead[1] + ahead[3])
    other = to_partner(rows)
    kv_grad = jnp.where(
        core == 0, jnp.stack([rows, other], 2), jnp.stack([other, rows], 2)
    ).reshape(BLOCK, 4 * HALF)
    return keys_values, kv_grad


def solution(mesh):
    in_specs = (
        P(("dp", "fsdp"), None, None),
        P("fsdp", None),
        P(),
        P(),
        P(("dp", "fsdp"), None),
        P(("dp", "fsdp")),
        P(("dp", "fsdp")),
        P(("dp", "fsdp")),
        P(("dp", "fsdp"), None, None),
    )
    out_specs = (P(("dp", "fsdp"), None, None), P("fsdp", None))
    return jax.shard_map(
        on_device, mesh=mesh, in_specs=in_specs, out_specs=out_specs, check_vma=False
    )
```

time: 497 us -> 262 us (0.53)
  waiting for transfers between devices: 301 us -> 76.5 us
  blocking collectives: 69.9 us -> 0 us
  starting transfers between devices: 9.83 us -> 74.1 us
  Pallas kernels: 0 us -> 60 us
  other arithmetic: 43 us -> 4.72 us
  matrix products: 31 us -> 0 us
  local copies, waits for them, and re-layouts: 26.2 us -> 44.5 us
  between operations: 13.9 us -> 0.99 us
    reduce_scatter x1 -> x0, waiting for transfers between devices: 129 us -> none  [on_device(): lax.psum_scatter(lax.dot_general(columns, scaled, (((0,), (0,)), ((), ())...]
    all_to_all x2 -> x4, waiting for transfers between devices: 112 us -> 5.84 us  [the longest x2 5.83 us: group_statistics(): lax.all_to_all(jnp.broadcast_to(sums, (count, 1, 2 * GROUPS)), axis, 0, 0...]
    ppermute x0 -> x31, waiting for transfers between devices: none -> 70.7 us  [the longest x12 30 us: along_z(): return lax.ppermute(value, 'fsdp', ring_yz(0, step))]
    psum x1 -> x0, blocking collectives: 69.9 us -> none  [on_device(): lax.psum((jnp.sum(member * scores[:, None], 0), jnp.sum(member * (scores...]
    pallas_call x0 -> x6, Pallas kernels: none -> 60 us  [the longest x4 26.1 us: gradient_call(): pl.pallas_call(gradient_kernel, grid_spec=pltpu.PrefetchScalarGridSpec(nu...]
    psum x1 -> x0, waiting for transfers between devices: 59.9 us -> none  [on_device(): kv_grad = lax.psum(grad_local, 'dp')]
    ppermute x0 -> x31, starting transfers between devices: none -> 50.2 us  [the longest x12 21 us: along_z(): return lax.ppermute(value, 'fsdp', ring_yz(0, step))]
    dot_general x2 -> x0, matrix products: 31 us -> none  [the longest x1 15.6 us: on_device(): lax.dot_general(columns, scaled, (((0,), (0,)), ((), ())), preferred_elem...]
  transfers between devices with their start and end apart: 5 -> 35, of which waited for: 3 -> 17; matrix products, arithmetic and copies ran while one was open for 10% -> 7% of each run, Pallas kernels for 0% -> 15%
where the time goes in v1:
time: 262 us; the launch traced here: 261 us
  waiting for transfers between devices  76.5 us (29%)
  starting transfers between devices  74.1 us (28%)
  Pallas kernels  60 us (23%)
  local copies, waits for them, and re-layouts  44.5 us (17%)
  other arithmetic  4.72 us (2%)
    ppermute x12, waiting for transfers between devices, along_z(): return lax.ppermute(value, 'fsdp', ring_yz(0, step))  30 us
    ppermute x12, waiting for transfers between devices, along_y(): return lax.ppermute(value, 'fsdp', ring_yz(step, 0))  28 us
    pallas_call x4, Pallas kernels, gradient_call(): pl.pallas_call(gradient_kernel, grid_spec=pltpu.PrefetchScalarGridSpec(nu...  26.1 us
    ppermute x12, starting transfers between devices, along_z(): return lax.ppermute(value, 'fsdp', ring_yz(0, step))  21 us
    pallas_call x1, Pallas kernels, project_call(): pl.pallas_call(project_kernel, grid_spec=pltpu.PrefetchScalarGridSpec(num...  19.1 us
    ppermute x12, starting transfers between devices, along_y(): return lax.ppermute(value, 'fsdp', ring_yz(step, 0))  19 us
    unnamed x56, local copies, waits for them, and re-layouts  18.3 us
    pallas_call x1, Pallas kernels, norm_call(): pl.pallas_call(norm_kernel, grid_spec=pltpu.PrefetchScalarGridSpec(num_sc...  14.8 us
  transfers between devices with their start and end apart: 35, of which 17 were waited for; matrix products, arithmetic and copies ran while one was open for 7% of the time, Pallas kernels for 15%

profile of v1, /device:TPU:1, one launch (start us, length us, event | category | flops | bytes accessed | tf_op | source)
XLA Modules:
  0.0 260.8 jit_solution(11479229132228769917)
XLA Ops:
  2.1 14.8 %input_norm.1 = (bf16[1024,5120]{1,0:T(8,128)(2,1)}, bf16[5120,1024]{1,0:T(8,128)(2,1)}) custom-call(s32[8]{0:T(128)S(1)} %select_reduce_fusion.1.order_ref, bf16[8,128,5120]{2,1,0:T(8,128)(2,1)} %hidden_ref.1, f32[1,5120]{1,0:T(1,128)S(1)} %bitcast.93), custom_call_target="tpu_custom_call" | custom-call | flops 41943040 | bytes 31457280 | tf_op jit(solution)/shard_map/input_norm/pallas_call | solution.py:61
  16.9 1.4 collective-permute-start.1
  19.2 4.9 %all-to-all-start = ((f32[8,1,128]{2,1,0:T(1,128)}), f32[8,1,128]{2,1,0:T(1,128)S(1)}, u32[]{:S(2)}, u32[]{:S(2)}) async-start(f32[8,1,128]{2,1,0:T(1,128)} %broadcast_in_dim.60), calls=%async_computation | async-start | bytes 8192 | tf_op jit(solution)/shard_map/all_to_all | solution.py:264
  25.6 2.8 %collective-permute-start.10 = (bf16[320,256]{1,0:T(8,128)(2,1)S(1)}, bf16[320,256]{1,0:T(8,128)(2,1)S(1)}, u32[]{:S(2)}, u32[]{:S(2)}) collective-permute-start(bf16[320,256]{1,0:T(8,128)(2,1)S(1)} %get-tuple-element.44), channel_id=1, source_target_pairs={{0,12},{1,13},{2,14},{3,15},{4,0},{5,1},{6,2},{7,3},{8,4},{9,5},{1... | collective-permute-start | bytes 491528 | tf_op jit(solution)/shard_map/ppermute | solution.py:37
  28.4 5.8 %all-to-all-done = f32[8,1,128]{2,1,0:T(1,128)S(1)} async-done(((f32[8,1,128]{2,1,0:T(1,128)}), f32[8,1,128]{2,1,0:T(1,128)S(1)}, u32[]{:S(2)}, u32[]{:S(2)}) %all-to-all-start) | async-done | bytes 4128 | tf_op jit(solution)/shard_map/all_to_all | solution.py:264
  34.9 7.9 %all-to-all-start.1 = ((f32[16,1,128]{2,1,0:T(1,128)}), f32[16,1,128]{2,1,0:T(1,128)S(1)}, u32[]{:S(2)}, u32[]{:S(2)}) async-start(f32[16,1,128]{2,1,0:T(1,128)} %broadcast_in_dim.61), calls=%async_computation.1 | async-start | bytes 16384 | tf_op jit(solution)/shard_map/all_to_all | solution.py:264
  42.8 2.8 %reshape.102 = bf16[4,2,128,2,2,256]{5,4,3,2,1,0:T(2,128)(2,1)} reshape(bf16[8,128,1024]{2,1,0:T(8,128)(2,1)S(1)} %copy-done.17) | data formatting | bytes 4194304 | tf_op jit(solution)/shard_map/reshape | solution.py:294
  45.5 3.4 %copy.37 = bf16[4,2,128,2,2,256]{5,3,2,1,4,0:T(2,128)(2,1)S(1)} copy(bf16[4,2,128,2,2,256]{5,4,3,2,1,0:T(2,128)(2,1)} %reshape.102) | data formatting | bytes 4194304 | tf_op jit(solution)/shard_map/reshape | solution.py:294
  48.9 2.6 %reshape.103 = bf16[8,2,128,512]{3,2,1,0:T(8,128)(2,1)} reshape(bf16[4,2,2,128,2,256]{5,4,3,2,1,0:T(2,128)(2,1)S(1)} %bitcast.95) | data formatting | bytes 4194304 | tf_op jit(solution)/shard_map/reshape | solution.py:296
  51.5 4.9 %all-to-all-start.2 = ((bf16[8,2,128,512]{3,2,1,0:T(8,128)(2,1)}), bf16[8,2,128,512]{3,2,1,0:T(8,128)(2,1)}, u32[]{:S(2)}, u32[]{:S(2)}) async-start(bf16[8,2,128,512]{3,2,1,0:T(8,128)(2,1)} %reshape.103), calls=%async_computation.2 | async-start | bytes 4194304 | tf_op jit(solution)/shard_map/all_to_all | solution.py:298
  56.9 3.2 %collective-permute-start.9 = (bf16[320,256]{1,0:T(8,128)(2,1)S(1)}, bf16[320,256]{1,0:T(8,128)(2,1)S(1)}, u32[]{:S(2)}, u32[]{:S(2)}) collective-permute-start(bf16[320,256]{1,0:T(8,128)(2,1)S(1)} %get-tuple-element.44), channel_id=1, source_target_pairs={{0,8},{1,9},{2,10},{3,11},{4,12},{5,13},{6,14},{7,15},{8,0},{9,1},... | collective-permute-start | bytes 491528 | tf_op jit(solution)/shard_map/ppermute | solution.py:37
  60.4 2.4 collective-permute-start.4
  62.8 1.5 collective-permute-done.9
  64.3 2.8 %collective-permute-start.3 = (bf16[320,256]{1,0:T(8,128)(2,1)S(1)}, bf16[320,256]{1,0:T(8,128)(2,1)S(1)}, u32[]{:S(2)}, u32[]{:S(2)}) collective-permute-start(bf16[320,256]{1,0:T(8,128)(2,1)S(1)} %get-tuple-element.43), channel_id=1, source_target_pairs={{0,2},{1,3},{2,0},{3,1},{4,6},{5,7},{6,4},{7,5},{8,10},{9,11},{10,... | collective-permute-start | bytes 491528 | tf_op jit(solution)/shard_map/ppermute | solution.py:41
  67.8 1.5 collective-permute-start.2
  70.7 2.4 collective-permute-start.12
  73.1 1.3 collective-permute-done.2
  76.5 9.3 %collective-permute-done.13.b3 = bf16[4,320,256]{2,1,0:T(8,128)(2,1)} collective-permute-done((bf16[4,320,256]{2,1,0:T(8,128)(2,1)S(1)}, bf16[4,320,256]{2,1,0:T(8,128)(2,1)}, u32[]{:S(2)}, u32[]{:S(2)}) %collective-permute-start.13) | collective-permute-done | bytes 655392 | tf_op jit(solution)/shard_map/ppermute | solution.py:41
  85.8 1.6 collective-permute-start.7
  88.1 2.9 %collective-permute-start.6 = (bf16[4,320,256]{2,1,0:T(8,128)(2,1)S(1)}, bf16[4,320,256]{2,1,0:T(8,128)(2,1)S(1)}, u32[]{:S(2)}, u32[]{:S(2)}) collective-permute-start(bf16[4,320,256]{2,1,0:T(8,128)(2,1)S(1)} %pad_maximum_fusion.a0), channel_id=1, source_target_pairs={{0,8},{1,9},{2,10},{3,11},{4,12},{5,13},{6,14},{7,15},{8,0},{9,1},... | collective-permute-start | bytes 1966088 | tf_op jit(solution)/shard_map/ppermute | solution.py:37
  91.0 13.5 %collective-permute-done.11.b1 = bf16[4,320,256]{2,1,0:T(8,128)(2,1)S(1)} collective-permute-done((bf16[4,320,256]{2,1,0:T(8,128)(2,1)S(1)}, bf16[4,320,256]{2,1,0:T(8,128)(2,1)S(1)}, u32[]{:S(2)}, u32[]{:S(2)}) %collective-permute-start.11) | collective-permute-done | bytes 655392 | tf_op jit(solution)/shard_map/ppermute | solution.py:41
  109.0 19.0 %collective-permute-done.5.a1 = bf16[4,320,256]{2,1,0:T(8,128)(2,1)S(1)} collective-permute-done((bf16[4,320,256]{2,1,0:T(8,128)(2,1)S(1)}, bf16[4,320,256]{2,1,0:T(8,128)(2,1)S(1)}, u32[]{:S(2)}, u32[]{:S(2)}) %collective-permute-start.5) | collective-permute-done | bytes 655392 | tf_op jit(solution)/shard_map/ppermute | solution.py:37
  130.2 1.3 copy-done.6
  135.8 19.1 %project.1 = (bf16[8,2,128,512]{3,2,1,0:T(8,128)(2,1)}, bf16[2048,512]{1,0:T(8,128)(2,1)}) custom-call(s32[3]{0:T(128)S(1)} %pad_add_fusion.place_ref, s32[16]{0:T(128)S(1)} %get-tuple-element.47.length_ref, f32[16]{0:T(128)S(1)} %get-tuple-element.46.weight_ref, f32[1,128]{1,0:T(1,128)S(1)} %bitcast.94, bf16[8,2,128,512]{3,2,1,0:T(8,128)(2,1)} %all-to-all-done.2.cot_ref, ...), custom_call_target="tpu_custom_call" | custom-call | flops 10737418240 | bytes 33554432 | tf_op jit(solution)/shard_map/project/pallas_call | solution.py:173
  154.9 1.6 copy-done.1
  156.5 6.6 %weight_gradient.6 = (bf16[4,320,256]{2,1,0:T(8,128)(2,1)S(1)}, bf16[4,320,256]{2,1,0:T(8,128)(2,1)}) custom-call(s32[3]{0:T(128)S(1)} %pad_add_fusion.place_ref, bf16[4,4,320,1024]{3,2,1,0:T(8,128)(2,1)S(1)} %bitcast.85, bf16[4,4,320,1024]{3,2,1,0:T(8,128)(2,1)} %bitcast.31.ap_ref.bp_ref, bf16[4,4,320,1024]{3,2,1,0:T(8,128)(2,1)S(1)} %bitcast.86, ...), custom_call_target="tpu_custom_call" | custom-call | flops 2684354560 | bytes 14680064 | tf_op jit(solution)/shard_map/weight_gradient/pallas_call | solution.py:231
  163.1 6.4 %collective-permute-start.23 = (bf16[4,320,256]{2,1,0:T(8,128)(2,1)}, bf16[4,320,256]{2,1,0:T(8,128)(2,1)}, u32[]{:S(2)}, u32[]{:S(2)}) collective-permute-start(bf16[4,320,256]{2,1,0:T(8,128)(2,1)} %get-tuple-element.24), channel_id=1, source_target_pairs={{0,3},{1,0},{2,1},{3,2},{4,7},{5,4},{6,5},{7,6},{8,11},{9,8},{10,9... | collective-permute-start | bytes 1966088 | tf_op jit(solution)/shard_map/ppermute | solution.py:41
  169.5 6.8 %weight_gradient.5 = (bf16[4,320,256]{2,1,0:T(8,128)(2,1)}, bf16[4,320,256]{2,1,0:T(8,128)(2,1)}) custom-call(s32[3]{0:T(128)S(1)} %pad_add_fusion.place_ref, bf16[4,4,320,1024]{3,2,1,0:T(8,128)(2,1)S(1)} %bitcast.87, bf16[4,4,320,1024]{3,2,1,0:T(8,128)(2,1)} %bitcast.31.ap_ref.bp_ref, bf16[4,4,320,1024]{3,2,1,0:T(8,128)(2,1)S(1)} %bitcast.88, ...), custom_call_target="tpu_custom_call" | custom-call | flops 2684354560 | bytes 14680064 | tf_op jit(solution)/shard_map/weight_gradient/pallas_call | solution.py:231
  176.3 1.5 collective-permute-start.16
  177.7 6.8 %weight_gradient.4 = (bf16[4,320,256]{2,1,0:T(8,128)(2,1)}, bf16[4,320,256]{2,1,0:T(8,128)(2,1)}) custom-call(s32[3]{0:T(128)S(1)} %pad_add_fusion.place_ref, bf16[4,4,320,1024]{3,2,1,0:T(8,128)(2,1)S(1)} %bitcast.89, bf16[4,4,320,1024]{3,2,1,0:T(8,128)(2,1)} %bitcast.31.ap_ref.bp_ref, bf16[4,4,320,1024]{3,2,1,0:T(8,128)(2,1)S(1)} %bitcast.90, ...), custom_call_target="tpu_custom_call" | custom-call | flops 2684354560 | bytes 14680064 | tf_op jit(solution)/shard_map/weight_gradient/pallas_call | solution.py:231
  184.5 2.8 %collective-permute-start.15 = (bf16[4,320,256]{2,1,0:T(8,128)(2,1)}, bf16[4,320,256]{2,1,0:T(8,128)(2,1)}, u32[]{:S(2)}, u32[]{:S(2)}) collective-permute-start(bf16[4,320,256]{2,1,0:T(8,128)(2,1)} %get-tuple-element.18), channel_id=1, source_target_pairs={{0,8},{1,9},{2,10},{3,11},{4,12},{5,13},{6,14},{7,15},{8,0},{9,1},... | collective-permute-start | bytes 1966088 | tf_op jit(solution)/shard_map/ppermute | solution.py:37
  188.5 6.3 %all-to-all-start.3 = ((bf16[8,2,128,512]{3,2,1,0:T(8,128)(2,1)}), bf16[8,2,128,512]{3,2,1,0:T(8,128)(2,1)}, u32[]{:S(2)}, u32[]{:S(2)}) async-start(bf16[8,2,128,512]{3,2,1,0:T(8,128)(2,1)} %get-tuple-element.15), calls=%async_computation.3 | async-start | bytes 4194304 | tf_op jit(solution)/shard_map/all_to_all | solution.py:318
  194.8 4.0 %copy-done = bf16[5120,1024]{1,0:T(8,128)(2,1)S(1)} copy-done((bf16[5120,1024]{1,0:T(8,128)(2,1)S(1)}, bf16[5120,1024]{1,0:T(8,128)(2,1)}, u32[]{:S(2)}) %copy-start) | copy-done | bytes 10485784
  198.8 6.0 %weight_gradient.7 = (bf16[4,320,256]{2,1,0:T(8,128)(2,1)S(1)}, bf16[4,320,256]{2,1,0:T(8,128)(2,1)S(1)}) custom-call(s32[3]{0:T(128)S(1)} %pad_add_fusion.place_ref, bf16[4,4,320,1024]{3,2,1,0:T(8,128)(2,1)S(1)} %bitcast.91, bf16[4,4,320,1024]{3,2,1,0:T(8,128)(2,1)} %bitcast.31.ap_ref.bp_ref, bf16[4,4,320,1024]{3,2,1,0:T(8,128)(2,1)S(1)} %bitcast.92, ...), custom_call_target="tpu_custom_call" | custom-call | flops 2684354560 | bytes 14680064 | tf_op jit(solution)/shard_map/weight_gradient/pallas_call | solution.py:231
  204.8 3.8 %collective-permute-done.15 = bf16[4,320,256]{2,1,0:T(8,128)(2,1)} collective-permute-done((bf16[4,320,256]{2,1,0:T(8,128)(2,1)}, bf16[4,320,256]{2,1,0:T(8,128)(2,1)}, u32[]{:S(2)}, u32[]{:S(2)}) %collective-permute-start.15) | collective-permute-done | bytes 655392 | tf_op jit(solution)/shard_map/ppermute | solution.py:37
  208.7 2.6 fusion.8
  213.2 2.7 %collective-permute-start.24 = (bf16[320,256]{1,0:T(8,128)(2,1)S(1)}, bf16[320,256]{1,0:T(8,128)(2,1)S(1)}, u32[]{:S(2)}, u32[]{:S(2)}) collective-permute-start(bf16[320,256]{1,0:T(8,128)(2,1)S(1)} %get-tuple-element.37), channel_id=1, source_target_pairs={{0,8},{1,9},{2,10},{3,11},{4,12},{5,13},{6,14},{7,15},{8,0},{9,1},... | collective-permute-start | bytes 491528 | tf_op jit(solution)/shard_map/ppermute | solution.py:37
  218.4 2.9 %collective-permute-done.19 = bf16[320,256]{1,0:T(8,128)(2,1)S(1)} collective-permute-done((bf16[320,256]{1,0:T(8,128)(2,1)S(1)}, bf16[320,256]{1,0:T(8,128)(2,1)S(1)}, u32[]{:S(2)}, u32[]{:S(2)}) %collective-permute-start.19) | collective-permute-done | bytes 163872 | tf_op jit(solution)/shard_map/ppermute | solution.py:41
  221.4 2.9 %collective-permute-done.25 = bf16[320,256]{1,0:T(8,128)(2,1)S(1)} collective-permute-done((bf16[320,256]{1,0:T(8,128)(2,1)S(1)}, bf16[320,256]{1,0:T(8,128)(2,1)S(1)}, u32[]{:S(2)}, u32[]{:S(2)}) %collective-permute-start.25) | collective-permute-done | bytes 163872 | tf_op jit(solution)/shard_map/ppermute | solution.py:37
  225.5 2.6 collective-permute-start.27
  229.1 2.5 collective-permute-done.28
  231.6 7.5 %collective-permute-done.27 = bf16[320,2,256]{2,0,1:T(8,128)(2,1)S(1)} collective-permute-done((bf16[320,2,256]{2,0,1:T(8,128)(2,1)S(1)}, bf16[320,2,256]{2,0,1:T(8,128)(2,1)S(1)}, u32[]{:S(2)}, u32[]{:S(2)}) %collective-permute-start.27) | collective-permute-done | bytes 327712 | tf_op jit(solution)/shard_map/ppermute | solution.py:45
  240.2 4.0 %collective-permute-start.30 = (f32[320,2,256]{2,0,1:T(8,128)S(1)}, f32[320,2,256]{2,0,1:T(8,128)S(1)}, u32[]{:S(2)}, u32[]{:S(2)}) collective-permute-start(f32[320,2,256]{2,0,1:T(8,128)S(1)} %add_add_fusion), channel_id=1, source_target_pairs={{0,16},{16,0},{32,48},{48,32},{64,80},{80,64},{96,112},{112,96},{1... | collective-permute-start | bytes 1966088 | tf_op jit(solution)/shard_map/ppermute | solution.py:49
  244.3 1.7 collective-permute-done.30
  247.1 2.1 select_n.38
  249.2 2.5 reshape.106
  251.8 4.6 %copy.28 = bf16[4,2,128,2,2,256]{5,4,3,2,1,0:T(2,128)(2,1)} copy(bf16[4,2,128,2,2,256]{5,3,2,1,4,0:T(2,128)(2,1)S(1)} %bitcast.96) | data formatting | bytes 4194304 | tf_op jit(solution)/shard_map/transpose | solution.py:320
  256.4 4.4 %reshape.107 = bf16[8,128,1024]{2,1,0:T(8,128)(2,1)} reshape(bf16[4,2,128,2,2,256]{5,4,3,2,1,0:T(2,128)(2,1)} %copy.28) | data formatting | bytes 4194304 | tf_op jit(solution)/shard_map/reshape | solution.py:320
  (128 shorter events, 31.5 us)
Async XLA Ops:
  2.1 16.2 %copy-start.23 = (s32[8]{0:T(128)S(1)}, s32[8]{0:T(128)}, u32[]{:S(2)}) copy-start(s32[8]{0:T(128)} %param.15) | copy-start | bytes 100
  2.1 16.2 %copy-start.21 = (s32[8]{0:T(128)S(1)}, s32[8]{0:T(128)}, u32[]{:S(2)}) copy-start(s32[8]{0:T(128)} %param.16) | copy-start | bytes 100
  2.1 21.9 %copy-start.20 = (bf16[320,1024]{1,0:T(8,128)(2,1)S(1)}, bf16[320,1024]{1,0:T(8,128)(2,1)}, u32[]{:S(2)}) copy-start(bf16[320,1024]{1,0:T(8,128)(2,1)} %param.10) | copy-start | bytes 1966084
  16.9 112.0 %collective-permute-start.1 = (bf16[1024,5120]{1,0:T(8,128)(2,1)}, bf16[1024,5120]{1,0:T(8,128)(2,1)}, u32[]{:S(2)}, u32[]{:S(2)}) collective-permute-start(bf16[1024,5120]{1,0:T(8,128)(2,1)} %get-tuple-element.14.own_ref), channel_id=1, source_target_pairs={{0,16},{16,0},{32,48},{48,32},{64,80},{80,64},{96,112},{112,96},{1... | collective-permute-start | bytes 31457288 | tf_op jit(solution)/shard_map/ppermute | solution.py:49
  18.3 136.5 %collective-permute-start.14 = (bf16[5120,1024]{1,0:T(8,128)(2,1)}, bf16[5120,1024]{1,0:T(8,128)(2,1)}, u32[]{:S(2)}, u32[]{:S(2)}) collective-permute-start(bf16[5120,1024]{1,0:T(8,128)(2,1)} %get-tuple-element.16), channel_id=1, source_target_pairs={{0,16},{16,0},{32,48},{48,32},{64,80},{80,64},{96,112},{112,96},{1... | collective-permute-start | bytes 31457288 | tf_op jit(solution)/shard_map/ppermute | solution.py:49
  19.2 15.1 %all-to-all-start = ((f32[8,1,128]{2,1,0:T(1,128)}), f32[8,1,128]{2,1,0:T(1,128)S(1)}, u32[]{:S(2)}, u32[]{:S(2)}) async-start(f32[8,1,128]{2,1,0:T(1,128)} %broadcast_in_dim.60), calls=%async_computation | async-start | bytes 8192 | tf_op jit(solution)/shard_map/all_to_all | solution.py:264
  25.4 3.0 %copy-start.24 = (s32[1,8]{1,0:T(1,128)S(1)}, s32[1,8]{1,0:T(1,128)}, u32[]{:S(2)}) copy-start(s32[1,8]{1,0:T(1,128)} %param.13) | copy-start | bytes 100
  25.4 17.3 %copy-start.22 = (s32[8]{0:T(128)S(1)}, s32[8]{0:T(128)}, u32[]{:S(2)}) copy-start(s32[8]{0:T(128)} %param.14) | copy-start | bytes 100
  25.5 17.3 %copy-start.17 = (bf16[8,128,1024]{2,1,0:T(8,128)(2,1)S(1)}, bf16[8,128,1024]{2,1,0:T(8,128)(2,1)}, u32[]{:S(2)}) copy-start(bf16[8,128,1024]{2,1,0:T(8,128)(2,1)} %param.17) | copy-start | bytes 6291460
  25.6 34.7 %collective-permute-start.10 = (bf16[320,256]{1,0:T(8,128)(2,1)S(1)}, bf16[320,256]{1,0:T(8,128)(2,1)S(1)}, u32[]{:S(2)}, u32[]{:S(2)}) collective-permute-start(bf16[320,256]{1,0:T(8,128)(2,1)S(1)} %get-tuple-element.44), channel_id=1, source_target_pairs={{0,12},{1,13},{2,14},{3,15},{4,0},{5,1},{6,2},{7,3},{8,4},{9,5},{1... | collective-permute-start | bytes 491528 | tf_op jit(solution)/shard_map/ppermute | solution.py:37
  34.9 16.6 %all-to-all-start.1 = ((f32[16,1,128]{2,1,0:T(1,128)}), f32[16,1,128]{2,1,0:T(1,128)S(1)}, u32[]{:S(2)}, u32[]{:S(2)}) async-start(f32[16,1,128]{2,1,0:T(1,128)} %broadcast_in_dim.61), calls=%async_computation.1 | async-start | bytes 16384 | tf_op jit(solution)/shard_map/all_to_all | solution.py:264
  51.5 77.4 %all-to-all-start.2 = ((bf16[8,2,128,512]{3,2,1,0:T(8,128)(2,1)}), bf16[8,2,128,512]{3,2,1,0:T(8,128)(2,1)}, u32[]{:S(2)}, u32[]{:S(2)}) async-start(bf16[8,2,128,512]{3,2,1,0:T(8,128)(2,1)} %reshape.103), calls=%async_computation.2 | async-start | bytes 4194304 | tf_op jit(solution)/shard_map/all_to_all | solution.py:298
  56.8 3.3 %collective-permute-start = (f32[2,8]{1,0:T(2,128)S(1)}, f32[2,8]{1,0:T(2,128)S(1)}, u32[]{:S(2)}, u32[]{:S(2)}) collective-permute-start(f32[2,8]{1,0:T(2,128)S(1)} %select_reduce_fusion), channel_id=1, source_target_pairs={{0,16},{16,0},{32,48},{48,32},{64,80},{80,64},{96,112},{112,96},{1... | collective-permute-start | bytes 200 | tf_op jit(solution)/shard_map/ppermute | solution.py:49
  56.9 7.4 %collective-permute-start.9 = (bf16[320,256]{1,0:T(8,128)(2,1)S(1)}, bf16[320,256]{1,0:T(8,128)(2,1)S(1)}, u32[]{:S(2)}, u32[]{:S(2)}) collective-permute-start(bf16[320,256]{1,0:T(8,128)(2,1)S(1)} %get-tuple-element.44), channel_id=1, source_target_pairs={{0,8},{1,9},{2,10},{3,11},{4,12},{5,13},{6,14},{7,15},{8,0},{9,1},... | collective-permute-start | bytes 491528 | tf_op jit(solution)/shard_map/ppermute | solution.py:37
  60.1 7.8 %collective-permute-start.8 = (bf16[320,256]{1,0:T(8,128)(2,1)S(1)}, bf16[320,256]{1,0:T(8,128)(2,1)S(1)}, u32[]{:S(2)}, u32[]{:S(2)}) collective-permute-start(bf16[320,256]{1,0:T(8,128)(2,1)S(1)} %get-tuple-element.44), channel_id=1, source_target_pairs={{0,4},{1,5},{2,6},{3,7},{4,8},{5,9},{6,10},{7,11},{8,12},{9,13},{1... | collective-permute-start | bytes 491528 | tf_op jit(solution)/shard_map/ppermute | solution.py:37
  60.4 9.1 %collective-permute-start.4 = (bf16[320,256]{1,0:T(8,128)(2,1)S(1)}, bf16[320,256]{1,0:T(8,128)(2,1)S(1)}, u32[]{:S(2)}, u32[]{:S(2)}) collective-permute-start(bf16[320,256]{1,0:T(8,128)(2,1)S(1)} %get-tuple-element.43), channel_id=1, source_target_pairs={{0,3},{1,0},{2,1},{3,2},{4,7},{5,4},{6,5},{7,6},{8,11},{9,8},{10,9... | collective-permute-start | bytes 491528 | tf_op jit(solution)/shard_map/ppermute | solution.py:41
  64.3 6.4 %collective-permute-start.3 = (bf16[320,256]{1,0:T(8,128)(2,1)S(1)}, bf16[320,256]{1,0:T(8,128)(2,1)S(1)}, u32[]{:S(2)}, u32[]{:S(2)}) collective-permute-start(bf16[320,256]{1,0:T(8,128)(2,1)S(1)} %get-tuple-element.43), channel_id=1, source_target_pairs={{0,2},{1,3},{2,0},{3,1},{4,6},{5,7},{6,4},{7,5},{8,10},{9,11},{10,... | collective-permute-start | bytes 491528 | tf_op jit(solution)/shard_map/ppermute | solution.py:41
  67.8 6.6 %collective-permute-start.2 = (bf16[320,256]{1,0:T(8,128)(2,1)S(1)}, bf16[320,256]{1,0:T(8,128)(2,1)S(1)}, u32[]{:S(2)}, u32[]{:S(2)}) collective-permute-start(bf16[320,256]{1,0:T(8,128)(2,1)S(1)} %get-tuple-element.43), channel_id=1, source_target_pairs={{0,1},{1,2},{2,3},{3,0},{4,5},{5,6},{6,7},{7,4},{8,9},{9,10},{10,1... | collective-permute-start | bytes 491528 | tf_op jit(solution)/shard_map/ppermute | solution.py:41
  69.3 59.6 %copy-start.16 = (f32[128]{0:T(128)S(1)}, f32[128]{0:T(128)}, u32[]{:S(2)}) copy-start(f32[128]{0:T(128)} %param.12) | copy-start | bytes 1540
  69.4 16.4 %collective-permute-start.13 = (bf16[4,320,256]{2,1,0:T(8,128)(2,1)S(1)}, bf16[4,320,256]{2,1,0:T(8,128)(2,1)}, u32[]{:S(2)}, u32[]{:S(2)}) collective-permute-start(bf16[4,320,256]{2,1,0:T(8,128)(2,1)S(1)} %pad_maximum_fusion.1.b0), channel_id=1, source_target_pairs={{0,3},{1,0},{2,1},{3,2},{4,7},{5,4},{6,5},{7,6},{8,11},{9,8},{10,9... | collective-permute-start | bytes 1966088 | tf_op jit(solution)/shard_map/ppermute | solution.py:41
  70.7 17.4 %collective-permute-start.12 = (bf16[4,320,256]{2,1,0:T(8,128)(2,1)S(1)}, bf16[4,320,256]{2,1,0:T(8,128)(2,1)}, u32[]{:S(2)}, u32[]{:S(2)}) collective-permute-start(bf16[4,320,256]{2,1,0:T(8,128)(2,1)S(1)} %pad_maximum_fusion.1.b0), channel_id=1, source_target_pairs={{0,2},{1,3},{2,0},{3,1},{4,6},{5,7},{6,4},{7,5},{8,10},{9,11},{10,... | collective-permute-start | bytes 1966088 | tf_op jit(solution)/shard_map/ppermute | solution.py:41
  74.4 30.0 %collective-permute-start.11 = (bf16[4,320,256]{2,1,0:T(8,128)(2,1)S(1)}, bf16[4,320,256]{2,1,0:T(8,128)(2,1)S(1)}, u32[]{:S(2)}, u32[]{:S(2)}) collective-permute-start(bf16[4,320,256]{2,1,0:T(8,128)(2,1)S(1)} %pad_maximum_fusion.1.b0), channel_id=1, source_target_pairs={{0,1},{1,2},{2,3},{3,0},{4,5},{5,6},{6,7},{7,4},{8,9},{9,10},{10,1... | collective-permute-start | bytes 1966088 | tf_op jit(solution)/shard_map/ppermute | solution.py:41
  85.8 21.5 %collective-permute-start.7 = (bf16[4,320,256]{2,1,0:T(8,128)(2,1)S(1)}, bf16[4,320,256]{2,1,0:T(8,128)(2,1)S(1)}, u32[]{:S(2)}, u32[]{:S(2)}) collective-permute-start(bf16[4,320,256]{2,1,0:T(8,128)(2,1)S(1)} %pad_maximum_fusion.a0), channel_id=1, source_target_pairs={{0,12},{1,13},{2,14},{3,15},{4,0},{5,1},{6,2},{7,3},{8,4},{9,5},{1... | collective-permute-start | bytes 1966088 | tf_op jit(solution)/shard_map/ppermute | solution.py:37
  88.1 20.1 %collective-permute-start.6 = (bf16[4,320,256]{2,1,0:T(8,128)(2,1)S(1)}, bf16[4,320,256]{2,1,0:T(8,128)(2,1)S(1)}, u32[]{:S(2)}, u32[]{:S(2)}) collective-permute-start(bf16[4,320,256]{2,1,0:T(8,128)(2,1)S(1)} %pad_maximum_fusion.a0), channel_id=1, source_target_pairs={{0,8},{1,9},{2,10},{3,11},{4,12},{5,13},{6,14},{7,15},{8,0},{9,1},... | collective-permute-start | bytes 1966088 | tf_op jit(solution)/shard_map/ppermute | solution.py:37
  105.3 22.7 %collective-permute-start.5 = (bf16[4,320,256]{2,1,0:T(8,128)(2,1)S(1)}, bf16[4,320,256]{2,1,0:T(8,128)(2,1)S(1)}, u32[]{:S(2)}, u32[]{:S(2)}) collective-permute-start(bf16[4,320,256]{2,1,0:T(8,128)(2,1)S(1)} %pad_maximum_fusion.a0), channel_id=1, source_target_pairs={{0,4},{1,5},{2,6},{3,7},{4,8},{5,9},{6,10},{7,11},{8,12},{9,13},{1... | collective-permute-start | bytes 1966088 | tf_op jit(solution)/shard_map/ppermute | solution.py:37
  128.9 26.0 %slice-start = ((s8[10485760]{0:T(1024)(128)(4,1)}), s8[4194304]{0:T(1024)(128)(4,1)S(1)}, s32[]{:S(2)}) async-start(s8[10485760]{0:T(1024)(128)(4,1)} %bitcast.83), calls=%async_computation.4 | async-start | bytes 8388608
  135.8 19.1 %slice-start.1 = ((s8[10485760]{0:T(1024)(128)(4,1)}), s8[4194304]{0:T(1024)(128)(4,1)S(1)}, s32[]{:S(2)}) async-start(s8[10485760]{0:T(1024)(128)(4,1)} %bitcast.83), calls=%async_computation.5 | async-start | bytes 8388608
  135.8 19.1 %slice-start.2 = ((s8[10485760]{0:T(1024)(128)(4,1)}), s8[2097152]{0:T(1024)(128)(4,1)S(1)}, s32[]{:S(2)}) async-start(s8[10485760]{0:T(1024)(128)(4,1)} %bitcast.83), calls=%async_computation.6 | async-start | bytes 4194304
  163.1 24.2 %collective-permute-start.17 = (bf16[4,320,256]{2,1,0:T(8,128)(2,1)S(1)}, bf16[4,320,256]{2,1,0:T(8,128)(2,1)S(1)}, u32[]{:S(2)}, u32[]{:S(2)}) collective-permute-start(bf16[4,320,256]{2,1,0:T(8,128)(2,1)S(1)} %get-tuple-element.20), channel_id=1, source_target_pairs={{0,12},{1,13},{2,14},{3,15},{4,0},{5,1},{6,2},{7,3},{8,4},{9,5},{1... | collective-permute-start | bytes 1966088 | tf_op jit(solution)/shard_map/ppermute | solution.py:37
  163.1 41.7 %collective-permute-start.23 = (bf16[4,320,256]{2,1,0:T(8,128)(2,1)}, bf16[4,320,256]{2,1,0:T(8,128)(2,1)}, u32[]{:S(2)}, u32[]{:S(2)}) collective-permute-start(bf16[4,320,256]{2,1,0:T(8,128)(2,1)} %get-tuple-element.24), channel_id=1, source_target_pairs={{0,3},{1,0},{2,1},{3,2},{4,7},{5,4},{6,5},{7,6},{8,11},{9,8},{10,9... | collective-permute-start | bytes 1966088 | tf_op jit(solution)/shard_map/ppermute | solution.py:41
  176.3 28.5 %collective-permute-start.16 = (bf16[4,320,256]{2,1,0:T(8,128)(2,1)}, bf16[4,320,256]{2,1,0:T(8,128)(2,1)}, u32[]{:S(2)}, u32[]{:S(2)}) collective-permute-start(bf16[4,320,256]{2,1,0:T(8,128)(2,1)} %get-tuple-element.19), channel_id=1, source_target_pairs={{0,4},{1,5},{2,6},{3,7},{4,8},{5,9},{6,10},{7,11},{8,12},{9,13},{1... | collective-permute-start | bytes 1966088 | tf_op jit(solution)/shard_map/ppermute | solution.py:37
  177.7 27.1 %collective-permute-start.22 = (bf16[4,320,256]{2,1,0:T(8,128)(2,1)}, bf16[4,320,256]{2,1,0:T(8,128)(2,1)}, u32[]{:S(2)}, u32[]{:S(2)}) collective-permute-start(bf16[4,320,256]{2,1,0:T(8,128)(2,1)} %get-tuple-element.23), channel_id=1, source_target_pairs={{0,1},{1,2},{2,3},{3,0},{4,5},{5,6},{6,7},{7,4},{8,9},{9,10},{10,1... | collective-permute-start | bytes 1966088 | tf_op jit(solution)/shard_map/ppermute | solution.py:41
  184.5 24.2 %collective-permute-start.15 = (bf16[4,320,256]{2,1,0:T(8,128)(2,1)}, bf16[4,320,256]{2,1,0:T(8,128)(2,1)}, u32[]{:S(2)}, u32[]{:S(2)}) collective-permute-start(bf16[4,320,256]{2,1,0:T(8,128)(2,1)} %get-tuple-element.18), channel_id=1, source_target_pairs={{0,8},{1,9},{2,10},{3,11},{4,12},{5,13},{6,14},{7,15},{8,0},{9,1},... | collective-permute-start | bytes 1966088 | tf_op jit(solution)/shard_map/ppermute | solution.py:37
  187.3 21.3 %collective-permute-start.21 = (bf16[4,320,256]{2,1,0:T(8,128)(2,1)}, bf16[4,320,256]{2,1,0:T(8,128)(2,1)}, u32[]{:S(2)}, u32[]{:S(2)}) collective-permute-start(bf16[4,320,256]{2,1,0:T(8,128)(2,1)} %get-tuple-element.22), channel_id=1, source_target_pairs={{0,2},{1,3},{2,0},{3,1},{4,6},{5,7},{6,4},{7,5},{8,10},{9,11},{10,... | collective-permute-start | bytes 1966088 | tf_op jit(solution)/shard_map/ppermute | solution.py:41
  188.5 6.3 %copy-start.2 = (bf16[2048,512]{1,0:T(8,128)(2,1)S(1)}, bf16[2048,512]{1,0:T(8,128)(2,1)}, u32[]{:S(2)}) copy-start(bf16[2048,512]{1,0:T(8,128)(2,1)} %get-tuple-element.17.scaled_ref) | copy-start | bytes 6291460
  188.5 60.7 %all-to-all-start.3 = ((bf16[8,2,128,512]{3,2,1,0:T(8,128)(2,1)}), bf16[8,2,128,512]{3,2,1,0:T(8,128)(2,1)}, u32[]{:S(2)}, u32[]{:S(2)}) async-start(bf16[8,2,128,512]{3,2,1,0:T(8,128)(2,1)} %get-tuple-element.15), calls=%async_computation.3 | async-start | bytes 4194304 | tf_op jit(solution)/shard_map/all_to_all | solution.py:318
  194.8 4.0 %copy-start = (bf16[5120,1024]{1,0:T(8,128)(2,1)S(1)}, bf16[5120,1024]{1,0:T(8,128)(2,1)}, u32[]{:S(2)}) copy-start(bf16[5120,1024]{1,0:T(8,128)(2,1)} %get-tuple-element.16) | copy-start | bytes 31457284
  198.8 9.9 %copy-start.19 = (bf16[4,320,256]{2,1,0:T(8,128)(2,1)S(1)}, bf16[4,320,256]{2,1,0:T(8,128)(2,1)}, u32[]{:S(2)}) copy-start(bf16[4,320,256]{2,1,0:T(8,128)(2,1)} %copy-done.18) | copy-start | bytes 1966084
  211.3 6.2 %collective-permute-start.18 = (bf16[320,256]{1,0:T(8,128)(2,1)S(1)}, bf16[320,256]{1,0:T(8,128)(2,1)S(1)}, u32[]{:S(2)}, u32[]{:S(2)}) collective-permute-start(bf16[320,256]{1,0:T(8,128)(2,1)S(1)} %get-tuple-element.34), channel_id=1, source_target_pairs={{0,2},{1,3},{2,0},{3,1},{4,6},{5,7},{6,4},{7,5},{8,10},{9,11},{10,... | collective-permute-start | bytes 491528 | tf_op jit(solution)/shard_map/ppermute | solution.py:41
  211.7 6.7 %collective-permute-start.20 = (bf16[320,256]{1,0:T(8,128)(2,1)S(1)}, bf16[320,256]{1,0:T(8,128)(2,1)S(1)}, u32[]{:S(2)}, u32[]{:S(2)}) collective-permute-start(bf16[320,256]{1,0:T(8,128)(2,1)S(1)} %get-tuple-element.35), channel_id=1, source_target_pairs={{0,3},{1,0},{2,1},{3,2},{4,7},{5,4},{6,5},{7,6},{8,11},{9,8},{10,9... | collective-permute-start | bytes 491528 | tf_op jit(solution)/shard_map/ppermute | solution.py:41
  212.7 8.6 %collective-permute-start.19 = (bf16[320,256]{1,0:T(8,128)(2,1)S(1)}, bf16[320,256]{1,0:T(8,128)(2,1)S(1)}, u32[]{:S(2)}, u32[]{:S(2)}) collective-permute-start(bf16[320,256]{1,0:T(8,128)(2,1)S(1)} %get-tuple-element.36), channel_id=1, source_target_pairs={{0,1},{1,2},{2,3},{3,0},{4,5},{5,6},{6,7},{7,4},{8,9},{9,10},{10,1... | collective-permute-start | bytes 491528 | tf_op jit(solution)/shard_map/ppermute | solution.py:41
  213.2 8.2 %collective-permute-start.24 = (bf16[320,256]{1,0:T(8,128)(2,1)S(1)}, bf16[320,256]{1,0:T(8,128)(2,1)S(1)}, u32[]{:S(2)}, u32[]{:S(2)}) collective-permute-start(bf16[320,256]{1,0:T(8,128)(2,1)S(1)} %get-tuple-element.37), channel_id=1, source_target_pairs={{0,8},{1,9},{2,10},{3,11},{4,12},{5,13},{6,14},{7,15},{8,0},{9,1},... | collective-permute-start | bytes 491528 | tf_op jit(solution)/shard_map/ppermute | solution.py:37
  215.9 5.5 %collective-permute-start.26 = (bf16[320,256]{1,0:T(8,128)(2,1)S(1)}, bf16[320,256]{1,0:T(8,128)(2,1)S(1)}, u32[]{:S(2)}, u32[]{:S(2)}) collective-permute-start(bf16[320,256]{1,0:T(8,128)(2,1)S(1)} %get-tuple-element.38), channel_id=1, source_target_pairs={{0,12},{1,13},{2,14},{3,15},{4,0},{5,1},{6,2},{7,3},{8,4},{9,5},{1... | collective-permute-start | bytes 491528 | tf_op jit(solution)/shard_map/ppermute | solution.py:37
  217.4 6.8 %collective-permute-start.25 = (bf16[320,256]{1,0:T(8,128)(2,1)S(1)}, bf16[320,256]{1,0:T(8,128)(2,1)S(1)}, u32[]{:S(2)}, u32[]{:S(2)}) collective-permute-start(bf16[320,256]{1,0:T(8,128)(2,1)S(1)} %get-tuple-element.39), channel_id=1, source_target_pairs={{0,4},{1,5},{2,6},{3,7},{4,8},{5,9},{6,10},{7,11},{8,12},{9,13},{1... | collective-permute-start | bytes 491528 | tf_op jit(solution)/shard_map/ppermute | solution.py:37
  224.4 7.2 %collective-permute-start.28 = (bf16[320,2,256]{2,0,1:T(8,128)(2,1)S(1)}, bf16[320,2,256]{2,0,1:T(8,128)(2,1)S(1)}, u32[]{:S(2)}, u32[]{:S(2)}) collective-permute-start(bf16[320,2,256]{2,0,1:T(8,128)(2,1)S(1)} %pad_maximum_fusion.2), channel_id=1, source_target_pairs={{0,32},{16,48},{32,64},{48,80},{64,96},{80,112},{96,0},{112,16},{1... | collective-permute-start | bytes 983048 | tf_op jit(solution)/shard_map/ppermute | solution.py:45
  225.5 13.6 %collective-permute-start.27 = (bf16[320,2,256]{2,0,1:T(8,128)(2,1)S(1)}, bf16[320,2,256]{2,0,1:T(8,128)(2,1)S(1)}, u32[]{:S(2)}, u32[]{:S(2)}) collective-permute-start(bf16[320,2,256]{2,0,1:T(8,128)(2,1)S(1)} %pad_maximum_fusion.2), channel_id=1, source_target_pairs={{0,64},{16,80},{32,96},{48,112},{64,0},{80,16},{96,32},{112,48},{1... | collective-permute-start | bytes 983048 | tf_op jit(solution)/shard_map/ppermute | solution.py:45
  228.1 12.0 %collective-permute-start.29 = (bf16[320,2,256]{2,0,1:T(8,128)(2,1)S(1)}, bf16[320,2,256]{2,0,1:T(8,128)(2,1)S(1)}, u32[]{:S(2)}, u32[]{:S(2)}) collective-permute-start(bf16[320,2,256]{2,0,1:T(8,128)(2,1)S(1)} %pad_maximum_fusion.2), channel_id=1, source_target_pairs={{0,96},{16,112},{32,0},{48,16},{64,32},{80,48},{96,64},{112,80},{1... | collective-permute-start | bytes 983048 | tf_op jit(solution)/shard_map/ppermute | solution.py:45
  240.2 5.7 %collective-permute-start.30 = (f32[320,2,256]{2,0,1:T(8,128)S(1)}, f32[320,2,256]{2,0,1:T(8,128)S(1)}, u32[]{:S(2)}, u32[]{:S(2)}) collective-permute-start(f32[320,2,256]{2,0,1:T(8,128)S(1)} %add_add_fusion), channel_id=1, source_target_pairs={{0,16},{16,0},{32,48},{48,32},{64,80},{80,64},{96,112},{112,96},{1... | collective-permute-start | bytes 1966088 | tf_op jit(solution)/shard_map/ppermute | solution.py:49
  (15 other events, 15.5 us)

commit v2 on v0

v2 whole, which is shorter than its diff:
```python
import jax
import jax.numpy as jnp
from jax import lax
from jax.experimental import pallas as pl
from jax.experimental.pallas import tpu as pltpu
from jax.sharding import PartitionSpec as P

HEAD = 128
GROUP = 16
GROUPS = 64
EPS = 1e-06
SEQS = 8
ROWS = 128
WIDTH = 5120
BLOCK = 320
PAIR = 2 * BLOCK
HALF = 256
COLS = 2 * HALF
TOKENS = SEQS * ROWS
MIB = 1 << 20
BOTH = ("dp", "fsdp")

bf16, f32 = jnp.bfloat16, jnp.float32
COST = pl.CostEstimate(flops=1, bytes_accessed=1, transcendentals=0)


def along(value, long_axis, flip):
    pairs = []
    for dp in range(8):
        for y in range(4):
            for z in range(4):
                there = (y ^ flip) * 4 + z if (dp % 2 == 0) == long_axis else y * 4 + (z ^ flip)
                pairs.append((dp * 16 + y * 4 + z, dp * 16 + there))
    return lax.ppermute(value, BOTH, pairs)


def along_x(value, flip):
    return lax.ppermute(value, "dp", [(i, i ^ (2 * flip)) for i in range(8)])


def to_partner(value):
    return lax.ppermute(value, "dp", [(i, i ^ 1) for i in range(8)])


def params():
    return pltpu.CompilerParams(vmem_limit_bytes=48 * MIB)


def window(pair_of, j, place):
    pair = pair_of(place)
    return jnp.where(place[0] == 0, 4 * pair + j, 2 * j + pair)


def own_pair(place):
    return lax.div(place[1], 2)


def other_pair(place):
    return 1 - lax.div(place[1], 2)


def scale_kernel(hidden_ref, scale_ref):
    values = hidden_ref[0].astype(f32)
    mean = jnp.sum(values * values, -1, keepdims=True) * (1.0 / WIDTH)
    scale_ref[...] = jnp.broadcast_to(lax.rsqrt(mean + EPS), (ROWS, HEAD))


def scale_call(hidden):
    return pl.pallas_call(
        scale_kernel,
        grid=(SEQS,),
        in_specs=[pl.BlockSpec((1, ROWS, WIDTH), lambda i: (i, 0, 0))],
        out_specs=pl.BlockSpec((ROWS, HEAD), lambda i: (i, 0)),
        out_shape=jax.ShapeDtypeStruct((TOKENS, HEAD), f32),
        compiler_params=params(),
        cost_estimate=COST,
        name="token_scale",
    )(hidden)


SEQ_STEP = 4
STEP = SEQ_STEP * ROWS


def load_weights(place, pieces, w_ref, sem):
    u, v = place[1], place[2]
    first = pl.program_id(0) == 0
    for m, piece in enumerate(pieces):
        for n in range(4):
            bit, vv = lax.rem(u + m, 2), lax.bitwise_xor(v, n)
            row = jnp.where(place[0] == 0, bit * 4 + vv, vv * 2 + bit) * BLOCK
            copy = pltpu.make_async_copy(
                piece.at[pl.ds(n * BLOCK, BLOCK)],
                w_ref.at[pl.ds(pl.multiple_of(row, BLOCK), BLOCK)],
                sem,
            )
            pl.when(first)(copy.start)

    @pl.when(first)
    def _():
        for piece in pieces:
            for n in range(4):
                span = pl.ds(n * BLOCK, BLOCK)
                pltpu.make_async_copy(piece.at[span], w_ref.at[span], sem).wait()


def product(refs, w_ref):
    values = jnp.concatenate([ref[...].reshape(STEP, PAIR) for ref in refs], 1)
    return jnp.dot(values, w_ref[...], preferred_element_type=f32)


def first_kernel(place, *refs):
    own, partner, pieces, (sum_ref, w_ref, sem) = refs[:4], refs[4:8], refs[8:10], refs[10:]
    load_weights(place, pieces, w_ref, sem)
    sum_ref[0] = product(own, w_ref)
    sum_ref[1] = product(partner, w_ref)


def group_of(totals, group):
    lane = lax.broadcasted_iota(jnp.int32, (1, 2 * GROUPS), 1)
    mean, square = (
        jnp.sum(jnp.where(lane == group + k * GROUPS, totals, 0.0), -1, keepdims=True) / GROUP
        for k in range(2)
    )
    return mean, square - mean * mean


def second_kernel(place, facts, *refs):
    own, partner, pieces = refs[:4], refs[4:8], refs[8:10]
    (
        totals_ref, sum_ref, cot_own, cot_partner, scale_own, scale_partner, gain_ref,
        kv_ref, scaled_ref, w_ref, pre_ref, sem,
    ) = refs[10:]
    load_weights(place, pieces, w_ref, sem)
    gain = gain_ref[...]
    totals = totals_ref[...]
    rows = lax.broadcasted_iota(jnp.int32, (ROWS, HEAD), 0)
    i = pl.program_id(0)
    for side, (tokens, cot_ref, scale_ref) in enumerate(
        ((own, cot_own, scale_own), (partner, cot_partner, scale_partner))
    ):
        pre_ref[...] = product(tokens, w_ref) + sum_ref[side]
        for q in range(SEQ_STEP):
            n = i * SEQ_STEP + q
            slot, live, reward, group = (facts[4 * side + k, n] for k in range(4))
            span = pl.ds(q * ROWS, ROWS)
            mean, spread = group_of(totals, group)
            weight = (reward.astype(f32) - mean) / jnp.sqrt(jnp.maximum(spread, 1.0))
            weight = weight / jnp.full((1, 1), live, jnp.int32).astype(f32)
            coef = jnp.where(rows < live, weight, 0.0).astype(bf16).astype(f32)
            scale = scale_ref[span]
            coef = coef * scale
            for part in range(COLS // HEAD):
                columns = pl.ds(part * HEAD, HEAD)
                values = pre_ref[span, columns] * scale
                cot = cot_ref[slot, :, columns].astype(f32)
                if part < HALF // HEAD:
                    root = lax.rsqrt(jnp.mean(values * values, -1, keepdims=True) + EPS)
                    unit = values * root
                    kv_ref[slot, side, :, columns] = (unit * gain).astype(bf16)
                    slope = cot * gain
                    inner = jnp.mean(unit * slope, -1, keepdims=True)
                    cot = (slope - unit * inner) * root
                else:
                    kv_ref[slot, side, :, columns] = values.astype(bf16)
                scaled_ref[side, span, columns] = (cot * coef).astype(bf16)


def token_specs(pair_of):
    return [
        pl.BlockSpec(
            (SEQ_STEP, ROWS, PAIR), lambda i, p, *s, j=j: (i, 0, window(pair_of, j, p))
        )
        for j in range(4)
    ] * 2


ANY_SPEC = pl.BlockSpec(memory_space=pl.ANY)
SUM_SPEC = pl.BlockSpec((2, STEP, COLS), lambda i, *s: (0, i, 0))
W_SCRATCH = pltpu.VMEM((4 * PAIR, COLS), bf16)


def first_call(place, own, partner, weights):
    return pl.pallas_call(
        first_kernel,
        grid_spec=pltpu.PrefetchScalarGridSpec(
            num_scalar_prefetch=1,
            grid=(TOKENS // STEP,),
            in_specs=token_specs(own_pair) + [ANY_SPEC] * 2,
            out_specs=SUM_SPEC,
            scratch_shapes=[W_SCRATCH, pltpu.SemaphoreType.DMA],
        ),
        out_shape=jax.ShapeDtypeStruct((2, TOKENS, COLS), f32),
        compiler_params=params(),
        cost_estimate=COST,
        name="project_first",
    )(place, *[own] * 4, *[partner] * 4, *weights)


def second_call(place, facts, totals, own, partner, weights, sums, cots, scales, k_gain):
    whole = pl.BlockSpec((SEQS, ROWS, COLS), lambda i, *s: (0, 0, 0))
    wide = pl.BlockSpec((STEP, HEAD), lambda i, *s: (i, 0))
    return pl.pallas_call(
        second_kernel,
        grid_spec=pltpu.PrefetchScalarGridSpec(
            num_scalar_prefetch=2,
            grid=(TOKENS // STEP,),
            in_specs=token_specs(other_pair)
            + [ANY_SPEC] * 2
            + [pl.BlockSpec((1, 2 * GROUPS), lambda i, *s: (0, 0))]
            + [SUM_SPEC, whole, whole, wide, wide]
            + [pl.BlockSpec((1, HEAD), lambda i, *s: (0, 0))],
            out_specs=[
                pl.BlockSpec((SEQS, 2, ROWS, COLS), lambda i, *s: (0, 0, 0, 0)),
                SUM_SPEC,
            ],
            scratch_shapes=[W_SCRATCH, pltpu.VMEM((STEP, COLS), f32), pltpu.SemaphoreType.DMA],
        ),
        out_shape=[
            jax.ShapeDtypeStruct((SEQS, 2, ROWS, COLS), bf16),
            jax.ShapeDtypeStruct((2, TOKENS, COLS), bf16),
        ],
        compiler_params=params(),
        cost_estimate=COST,
        name="project_second",
    )(
        place, facts, *[own] * 4, *[partner] * 4, *weights, totals, sums, *cots, *scales,
        k_gain.reshape(1, HEAD),
    )


def gradient_kernel(place, own_ref, partner_ref, scaled_ref, same_ref, cross_ref):
    core, u, v = place[0], place[1], place[2]
    j = pl.program_id(0)
    total = None
    for side, ref in enumerate((own_ref, partner_ref)):
        part = lax.dot_general(
            ref[...].reshape(TOKENS, PAIR),
            scaled_ref[side],
            (((0,), (0,)), ((), ())),
            preferred_element_type=f32,
        )
        total = part if total is None else total + part
    total = total.astype(bf16)
    for s in range(2):
        bit = jnp.where(core == 0, lax.div(j, 2), s)
        vv = jnp.where(core == 0, 2 * lax.rem(j, 2) + s, j)
        n = lax.bitwise_xor(vv, v)
        rows = total[s * BLOCK : (s + 1) * BLOCK]
        same = bit == lax.rem(u, 2)

        @pl.when(same)
        def _():
            same_ref[n] = rows

        @pl.when(jnp.logical_not(same))
        def _():
            cross_ref[n] = rows


def gradient_call(pair_of, place, own, partner, scaled):
    tokens = pl.BlockSpec((SEQS, ROWS, PAIR), lambda j, p: (0, 0, window(pair_of, j, p)))
    out = pl.BlockSpec((4, BLOCK, COLS), lambda j, p: (0, 0, 0))
    return pl.pallas_call(
        gradient_kernel,
        grid_spec=pltpu.PrefetchScalarGridSpec(
            num_scalar_prefetch=1,
            grid=(4,),
            in_specs=[tokens, tokens, pl.BlockSpec((2, TOKENS, COLS), lambda j, p: (0, 0, 0))],
            out_specs=[out, out],
        ),
        out_shape=[jax.ShapeDtypeStruct((4, BLOCK, COLS), bf16)] * 2,
        compiler_params=params(),
        cost_estimate=COST,
        name="weight_gradient",
    )(place, own, partner, scaled)


def group_sums(rewards, group_ids):
    scores = rewards.astype(f32)
    member = (group_ids[:, None] == jnp.arange(GROUPS, dtype=jnp.int32)[None, :]).astype(f32)
    return jnp.concatenate(
        [jnp.sum(member * scores[:, None], 0), jnp.sum(member * (scores * scores)[:, None], 0)]
    ).reshape(1, 1, 2 * GROUPS)


def summed_over(sums, axis):
    sums = jnp.broadcast_to(sums, (lax.axis_size(axis), 1, 2 * GROUPS))
    return lax.all_to_all(sums, axis, 0, 0, tiled=True).sum(0, keepdims=True)


def columns_of(core, array):
    k0, k1, v0, v1 = (array[..., i * HALF : (i + 1) * HALF] for i in range(4))
    return jnp.where(
        core == 0, jnp.concatenate([k0, v0], -1), jnp.concatenate([k1, v1], -1)
    )


def all_columns(core, mine, other):
    low, high = jnp.where(core == 0, mine, other), jnp.where(core == 0, other, mine)
    return jnp.concatenate(
        [low[..., :HALF], high[..., :HALF], low[..., HALF:], high[..., HALF:]], -1
    )


def on_device(
    hidden_in, kv_weight, ln_gain, k_gain, cost_slots, lengths, rewards, group_ids, kv_cotangent
):
    place_f = lax.axis_index("fsdp")
    core = lax.rem(lax.axis_index("dp"), 2)
    y, z = lax.div(place_f, 4), lax.rem(place_f, 4)
    place = jnp.stack([core, jnp.where(core == 0, y, z), jnp.where(core == 0, z, y)])
    place = place.astype(jnp.int32)
    gain = lax.dynamic_slice(ln_gain, (place_f * BLOCK,), (BLOCK,))[:, None]

    facts = jnp.stack([cost_slots[0], lengths, rewards, group_ids])
    facts = jnp.concatenate([facts, to_partner(facts)])

    mine = (columns_of(core, kv_weight).astype(f32) * gain).astype(bf16)
    totals = summed_over(group_sums(rewards, group_ids), "dp")
    piece = jnp.concatenate([mine] + [along(mine, False, n) for n in (1, 2, 3)])
    pieces = [piece] + [along(piece, True, m) for m in (1, 2, 3)]

    kv_cotangent, _ = lax.optimization_barrier((kv_cotangent, totals))
    cot = lax.all_to_all(kv_cotangent, "dp", split_axis=0, concat_axis=0, tiled=True)
    swapped, totals, _ = lax.optimization_barrier((hidden_in, totals, piece))
    partner = to_partner(swapped)
    totals = summed_over(totals, "fsdp").reshape(1, 2 * GROUPS)

    scale = scale_call(hidden_in)
    cot, scale, totals = lax.optimization_barrier((cot, scale, totals))
    cots = columns_of(core, cot), to_partner(columns_of(1 - core, cot))

    scales = scale, to_partner(scale)
    sums = first_call(place, hidden_in, partner, pieces[:2])
    kv, scaled = second_call(
        place, facts, totals, hidden_in, partner, pieces[2:], sums, cots, scales, k_gain
    )
    kv = lax.all_to_all(kv, "dp", split_axis=0, concat_axis=0, tiled=True)

    two, three = gradient_call(other_pair, place, hidden_in, partner, scaled)
    here, one = gradient_call(own_pair, place, hidden_in, partner, scaled)
    total = (
        here.astype(f32)
        + along(two, True, 2).astype(f32)
        + along(three, True, 3).astype(f32)
        + along(one, True, 1).astype(f32)
    )
    total = sum(along(total[n].astype(bf16), False, n).astype(f32) for n in (2, 1, 3)) + total[0]
    rows = total.astype(bf16)
    kv, rows = lax.optimization_barrier((kv, rows))
    kv = kv.reshape(4, 2, 2, ROWS, COLS)
    low, high = kv[:, 0], jnp.stack([kv[:, 1, 1], kv[:, 1, 0]], 1)
    keys_values = jnp.concatenate(
        [low[..., :HALF], high[..., :HALF], low[..., HALF:], high[..., HALF:]], -1
    ).reshape(SEQS, ROWS, 2 * COLS)
    ring = [rows.astype(f32)] + [along_x(rows, k).astype(f32) for k in (1, 2, 3)]
    rows = ((ring[0] + ring[2]) + (ring[1] + ring[3])) * gain
    rows, keys_values = lax.optimization_barrier((rows, keys_values))
    return keys_values, all_columns(core, rows, to_partner(rows))


def solution(mesh):
    in_specs = (
        P(("dp", "fsdp"), None, None),
        P("fsdp", None),
        P(),
        P(),
        P(("dp", "fsdp"), None),
        P(("dp", "fsdp")),
        P(("dp", "fsdp")),
        P(("dp", "fsdp")),
        P(("dp", "fsdp"), None, None),
    )
    out_specs = (P(("dp", "fsdp"), None, None), P("fsdp", None))
    return jax.shard_map(
        on_device, mesh=mesh, in_specs=in_specs, out_specs=out_specs, check_vma=False
    )
```

time: 497 us -> 180 us (0.36)
  waiting for transfers between devices: 301 us -> 54.6 us
  blocking collectives: 69.9 us -> 10.9 us
  Pallas kernels: 0 us -> 55.4 us
  other arithmetic: 43 us -> 6.91 us
  matrix products: 31 us -> 0 us
  starting transfers between devices: 9.83 us -> 40.3 us
  local copies, waits for them, and re-layouts: 26.2 us -> 10.1 us
  between operations: 13.9 us -> 0.92 us
    reduce_scatter x1 -> x0, waiting for transfers between devices: 129 us -> none  [on_device(): lax.psum_scatter(lax.dot_general(columns, scaled, (((0,), (0,)), ((), ())...]
    all_to_all x2 -> x3, waiting for transfers between devices: 112 us -> 21.9 us  [the longest x1 15.6 us: on_device(): lax.all_to_all(kv_cotangent, 'dp', split_axis=0, concat_axis=0, tiled=True)]
    psum x1 -> x0, blocking collectives: 69.9 us -> none  [on_device(): lax.psum((jnp.sum(member * scores[:, None], 0), jnp.sum(member * (scores...]
    psum x1 -> x0, waiting for transfers between devices: 59.9 us -> none  [on_device(): kv_grad = lax.psum(grad_local, 'dp')]
    pallas_call x0 -> x5, Pallas kernels: none -> 55.4 us  [the longest x2 19.9 us: gradient_call(): pl.pallas_call(gradient_kernel, grid_spec=pltpu.PrefetchScalarGridSpec(nu...]
    ppermute x0 -> x20, waiting for transfers between devices: none -> 32.7 us  [the longest x12 23.1 us: along(): return lax.ppermute(value, BOTH, pairs)]
    dot_general x2 -> x0, matrix products: 31 us -> none  [the longest x1 15.6 us: on_device(): lax.dot_general(columns, scaled, (((0,), (0,)), ((), ())), preferred_elem...]
    ppermute x0 -> x20, starting transfers between devices: none -> 22.3 us  [the longest x12 12.6 us: along(): return lax.ppermute(value, BOTH, pairs)]
  transfers between devices with their start and end apart: 5 -> 23, of which waited for: 3 -> 8; matrix products, arithmetic and copies ran while one was open for 10% -> 6% of each run, Pallas kernels for 0% -> 17%
where the time goes in v2:
time: 180 us; the launch traced here: 179 us
  Pallas kernels  55.4 us (31%)
  waiting for transfers between devices  54.6 us (30%)
  starting transfers between devices  40.3 us (22%)
  blocking collectives  10.9 us (6%)
  local copies, waits for them, and re-layouts  10.1 us (6%)
  other arithmetic  6.91 us (4%)
    ppermute x12, waiting for transfers between devices, along(): return lax.ppermute(value, BOTH, pairs)  23.1 us
    pallas_call x2, Pallas kernels, gradient_call(): pl.pallas_call(gradient_kernel, grid_spec=pltpu.PrefetchScalarGridSpec(nu...  19.9 us
    pallas_call x1, Pallas kernels, second_call(): pl.pallas_call(second_kernel, grid_spec=pltpu.PrefetchScalarGridSpec(num_...  15.6 us
    all_to_all x1, waiting for transfers between devices, on_device(): lax.all_to_all(kv_cotangent, 'dp', split_axis=0, concat_axis=0, tiled=True)  15.6 us
    ppermute x12, starting transfers between devices, along(): return lax.ppermute(value, BOTH, pairs)  12.6 us
    pallas_call x1, Pallas kernels, first_call(): pl.pallas_call(first_kernel, grid_spec=pltpu.PrefetchScalarGridSpec(num_s...  12.5 us
    all_to_all x1, blocking collectives, summed_over(): return lax.all_to_all(sums, axis, 0, 0, tiled=True).sum(0, keepdims=True)  10.9 us
    ppermute x3, waiting for transfers between devices, along_x(): return lax.ppermute(value, 'dp', [(i, i ^ 2 * flip) for i in range(8)])  7.86 us
  transfers between devices with their start and end apart: 23, of which 8 were waited for; matrix products, arithmetic and copies ran while one was open for 6% of the time, Pallas kernels for 17%

profile of v2, /device:TPU:1, one launch (start us, length us, event | category | flops | bytes accessed | tf_op | source)
XLA Modules:
  0.0 179.2 jit_solution(6781060320296797090)
XLA Ops:
  0.7 1.2 fusion.12
  1.9 0.8 dynamic_slice.3
  2.8 3.6 %collective-permute-start.3 = (bf16[320,512]{1,0:T(8,128)(2,1)S(1)}, bf16[320,512]{1,0:T(8,128)(2,1)S(1)}, u32[]{:S(2)}, u32[]{:S(2)}) collective-permute-start(bf16[320,512]{1,0:T(8,128)(2,1)S(1)} %multiply_convert_fusion), channel_id=1, source_target_pairs={{0,3},{1,2},{2,1},{3,0},{4,7},{5,6},{6,5},{7,4},{8,11},{9,10},{10,... | collective-permute-start | bytes 983048 | tf_op jit(solution)/shard_map/ppermute | solution.py:34
  6.4 0.3 collective-permute-start.2
  6.8 0.3 collective-permute-start.1
  7.3 10.9 %all_to_all.20 = f32[8,1,128]{2,1,0:T(1,128)S(1)} all-to-all(f32[8,1,128]{2,1,0:T(1,128)S(1)} %broadcast_in_dim.8), channel_id=1, replica_groups=mesh['dp'=8,'fsdp'=16] {'dp'}, dimensions={0} | all-to-all | bytes 8192 | tf_op jit(solution)/shard_map/all_to_all | solution.py:289
  18.3 0.8 collective-permute-start.4
  19.1 0.6 broadcast_in_dim.11
  19.7 6.9 %all-to-all-start.2 = ((f32[16,1,128]{2,1,0:T(1,128)}), f32[16,1,128]{2,1,0:T(1,128)S(1)}, u32[]{:S(2)}, u32[]{:S(2)}) async-start(f32[16,1,128]{2,1,0:T(1,128)} %broadcast_in_dim.11), calls=%async_computation.2 | async-start | bytes 16384 | tf_op jit(solution)/shard_map/all_to_all | solution.py:289
  26.6 6.3 %all-to-all-done.2 = f32[16,1,128]{2,1,0:T(1,128)S(1)} async-done(((f32[16,1,128]{2,1,0:T(1,128)}), f32[16,1,128]{2,1,0:T(1,128)S(1)}, u32[]{:S(2)}, u32[]{:S(2)}) %all-to-all-start.2) | async-done | bytes 8224 | tf_op jit(solution)/shard_map/all_to_all | solution.py:289
  32.9 5.7 %all-to-all-start.1 = ((bf16[8,128,1024]{2,1,0:T(8,128)(2,1)}), bf16[8,128,1024]{2,1,0:T(8,128)(2,1)}, u32[]{:S(2)}, u32[]{:S(2)}) async-start(bf16[8,128,1024]{2,1,0:T(8,128)(2,1)} %param.17), calls=%async_computation.1 | async-start | bytes 4194304 | tf_op jit(solution)/shard_map/all_to_all | solution.py:325
  38.6 0.3 collective-permute-start.7
  38.9 0.6 collective-permute-start
  39.5 7.3 %token_scale.1.refs_14_ = f32[1024,128]{1,0:T(8,128)S(1)} custom-call(bf16[8,128,5120]{2,1,0:T(8,128)(2,1)} %own_ref.3), custom_call_target="tpu_custom_call" | custom-call | flops 1 | bytes 1 | tf_op jit(solution)/shard_map/token_scale/pallas_call | solution.py:69
  46.8 1.0 collective-permute-start.6
  47.8 1.6 collective-permute-start.5
  49.4 15.6 %all-to-all-done.1 = bf16[8,128,1024]{2,1,0:T(8,128)(2,1)} async-done(((bf16[8,128,1024]{2,1,0:T(8,128)(2,1)}), bf16[8,128,1024]{2,1,0:T(8,128)(2,1)}, u32[]{:S(2)}, u32[]{:S(2)}) %all-to-all-start.1) | async-done | bytes 2097184 | tf_op jit(solution)/shard_map/all_to_all | solution.py:325
  65.1 1.7 fusion.8
  66.7 1.4 broadcast_select_fusion
  68.2 0.9 collective-permute-start.8
  69.2 12.5 %project_first.1.refs_11_ = f32[2,1024,512]{2,1,0:T(8,128)} custom-call(s32[3]{0:T(128)S(1)} %pad_add_fusion.1.place, bf16[8,128,5120]{2,1,0:T(8,128)(2,1)} %own_ref.3, bf16[8,128,5120]{2,1,0:T(8,128)(2,1)} %own_ref.3, bf16[8,128,5120]{2,1,0:T(8,128)(2,1)} %own_ref.3, bf16[8,128,5120]{2,1,0:T(8,128)(2,1)} %own_ref.3, ...), custom_call_target="tpu_custom_call" | custom-call | flops 1 | bytes 1 | tf_op jit(solution)/shard_map/project_first/pallas_call | solution.py:184
  81.8 15.6 %project_second.1 = (bf16[8,2,128,512]{3,2,1,0:T(8,128)(2,1)}, bf16[2,1024,512]{2,1,0:T(8,128)(2,1)}) custom-call(s32[3]{0:T(128)S(1)} %pad_add_fusion.1.place, s32[8,8]{1,0:T(8,128)S(1)} %concatenate.30.facts, bf16[8,128,5120]{2,1,0:T(8,128)(2,1)} %own_ref.3, bf16[8,128,5120]{2,1,0:T(8,128)(2,1)} %own_ref.3, bf16[8,128,5120]{2,1,0:T(8,128)(2,1)} %own_ref.3, ...), custom_call_target="tpu_custom_call" | custom-call | flops 1 | bytes 1 | tf_op jit(solution)/shard_map/project_second/pallas_call | solution.py:203
  97.5 1.6 copy-done
  99.0 9.9 %weight_gradient.3 = (bf16[4,320,512]{2,1,0:T(8,128)(2,1)}, bf16[4,320,512]{2,1,0:T(8,128)(2,1)S(1)}) custom-call(s32[3]{0:T(128)S(1)} %pad_add_fusion.1.place, bf16[8,128,5120]{2,1,0:T(8,128)(2,1)} %own_ref.3, bf16[8,128,5120]{2,1,0:T(8,128)(2,1)} %collective-permute-done.4.refs_4_.refs_5_.refs_6_.refs_7_.partner_ref, bf16[2,1024,512]{2,1,0:T(8,128)(2,1)S(1)} %copy-done), custom_call_target="tpu_custom_call" | custom-call | flops 1 | bytes 1 | tf_op jit(solution)/shard_map/weight_gradient/pallas_call | solution.py:264
  109.0 0.9 collective-permute-start.10
  109.9 1.8 collective-permute-start.11
  111.7 10.0 %weight_gradient.2 = (bf16[4,320,512]{2,1,0:T(8,128)(2,1)S(1)}, bf16[4,320,512]{2,1,0:T(8,128)(2,1)}) custom-call(s32[3]{0:T(128)S(1)} %pad_add_fusion.1.place, bf16[8,128,5120]{2,1,0:T(8,128)(2,1)} %own_ref.3, bf16[8,128,5120]{2,1,0:T(8,128)(2,1)} %collective-permute-done.4.refs_4_.refs_5_.refs_6_.refs_7_.partner_ref, bf16[2,1024,512]{2,1,0:T(8,128)(2,1)S(1)} %copy-done), custom_call_target="tpu_custom_call" | custom-call | flops 1 | bytes 1 | tf_op jit(solution)/shard_map/weight_gradient/pallas_call | solution.py:264
  121.6 5.4 %all-to-all-start.3 = ((bf16[8,2,128,512]{3,2,1,0:T(8,128)(2,1)}), bf16[8,2,128,512]{3,2,1,0:T(8,128)(2,1)}, u32[]{:S(2)}, u32[]{:S(2)}) async-start(bf16[8,2,128,512]{3,2,1,0:T(8,128)(2,1)} %get-tuple-element.24), calls=%async_computation.3 | async-start | bytes 4194304 | tf_op jit(solution)/shard_map/all_to_all | solution.py:339
  127.1 0.5 collective-permute-done.10
  127.6 14.0 %collective-permute-done.11 = bf16[4,320,512]{2,1,0:T(8,128)(2,1)} collective-permute-done((bf16[4,320,512]{2,1,0:T(8,128)(2,1)S(1)}, bf16[4,320,512]{2,1,0:T(8,128)(2,1)}, u32[]{:S(2)}, u32[]{:S(2)}) %collective-permute-start.11) | collective-permute-done | bytes 1310752 | tf_op jit(solution)/shard_map/ppermute | solution.py:34
  141.6 2.9 %fusion.7 = (bf16[4,320,512]{2,1,0:T(8,128)(2,1)S(1)}, f32[4,320,512]{2,1,0:T(8,128)S(1)}) fusion(bf16[4,320,512]{2,1,0:T(8,128)(2,1)} %collective-permute-done.12, bf16[4,320,512]{2,1,0:T(8,128)(2,1)} %collective-permute-done.11, bf16[4,320,512]{2,1,0:T(8,128)(2,1)} %collective-permute-done.10, bf16[4,320,512]{2,1,0:T(8,128)(2,1)S(1)} %get-tuple-element.26), kind=kLoop, calls=%fused_computation.36 | loop fusion | flops 5242880 | bytes 9175040 | tf_op jit(solution)/shard_map/convert.2
  144.6 1.0 collective-permute-start.13
  145.6 1.8 collective-permute-start.15
  147.3 5.2 %collective-permute-done.13 = bf16[320,512]{1,0:T(8,128)(2,1)S(1)} collective-permute-done((bf16[320,512]{1,0:T(8,128)(2,1)S(1)}, bf16[320,512]{1,0:T(8,128)(2,1)S(1)}, u32[]{:S(2)}, u32[]{:S(2)}) %collective-permute-start.13) | collective-permute-done | bytes 327712 | tf_op jit(solution)/shard_map/ppermute | solution.py:34
  152.5 3.4 %collective-permute-done.15 = bf16[320,512]{1,0:T(8,128)(2,1)S(1)} collective-permute-done((bf16[320,512]{1,0:T(8,128)(2,1)S(1)}, bf16[320,512]{1,0:T(8,128)(2,1)S(1)}, u32[]{:S(2)}, u32[]{:S(2)}) %collective-permute-start.15) | collective-permute-done | bytes 327712 | tf_op jit(solution)/shard_map/ppermute | solution.py:34
  155.9 0.2 fusion.5
  156.1 1.0 collective-permute-start.18
  157.0 3.0 %collective-permute-start.16 = (bf16[320,512]{1,0:T(8,128)(2,1)S(1)}, bf16[320,512]{1,0:T(8,128)(2,1)S(1)}, u32[]{:S(2)}, u32[]{:S(2)}) collective-permute-start(bf16[320,512]{1,0:T(8,128)(2,1)S(1)} %fusion.5), channel_id=1, source_target_pairs={{0,64},{16,80},{32,96},{48,112},{64,0},{80,16},{96,32},{112,48},{1... | collective-permute-start | bytes 983048 | tf_op jit(solution)/shard_map/ppermute | solution.py:38
  160.0 1.3 copy_bitcast_fusion
  161.3 1.3 slice_bitcast_fusion.2
  162.7 0.3 fusion.3
  163.0 1.5 copy.21
  164.5 7.9 %collective-permute-done.16 = bf16[320,512]{1,0:T(8,128)(2,1)S(1)} collective-permute-done((bf16[320,512]{1,0:T(8,128)(2,1)S(1)}, bf16[320,512]{1,0:T(8,128)(2,1)S(1)}, u32[]{:S(2)}, u32[]{:S(2)}) %collective-permute-start.16) | collective-permute-done | bytes 327712 | tf_op jit(solution)/shard_map/ppermute | solution.py:38
  172.4 0.2 add_multiply_fusion
  172.6 3.4 %collective-permute-start.19 = (f32[320,512]{1,0:T(8,128)S(1)}, f32[320,512]{1,0:T(8,128)S(1)}, u32[]{:S(2)}, u32[]{:S(2)}) collective-permute-start(f32[320,512]{1,0:T(8,128)S(1)} %add_multiply_fusion), channel_id=1, source_target_pairs={{0,16},{16,0},{32,48},{48,32},{64,80},{80,64},{96,112},{112,96},{1... | collective-permute-start | bytes 1966088 | tf_op jit(solution)/shard_map/ppermute | solution.py:42
  176.0 1.7 collective-permute-done.19
  177.7 0.2 broadcast_select_fusion.3
  178.0 1.2 pad_maximum_fusion.1
  (46 shorter events, 0.9 us)
Async XLA Ops:
  0.6 6.5 %copy-start.5 = (s32[8]{0:T(128)S(1)}, s32[8]{0:T(128)}, u32[]{:S(2)}) copy-start(s32[8]{0:T(128)} %param.15) | copy-start | bytes 100
  0.6 6.5 %copy-start.2 = (s32[8]{0:T(128)S(1)}, s32[8]{0:T(128)}, u32[]{:S(2)}) copy-start(s32[8]{0:T(128)} %param.16) | copy-start | bytes 100
  2.8 15.4 %collective-permute-start.3 = (bf16[320,512]{1,0:T(8,128)(2,1)S(1)}, bf16[320,512]{1,0:T(8,128)(2,1)S(1)}, u32[]{:S(2)}, u32[]{:S(2)}) collective-permute-start(bf16[320,512]{1,0:T(8,128)(2,1)S(1)} %multiply_convert_fusion), channel_id=1, source_target_pairs={{0,3},{1,2},{2,1},{3,0},{4,7},{5,6},{6,5},{7,4},{8,11},{9,10},{10,... | collective-permute-start | bytes 983048 | tf_op jit(solution)/shard_map/ppermute | solution.py:34
  6.4 11.8 %collective-permute-start.2 = (bf16[320,512]{1,0:T(8,128)(2,1)S(1)}, bf16[320,512]{1,0:T(8,128)(2,1)S(1)}, u32[]{:S(2)}, u32[]{:S(2)}) collective-permute-start(bf16[320,512]{1,0:T(8,128)(2,1)S(1)} %multiply_convert_fusion), channel_id=1, source_target_pairs={{0,2},{1,3},{2,0},{3,1},{4,6},{5,7},{6,4},{7,5},{8,10},{9,11},{10,... | collective-permute-start | bytes 983048 | tf_op jit(solution)/shard_map/ppermute | solution.py:34
  6.8 11.5 %collective-permute-start.1 = (bf16[320,512]{1,0:T(8,128)(2,1)S(1)}, bf16[320,512]{1,0:T(8,128)(2,1)S(1)}, u32[]{:S(2)}, u32[]{:S(2)}) collective-permute-start(bf16[320,512]{1,0:T(8,128)(2,1)S(1)} %multiply_convert_fusion), channel_id=1, source_target_pairs={{0,1},{1,0},{2,3},{3,2},{4,5},{5,4},{6,7},{7,6},{8,9},{9,8},{10,11... | collective-permute-start | bytes 983048 | tf_op jit(solution)/shard_map/ppermute | solution.py:34
  18.3 50.9 %collective-permute-start.4 = (bf16[8,128,5120]{2,1,0:T(8,128)(2,1)}, bf16[8,128,5120]{2,1,0:T(8,128)(2,1)}, u32[]{:S(2)}, u32[]{:S(2)}) collective-permute-start(bf16[8,128,5120]{2,1,0:T(8,128)(2,1)} %own_ref.3), channel_id=1, source_target_pairs={{0,16},{16,0},{32,48},{48,32},{64,80},{80,64},{96,112},{112,96},{1... | collective-permute-start | bytes 31457288 | tf_op jit(solution)/shard_map/ppermute | solution.py:42
  19.7 13.2 %all-to-all-start.2 = ((f32[16,1,128]{2,1,0:T(1,128)}), f32[16,1,128]{2,1,0:T(1,128)S(1)}, u32[]{:S(2)}, u32[]{:S(2)}) async-start(f32[16,1,128]{2,1,0:T(1,128)} %broadcast_in_dim.11), calls=%async_computation.2 | async-start | bytes 16384 | tf_op jit(solution)/shard_map/all_to_all | solution.py:289
  26.6 12.3 %copy-start.3 = (s32[1,8]{1,0:T(1,128)S(1)}, s32[1,8]{1,0:T(1,128)}, u32[]{:S(2)}) copy-start(s32[1,8]{1,0:T(1,128)} %param.13) | copy-start | bytes 100
  26.6 12.3 %copy-start.4 = (s32[8]{0:T(128)S(1)}, s32[8]{0:T(128)}, u32[]{:S(2)}) copy-start(s32[8]{0:T(128)} %param.14) | copy-start | bytes 100
  32.9 32.1 %all-to-all-start.1 = ((bf16[8,128,1024]{2,1,0:T(8,128)(2,1)}), bf16[8,128,1024]{2,1,0:T(8,128)(2,1)}, u32[]{:S(2)}, u32[]{:S(2)}) async-start(bf16[8,128,1024]{2,1,0:T(8,128)(2,1)} %param.17), calls=%async_computation.1 | async-start | bytes 4194304 | tf_op jit(solution)/shard_map/all_to_all | solution.py:325
  38.6 30.4 %collective-permute-start.7 = (bf16[1280,512]{1,0:T(8,128)(2,1)S(1)}, bf16[1280,512]{1,0:T(8,128)(2,1)}, u32[]{:S(2)}, u32[]{:S(2)}) collective-permute-start(bf16[1280,512]{1,0:T(8,128)(2,1)S(1)} %pad_maximum_fusion.refs_8_), channel_id=1, source_target_pairs={{0,4},{1,5},{2,6},{3,7},{4,0},{5,1},{6,2},{7,3},{8,12},{9,13},{10,... | collective-permute-start | bytes 3932168 | tf_op jit(solution)/shard_map/ppermute | solution.py:34
  38.9 29.3 %collective-permute-start = (s32[4,8]{1,0:T(4,128)S(1)}, s32[4,8]{1,0:T(4,128)S(1)}, u32[]{:S(2)}, u32[]{:S(2)}) collective-permute-start(s32[4,8]{1,0:T(4,128)S(1)} %pad_add_fusion), channel_id=1, source_target_pairs={{0,16},{16,0},{32,48},{48,32},{64,80},{80,64},{96,112},{112,96},{1... | collective-permute-start | bytes 392 | tf_op jit(solution)/shard_map/ppermute | solution.py:42
  46.8 34.9 %collective-permute-start.6 = (bf16[1280,512]{1,0:T(8,128)(2,1)S(1)}, bf16[1280,512]{1,0:T(8,128)(2,1)}, u32[]{:S(2)}, u32[]{:S(2)}) collective-permute-start(bf16[1280,512]{1,0:T(8,128)(2,1)S(1)} %pad_maximum_fusion.refs_8_), channel_id=1, source_target_pairs={{0,12},{1,13},{2,14},{3,15},{4,8},{5,9},{6,10},{7,11},{8,4},{9,5},... | collective-permute-start | bytes 3932168 | tf_op jit(solution)/shard_map/ppermute | solution.py:34
  47.8 34.0 %collective-permute-start.5 = (bf16[1280,512]{1,0:T(8,128)(2,1)S(1)}, bf16[1280,512]{1,0:T(8,128)(2,1)}, u32[]{:S(2)}, u32[]{:S(2)}) collective-permute-start(bf16[1280,512]{1,0:T(8,128)(2,1)S(1)} %pad_maximum_fusion.refs_8_), channel_id=1, source_target_pairs={{0,8},{1,9},{2,10},{3,11},{4,12},{5,13},{6,14},{7,15},{8,0},{9,1},... | collective-permute-start | bytes 3932168 | tf_op jit(solution)/shard_map/ppermute | solution.py:34
  68.2 13.6 %collective-permute-start.8 = (bf16[8,128,512]{2,1,0:T(8,128)(2,1)}, bf16[8,128,512]{2,1,0:T(8,128)(2,1)}, u32[]{:S(2)}, u32[]{:S(2)}) collective-permute-start(bf16[8,128,512]{2,1,0:T(8,128)(2,1)} %get-tuple-element.40), channel_id=1, source_target_pairs={{0,16},{16,0},{32,48},{48,32},{64,80},{80,64},{96,112},{112,96},{1... | collective-permute-start | bytes 3145736 | tf_op jit(solution)/shard_map/ppermute | solution.py:42
  69.0 12.7 %collective-permute-start.9 = (f32[1024,128]{1,0:T(8,128)S(1)}, f32[1024,128]{1,0:T(8,128)S(1)}, u32[]{:S(2)}, u32[]{:S(2)}) collective-permute-start(f32[1024,128]{1,0:T(8,128)S(1)} %token_scale.1.refs_14_), channel_id=1, source_target_pairs={{0,16},{16,0},{32,48},{48,32},{64,80},{80,64},{96,112},{112,96},{1... | collective-permute-start | bytes 1572872 | tf_op jit(solution)/shard_map/ppermute | solution.py:42
  69.2 12.6 %copy-start.1 = (f32[128]{0:T(128)S(1)}, f32[128]{0:T(128)}, u32[]{:S(2)}) copy-start(f32[128]{0:T(128)} %param.12) | copy-start | bytes 1540
  97.5 1.6 copy-start
  109.0 18.6 %collective-permute-start.10 = (bf16[4,320,512]{2,1,0:T(8,128)(2,1)}, bf16[4,320,512]{2,1,0:T(8,128)(2,1)}, u32[]{:S(2)}, u32[]{:S(2)}) collective-permute-start(bf16[4,320,512]{2,1,0:T(8,128)(2,1)} %get-tuple-element.27), channel_id=1, source_target_pairs={{0,8},{1,9},{2,10},{3,11},{4,12},{5,13},{6,14},{7,15},{8,0},{9,1},... | collective-permute-start | bytes 3932168 | tf_op jit(solution)/shard_map/ppermute | solution.py:34
  109.9 31.7 %collective-permute-start.11 = (bf16[4,320,512]{2,1,0:T(8,128)(2,1)S(1)}, bf16[4,320,512]{2,1,0:T(8,128)(2,1)}, u32[]{:S(2)}, u32[]{:S(2)}) collective-permute-start(bf16[4,320,512]{2,1,0:T(8,128)(2,1)S(1)} %get-tuple-element.28), channel_id=1, source_target_pairs={{0,12},{1,13},{2,14},{3,15},{4,8},{5,9},{6,10},{7,11},{8,4},{9,5},... | collective-permute-start | bytes 3932168 | tf_op jit(solution)/shard_map/ppermute | solution.py:34
  121.6 20.0 %collective-permute-start.12 = (bf16[4,320,512]{2,1,0:T(8,128)(2,1)}, bf16[4,320,512]{2,1,0:T(8,128)(2,1)}, u32[]{:S(2)}, u32[]{:S(2)}) collective-permute-start(bf16[4,320,512]{2,1,0:T(8,128)(2,1)} %get-tuple-element.29), channel_id=1, source_target_pairs={{0,4},{1,5},{2,6},{3,7},{4,0},{5,1},{6,2},{7,3},{8,12},{9,13},{10,... | collective-permute-start | bytes 3932168 | tf_op jit(solution)/shard_map/ppermute | solution.py:34
  121.6 34.4 %all-to-all-start.3 = ((bf16[8,2,128,512]{3,2,1,0:T(8,128)(2,1)}), bf16[8,2,128,512]{3,2,1,0:T(8,128)(2,1)}, u32[]{:S(2)}, u32[]{:S(2)}) async-start(bf16[8,2,128,512]{3,2,1,0:T(8,128)(2,1)} %get-tuple-element.24), calls=%async_computation.3 | async-start | bytes 4194304 | tf_op jit(solution)/shard_map/all_to_all | solution.py:339
  144.6 8.0 %collective-permute-start.13 = (bf16[320,512]{1,0:T(8,128)(2,1)S(1)}, bf16[320,512]{1,0:T(8,128)(2,1)S(1)}, u32[]{:S(2)}, u32[]{:S(2)}) collective-permute-start(bf16[320,512]{1,0:T(8,128)(2,1)S(1)} %get-tuple-element.48), channel_id=1, source_target_pairs={{0,2},{1,3},{2,0},{3,1},{4,6},{5,7},{6,4},{7,5},{8,10},{9,11},{10,... | collective-permute-start | bytes 983048 | tf_op jit(solution)/shard_map/ppermute | solution.py:34
  145.6 10.3 %collective-permute-start.15 = (bf16[320,512]{1,0:T(8,128)(2,1)S(1)}, bf16[320,512]{1,0:T(8,128)(2,1)S(1)}, u32[]{:S(2)}, u32[]{:S(2)}) collective-permute-start(bf16[320,512]{1,0:T(8,128)(2,1)S(1)} %get-tuple-element.49), channel_id=1, source_target_pairs={{0,3},{1,2},{2,1},{3,0},{4,7},{5,6},{6,5},{7,4},{8,11},{9,10},{10,... | collective-permute-start | bytes 983048 | tf_op jit(solution)/shard_map/ppermute | solution.py:34
  147.3 8.6 %collective-permute-start.14 = (bf16[320,512]{1,0:T(8,128)(2,1)S(1)}, bf16[320,512]{1,0:T(8,128)(2,1)S(1)}, u32[]{:S(2)}, u32[]{:S(2)}) collective-permute-start(bf16[320,512]{1,0:T(8,128)(2,1)S(1)} %get-tuple-element.50), channel_id=1, source_target_pairs={{0,1},{1,0},{2,3},{3,2},{4,5},{5,4},{6,7},{7,6},{8,9},{9,8},{10,11... | collective-permute-start | bytes 983048 | tf_op jit(solution)/shard_map/ppermute | solution.py:34
  156.1 8.4 %collective-permute-start.18 = (bf16[320,512]{1,0:T(8,128)(2,1)S(1)}, bf16[320,512]{1,0:T(8,128)(2,1)S(1)}, u32[]{:S(2)}, u32[]{:S(2)}) collective-permute-start(bf16[320,512]{1,0:T(8,128)(2,1)S(1)} %fusion.5), channel_id=1, source_target_pairs={{0,96},{16,112},{32,64},{48,80},{64,32},{80,48},{96,0},{112,16},{1... | collective-permute-start | bytes 983048 | tf_op jit(solution)/shard_map/ppermute | solution.py:38
  157.0 7.5 %collective-permute-start.17 = (bf16[320,512]{1,0:T(8,128)(2,1)S(1)}, bf16[320,512]{1,0:T(8,128)(2,1)S(1)}, u32[]{:S(2)}, u32[]{:S(2)}) collective-permute-start(bf16[320,512]{1,0:T(8,128)(2,1)S(1)} %fusion.5), channel_id=1, source_target_pairs={{0,32},{16,48},{32,0},{48,16},{64,96},{80,112},{96,64},{112,80},{1... | collective-permute-start | bytes 983048 | tf_op jit(solution)/shard_map/ppermute | solution.py:38
  157.0 15.3 %collective-permute-start.16 = (bf16[320,512]{1,0:T(8,128)(2,1)S(1)}, bf16[320,512]{1,0:T(8,128)(2,1)S(1)}, u32[]{:S(2)}, u32[]{:S(2)}) collective-permute-start(bf16[320,512]{1,0:T(8,128)(2,1)S(1)} %fusion.5), channel_id=1, source_target_pairs={{0,64},{16,80},{32,96},{48,112},{64,0},{80,16},{96,32},{112,48},{1... | collective-permute-start | bytes 983048 | tf_op jit(solution)/shard_map/ppermute | solution.py:38
  172.6 5.1 %collective-permute-start.19 = (f32[320,512]{1,0:T(8,128)S(1)}, f32[320,512]{1,0:T(8,128)S(1)}, u32[]{:S(2)}, u32[]{:S(2)}) collective-permute-start(f32[320,512]{1,0:T(8,128)S(1)} %add_multiply_fusion), channel_id=1, source_target_pairs={{0,16},{16,0},{32,48},{48,32},{64,80},{80,64},{96,112},{112,96},{1... | collective-permute-start | bytes 1966088 | tf_op jit(solution)/shard_map/ppermute | solution.py:42

commit v3 on v2

--- a/solution.py
+++ b/solution.py
@@ -17,6 +17,7 @@
 HALF = 256
 COLS = 2 * HALF
 TOKENS = SEQS * ROWS
+EXTRA = 16
 MIB = 1 << 20
 BOTH = ("dp", "fsdp")
 
@@ -128,18 +129,17 @@
 def second_kernel(place, facts, *refs):
     own, partner, pieces = refs[:4], refs[4:8], refs[8:10]
     (
-        totals_ref, sum_ref, cot_own, cot_partner, scale_own, scale_partner, gain_ref,
+        sum_ref, cot_ref, scale_own, scale_partner, gain_ref,
         kv_ref, scaled_ref, w_ref, pre_ref, sem,
     ) = refs[10:]
     load_weights(place, pieces, w_ref, sem)
     gain = gain_ref[...]
-    totals = totals_ref[...]
+    totals = sum(cot_ref[d, 0, ROWS : ROWS + 1, : 2 * GROUPS].astype(f32) for d in range(SEQS))
     rows = lax.broadcasted_iota(jnp.int32, (ROWS, HEAD), 0)
     i = pl.program_id(0)
-    for side, (tokens, cot_ref, scale_ref) in enumerate(
-        ((own, cot_own, scale_own), (partner, cot_partner, scale_partner))
-    ):
-        pre_ref[...] = product(tokens, w_ref) + sum_ref[side]
+    for side, (tokens, scale_ref) in enumerate(((own, scale_own), (partner, scale_partner))):
+        source = lax.bitwise_xor(place[0], side)
+        pre_ref[side] = product(tokens, w_ref) + sum_ref[side]
         for q in range(SEQ_STEP):
             n = i * SEQ_STEP + q
             slot, live, reward, group = (facts[4 * side + k, n] for k in range(4))
@@ -152,8 +152,8 @@
             coef = coef * scale
             for part in range(COLS // HEAD):
                 columns = pl.ds(part * HEAD, HEAD)
-                values = pre_ref[span, columns] * scale
-                cot = cot_ref[slot, :, columns].astype(f32)
+                values = pre_ref[side, span, columns] * scale
+                cot = cot_ref[slot, source, 0:ROWS, columns].astype(f32)
                 if part < HALF // HEAD:
                     root = lax.rsqrt(jnp.mean(values * values, -1, keepdims=True) + EPS)
                     unit = values * root
@@ -197,8 +197,9 @@
     )(place, *[own] * 4, *[partner] * 4, *weights)
 
 
-def second_call(place, facts, totals, own, partner, weights, sums, cots, scales, k_gain):
-    whole = pl.BlockSpec((SEQS, ROWS, COLS), lambda i, *s: (0, 0, 0))
+def second_call(place, facts, own, partner, weights, sums, cot, scales, k_gain):
+    whole = pl.BlockSpec((SEQS, 2, ROWS, COLS), lambda i, *s: (0, 0, 0, 0))
+    cots = pl.BlockSpec((SEQS, 2, ROWS + EXTRA, COLS), lambda i, *s: (0, 0, 0, 0))
     wide = pl.BlockSpec((STEP, HEAD), lambda i, *s: (i, 0))
     return pl.pallas_call(
         second_kernel,
@@ -207,14 +208,10 @@
             grid=(TOKENS // STEP,),
             in_specs=token_specs(other_pair)
             + [ANY_SPEC] * 2
-            + [pl.BlockSpec((1, 2 * GROUPS), lambda i, *s: (0, 0))]
-            + [SUM_SPEC, whole, whole, wide, wide]
+            + [SUM_SPEC, cots, wide, wide]
             + [pl.BlockSpec((1, HEAD), lambda i, *s: (0, 0))],
-            out_specs=[
-                pl.BlockSpec((SEQS, 2, ROWS, COLS), lambda i, *s: (0, 0, 0, 0)),
-                SUM_SPEC,
-            ],
-            scratch_shapes=[W_SCRATCH, pltpu.VMEM((STEP, COLS), f32), pltpu.SemaphoreType.DMA],
+            out_specs=[whole, SUM_SPEC],
+            scratch_shapes=[W_SCRATCH, pltpu.VMEM((2, STEP, COLS), f32), pltpu.SemaphoreType.DMA],
         ),
         out_shape=[
             jax.ShapeDtypeStruct((SEQS, 2, ROWS, COLS), bf16),
@@ -224,7 +221,7 @@
         cost_estimate=COST,
         name="project_second",
     )(
-        place, facts, *[own] * 4, *[partner] * 4, *weights, totals, sums, *cots, *scales,
+        place, facts, *[own] * 4, *[partner] * 4, *weights, sums, cot, *scales,
         k_gain.reshape(1, HEAD),
     )
 
@@ -281,12 +278,11 @@
     member = (group_ids[:, None] == jnp.arange(GROUPS, dtype=jnp.int32)[None, :]).astype(f32)
     return jnp.concatenate(
         [jnp.sum(member * scores[:, None], 0), jnp.sum(member * (scores * scores)[:, None], 0)]
-    ).reshape(1, 1, 2 * GROUPS)
-
-
-def summed_over(sums, axis):
-    sums = jnp.broadcast_to(sums, (lax.axis_size(axis), 1, 2 * GROUPS))
-    return lax.all_to_all(sums, axis, 0, 0, tiled=True).sum(0, keepdims=True)
+    ).reshape(1, 2 * GROUPS)
+
+
+def as_rows(sums):
+    return jnp.pad(sums.astype(bf16), ((0, EXTRA - 1), (0, COLS - 2 * GROUPS)))
 
 
 def columns_of(core, array):
@@ -317,24 +313,32 @@
     facts = jnp.concatenate([facts, to_partner(facts)])
 
     mine = (columns_of(core, kv_weight).astype(f32) * gain).astype(bf16)
-    totals = summed_over(group_sums(rewards, group_ids), "dp")
-    piece = jnp.concatenate([mine] + [along(mine, False, n) for n in (1, 2, 3)])
+    sums = group_sums(rewards, group_ids)
+    sums = sums + sum(along(sums, True, m) for m in (1, 2, 3))
+    mine = jnp.concatenate([mine, as_rows(sums)])
+    blocks = [mine] + [along(mine, False, n) for n in (1, 2, 3)]
+    piece = jnp.concatenate([block[:BLOCK] for block in blocks])
     pieces = [piece] + [along(piece, True, m) for m in (1, 2, 3)]
 
-    kv_cotangent, _ = lax.optimization_barrier((kv_cotangent, totals))
-    cot = lax.all_to_all(kv_cotangent, "dp", split_axis=0, concat_axis=0, tiled=True)
-    swapped, totals, _ = lax.optimization_barrier((hidden_in, totals, piece))
+    totals = sum(block[BLOCK : BLOCK + 1, : 2 * GROUPS].astype(f32) for block in blocks)
+
+    k0, k1, v0, v1 = (
+        kv_cotangent[..., i * HALF : (i + 1) * HALF].reshape(4, 2, ROWS, HALF) for i in range(4)
+    )
+    cot = jnp.stack([jnp.concatenate([k0, v0], -1), jnp.concatenate([k1, v1], -1)], 1)
+    totals = jnp.broadcast_to(as_rows(totals), (SEQS, 2, EXTRA, COLS))
+    cot = jnp.concatenate([cot.reshape(SEQS, 2, ROWS, COLS), totals], 2)
+    cot = lax.all_to_all(cot, "dp", split_axis=0, concat_axis=0, tiled=True)
+
+    swapped, _ = lax.optimization_barrier((hidden_in, piece))
     partner = to_partner(swapped)
-    totals = summed_over(totals, "fsdp").reshape(1, 2 * GROUPS)
 
     scale = scale_call(hidden_in)
-    cot, scale, totals = lax.optimization_barrier((cot, scale, totals))
-    cots = columns_of(core, cot), to_partner(columns_of(1 - core, cot))
 
     scales = scale, to_partner(scale)
     sums = first_call(place, hidden_in, partner, pieces[:2])
     kv, scaled = second_call(
-        place, facts, totals, hidden_in, partner, pieces[2:], sums, cots, scales, k_gain
+        place, facts, hidden_in, partner, pieces[2:], sums, cot, scales, k_gain
     )
     kv = lax.all_to_all(kv, "dp", split_axis=0, concat_axis=0, tiled=True)
 

time: 180 us -> 165 us (0.917)
  blocking collectives: 10.9 us -> 0 us
  waiting for transfers between devices: 54.6 us -> 50.9 us
  other arithmetic: 6.91 us -> 9.46 us
    all_to_all x2 -> x1, waiting for transfers between devices: 21.9 us -> 0.01 us  [on_device(): cot = lax.all_to_all(cot, 'dp', split_axis=0, concat_axis=0, tiled=True)]
    ppermute x12 -> x15, waiting for transfers between devices: 23.1 us -> 41.4 us  [along(): return lax.ppermute(value, BOTH, pairs)]
    all_to_all x1 -> x0, blocking collectives: 10.9 us -> none  [summed_over(): return lax.all_to_all(sums, axis, 0, 0, tiled=True).sum(0, keepdims=True)]
    all_to_all x2 -> x1, starting transfers between devices: 12.6 us -> 4.86 us  [on_device(): cot = lax.all_to_all(cot, 'dp', split_axis=0, concat_axis=0, tiled=True)]
    ppermute x12 -> x15, starting transfers between devices: 12.6 us -> 18.3 us  [along(): return lax.ppermute(value, BOTH, pairs)]
    ppermute x5 -> x4, starting transfers between devices: 5.71 us -> 7.14 us  [to_partner(): return lax.ppermute(value, 'dp', [(i, i ^ 1) for i in range(8)])]
  transfers between devices with their start and end apart: 23 -> 24, of which waited for: 8 -> 13; matrix products, arithmetic and copies ran while one was open for 6% -> 7% of each run, Pallas kernels for 17% -> 18%
where the time goes in v3:
time: 165 us
  Pallas kernels  55.5 us (34%)
  waiting for transfers between devices  50.9 us (31%)
  starting transfers between devices  39.6 us (24%)
  other arithmetic  9.46 us (6%)
  local copies, waits for them, and re-layouts  8.3 us (5%)
    ppermute x15, waiting for transfers between devices, along(): return lax.ppermute(value, BOTH, pairs)  41.4 us
    pallas_call x2, Pallas kernels, gradient_call(): pl.pallas_call(gradient_kernel, grid_spec=pltpu.PrefetchScalarGridSpec(nu...  20 us
    ppermute x15, starting transfers between devices, along(): return lax.ppermute(value, BOTH, pairs)  18.3 us
    pallas_call x1, Pallas kernels, second_call(): pl.pallas_call(second_kernel, grid_spec=pltpu.PrefetchScalarGridSpec(num_...  15.7 us
    pallas_call x1, Pallas kernels, first_call(): pl.pallas_call(first_kernel, grid_spec=pltpu.PrefetchScalarGridSpec(num_s...  12.5 us
    ppermute x3, waiting for transfers between devices, along_x(): return lax.ppermute(value, 'dp', [(i, i ^ 2 * flip) for i in range(8)])  7.72 us
    pallas_call x1, Pallas kernels, scale_call(): pl.pallas_call(scale_kernel, grid=(SEQS,), in_specs=[pl.BlockSpec((1, ROW...  7.35 us
    ppermute x4, starting transfers between devices, to_partner(): return lax.ppermute(value, 'dp', [(i, i ^ 1) for i in range(8)])  7.14 us
  transfers between devices with their start and end apart: 24, of which 13 were waited for; matrix products, arithmetic and copies ran while one was open for 7% of the time, Pallas kernels for 18%

profile of v3, /device:TPU:1, one launch (start us, length us, event | category | flops | bytes accessed | tf_op | source)
XLA Modules:
  0.0 164.6 jit_solution(8873892044559400935)
XLA Ops:
  0.6 0.7 convert_multiply_fusion
  1.3 0.7 convert_element_type.81
  1.9 0.7 select_reduce_fusion.1
  2.8 4.6 %collective-permute-start.3 = (f32[1,128]{1,0:T(1,128)S(1)}, f32[1,128]{1,0:T(1,128)S(1)}, u32[]{:S(2)}, u32[]{:S(2)}) collective-permute-start(f32[1,128]{1,0:T(1,128)S(1)} %maximum_bitcast_fusion.2), channel_id=1, source_target_pairs={{0,12},{1,13},{2,14},{3,15},{4,8},{5,9},{6,10},{7,11},{8,4},{9,5},... | collective-permute-start | bytes 1544 | tf_op jit(solution)/shard_map/ppermute | solution.py:35
  7.4 0.7 collective-permute-start.1
  8.0 1.2 fusion.18
  9.2 0.8 dynamic_slice.3
  10.2 1.1 collective-permute-done.2
  11.3 2.8 %collective-permute-start.6 = (bf16[336,512]{1,0:T(8,128)(2,1)S(1)}, bf16[336,512]{1,0:T(8,128)(2,1)S(1)}, u32[]{:S(2)}, u32[]{:S(2)}) collective-permute-start(bf16[336,512]{1,0:T(8,128)(2,1)S(1)} %fusion.8), channel_id=1, source_target_pairs={{0,3},{1,2},{2,1},{3,0},{4,7},{5,6},{6,5},{7,4},{8,11},{9,10},{10,... | collective-permute-start | bytes 1032200 | tf_op jit(solution)/shard_map/ppermute | solution.py:35
  14.8 8.0 %collective-permute-done.6 = bf16[336,512]{1,0:T(8,128)(2,1)S(1)} collective-permute-done((bf16[336,512]{1,0:T(8,128)(2,1)S(1)}, bf16[336,512]{1,0:T(8,128)(2,1)S(1)}, u32[]{:S(2)}, u32[]{:S(2)}) %collective-permute-start.6) | collective-permute-done | bytes 344096 | tf_op jit(solution)/shard_map/ppermute | solution.py:35
  22.8 0.6 collective-permute-done.4
  23.6 3.0 %collective-permute-start.7 = (bf16[8,128,5120]{2,1,0:T(8,128)(2,1)}, bf16[8,128,5120]{2,1,0:T(8,128)(2,1)}, u32[]{:S(2)}, u32[]{:S(2)}) collective-permute-start(bf16[8,128,5120]{2,1,0:T(8,128)(2,1)} %own_ref.3), channel_id=1, source_target_pairs={{0,16},{16,0},{32,48},{48,32},{64,80},{80,64},{96,112},{112,96},{1... | collective-permute-start | bytes 31457288 | tf_op jit(solution)/shard_map/ppermute | solution.py:43
  27.3 1.7 %pad_maximum_fusion = bf16[8,2,144,512]{3,2,1,0:T(8,128)(2,1)} fusion(bf16[8,2,16,512]{3,2,1,0:T(8,128)(2,1)S(1)} %broadcast_in_dim.2, bf16[8,2,128,512]{3,2,1,0:T(8,128)(2,1)S(1)} %bitcast.41), kind=kLoop, calls=%fused_computation.4 | loop fusion | flops 4718592 | bytes 4718592 | tf_op jit(solution)/shard_map/concatenate | solution.py:330
  29.0 4.9 %all-to-all-start = ((bf16[8,2,144,512]{3,2,1,0:T(8,128)(2,1)}), bf16[8,2,144,512]{3,2,1,0:T(8,128)(2,1)}, u32[]{:S(2)}, u32[]{:S(2)}) async-start(bf16[8,2,144,512]{3,2,1,0:T(8,128)(2,1)} %pad_maximum_fusion), calls=%async_computation | async-start | bytes 4718592 | tf_op jit(solution)/shard_map/all_to_all | solution.py:331
  33.9 0.5 collective-permute-start.10
  34.3 2.5 %collective-permute-start.9 = (bf16[1280,512]{1,0:T(8,128)(2,1)S(1)}, bf16[1280,512]{1,0:T(8,128)(2,1)S(1)}, u32[]{:S(2)}, u32[]{:S(2)}) collective-permute-start(bf16[1280,512]{1,0:T(8,128)(2,1)S(1)} %pad_maximum_fusion.2.refs_8_), channel_id=1, source_target_pairs={{0,12},{1,13},{2,14},{3,15},{4,8},{5,9},{6,10},{7,11},{8,4},{9,5},... | collective-permute-start | bytes 3932168 | tf_op jit(solution)/shard_map/ppermute | solution.py:35
  36.8 1.2 collective-permute-start.8
  38.2 7.3 %token_scale.1.refs_12_ = f32[1024,128]{1,0:T(8,128)S(1)} custom-call(bf16[8,128,5120]{2,1,0:T(8,128)(2,1)} %own_ref.3), custom_call_target="tpu_custom_call" | custom-call | flops 1 | bytes 1 | tf_op jit(solution)/shard_map/token_scale/pallas_call | solution.py:70
  45.6 0.5 collective-permute-start.11
  46.2 4.6 %collective-permute-done.10.refs_9_ = bf16[1280,512]{1,0:T(8,128)(2,1)} collective-permute-done((bf16[1280,512]{1,0:T(8,128)(2,1)S(1)}, bf16[1280,512]{1,0:T(8,128)(2,1)}, u32[]{:S(2)}, u32[]{:S(2)}) %collective-permute-start.10) | collective-permute-done | bytes 1310752 | tf_op jit(solution)/shard_map/ppermute | solution.py:35
  50.7 12.5 %project_first.1.refs_10_ = f32[2,1024,512]{2,1,0:T(8,128)} custom-call(s32[3]{0:T(128)S(1)} %pad_add_fusion.1.place, bf16[8,128,5120]{2,1,0:T(8,128)(2,1)} %own_ref.3, bf16[8,128,5120]{2,1,0:T(8,128)(2,1)} %own_ref.3, bf16[8,128,5120]{2,1,0:T(8,128)(2,1)} %own_ref.3, bf16[8,128,5120]{2,1,0:T(8,128)(2,1)} %own_ref.3, ...), custom_call_target="tpu_custom_call" | custom-call | flops 1 | bytes 1 | tf_op jit(solution)/shard_map/project_first/pallas_call | solution.py:184
  63.2 2.2 %collective-permute-done.9.refs_9_ = bf16[1280,512]{1,0:T(8,128)(2,1)S(1)} collective-permute-done((bf16[1280,512]{1,0:T(8,128)(2,1)S(1)}, bf16[1280,512]{1,0:T(8,128)(2,1)S(1)}, u32[]{:S(2)}, u32[]{:S(2)}) %collective-permute-start.9) | collective-permute-done | bytes 1310752 | tf_op jit(solution)/shard_map/ppermute | solution.py:35
  65.4 1.7 %collective-permute-done.8.refs_8_ = bf16[1280,512]{1,0:T(8,128)(2,1)} collective-permute-done((bf16[1280,512]{1,0:T(8,128)(2,1)S(1)}, bf16[1280,512]{1,0:T(8,128)(2,1)}, u32[]{:S(2)}, u32[]{:S(2)}) %collective-permute-start.8) | collective-permute-done | bytes 1310752 | tf_op jit(solution)/shard_map/ppermute | solution.py:35
  67.1 15.7 %project_second.1 = (bf16[8,2,128,512]{3,2,1,0:T(8,128)(2,1)}, bf16[2,1024,512]{2,1,0:T(8,128)(2,1)}) custom-call(s32[3]{0:T(128)S(1)} %pad_add_fusion.1.place, s32[8,8]{1,0:T(8,128)S(1)} %concatenate.34.facts, bf16[8,128,5120]{2,1,0:T(8,128)(2,1)} %own_ref.3, bf16[8,128,5120]{2,1,0:T(8,128)(2,1)} %own_ref.3, bf16[8,128,5120]{2,1,0:T(8,128)(2,1)} %own_ref.3, ...), custom_call_target="tpu_custom_call" | custom-call | flops 1 | bytes 1 | tf_op jit(solution)/shard_map/project_second/pallas_call | solution.py:204
  82.8 1.6 copy-done
  84.4 10.0 %weight_gradient.3 = (bf16[4,320,512]{2,1,0:T(8,128)(2,1)}, bf16[4,320,512]{2,1,0:T(8,128)(2,1)S(1)}) custom-call(s32[3]{0:T(128)S(1)} %pad_add_fusion.1.place, bf16[8,128,5120]{2,1,0:T(8,128)(2,1)} %own_ref.3, bf16[8,128,5120]{2,1,0:T(8,128)(2,1)} %collective-permute-done.7.refs_4_.refs_5_.refs_6_.refs_7_.partner_ref, bf16[2,1024,512]{2,1,0:T(8,128)(2,1)S(1)} %copy-done), custom_call_target="tpu_custom_call" | custom-call | flops 1 | bytes 1 | tf_op jit(solution)/shard_map/weight_gradient/pallas_call | solution.py:261
  94.4 1.7 %collective-permute-start.12 = (bf16[4,320,512]{2,1,0:T(8,128)(2,1)}, bf16[4,320,512]{2,1,0:T(8,128)(2,1)}, u32[]{:S(2)}, u32[]{:S(2)}) collective-permute-start(bf16[4,320,512]{2,1,0:T(8,128)(2,1)} %get-tuple-element.17), channel_id=1, source_target_pairs={{0,8},{1,9},{2,10},{3,11},{4,12},{5,13},{6,14},{7,15},{8,0},{9,1},... | collective-permute-start | bytes 3932168 | tf_op jit(solution)/shard_map/ppermute | solution.py:35
  96.2 0.5 collective-permute-start.13
  96.7 10.0 %weight_gradient.2 = (bf16[4,320,512]{2,1,0:T(8,128)(2,1)S(1)}, bf16[4,320,512]{2,1,0:T(8,128)(2,1)}) custom-call(s32[3]{0:T(128)S(1)} %pad_add_fusion.1.place, bf16[8,128,5120]{2,1,0:T(8,128)(2,1)} %own_ref.3, bf16[8,128,5120]{2,1,0:T(8,128)(2,1)} %collective-permute-done.7.refs_4_.refs_5_.refs_6_.refs_7_.partner_ref, bf16[2,1024,512]{2,1,0:T(8,128)(2,1)S(1)} %copy-done), custom_call_target="tpu_custom_call" | custom-call | flops 1 | bytes 1 | tf_op jit(solution)/shard_map/weight_gradient/pallas_call | solution.py:261
  107.0 5.3 %all-to-all-start.1 = ((bf16[8,2,128,512]{3,2,1,0:T(8,128)(2,1)}), bf16[8,2,128,512]{3,2,1,0:T(8,128)(2,1)}, u32[]{:S(2)}, u32[]{:S(2)}) async-start(bf16[8,2,128,512]{3,2,1,0:T(8,128)(2,1)} %get-tuple-element.14), calls=%async_computation.1 | async-start | bytes 4194304 | tf_op jit(solution)/shard_map/all_to_all | solution.py:343
  112.4 0.7 collective-permute-done.12
  113.0 14.0 %collective-permute-done.13 = bf16[4,320,512]{2,1,0:T(8,128)(2,1)} collective-permute-done((bf16[4,320,512]{2,1,0:T(8,128)(2,1)S(1)}, bf16[4,320,512]{2,1,0:T(8,128)(2,1)}, u32[]{:S(2)}, u32[]{:S(2)}) %collective-permute-start.13) | collective-permute-done | bytes 1310752 | tf_op jit(solution)/shard_map/ppermute | solution.py:35
  127.0 2.9 %fusion.13 = (bf16[4,320,512]{2,1,0:T(8,128)(2,1)S(1)}, f32[4,320,512]{2,1,0:T(8,128)S(1)}) fusion(bf16[4,320,512]{2,1,0:T(8,128)(2,1)} %collective-permute-done.14, bf16[4,320,512]{2,1,0:T(8,128)(2,1)} %collective-permute-done.13, bf16[4,320,512]{2,1,0:T(8,128)(2,1)} %collective-permute-done.12, bf16[4,320,512]{2,1,0:T(8,128)(2,1)S(1)} %get-tuple-element.16), kind=kLoop, calls=%fused_computation.47 | loop fusion | flops 5242880 | bytes 9175040 | tf_op jit(solution)/shard_map/convert.2
  130.0 1.8 %collective-permute-start.15 = (bf16[320,512]{1,0:T(8,128)(2,1)S(1)}, bf16[320,512]{1,0:T(8,128)(2,1)S(1)}, u32[]{:S(2)}, u32[]{:S(2)}) collective-permute-start(bf16[320,512]{1,0:T(8,128)(2,1)S(1)} %get-tuple-element.36), channel_id=1, source_target_pairs={{0,2},{1,3},{2,0},{3,1},{4,6},{5,7},{6,4},{7,5},{8,10},{9,11},{10,... | collective-permute-start | bytes 983048 | tf_op jit(solution)/shard_map/ppermute | solution.py:35
  131.8 0.5 collective-permute-start.17
  132.3 0.4 collective-permute-start.16
  132.7 5.2 %collective-permute-done.15 = bf16[320,512]{1,0:T(8,128)(2,1)S(1)} collective-permute-done((bf16[320,512]{1,0:T(8,128)(2,1)S(1)}, bf16[320,512]{1,0:T(8,128)(2,1)S(1)}, u32[]{:S(2)}, u32[]{:S(2)}) %collective-permute-start.15) | collective-permute-done | bytes 327712 | tf_op jit(solution)/shard_map/ppermute | solution.py:35
  138.0 3.4 %collective-permute-done.17 = bf16[320,512]{1,0:T(8,128)(2,1)S(1)} collective-permute-done((bf16[320,512]{1,0:T(8,128)(2,1)S(1)}, bf16[320,512]{1,0:T(8,128)(2,1)S(1)}, u32[]{:S(2)}, u32[]{:S(2)}) %collective-permute-start.17) | collective-permute-done | bytes 327712 | tf_op jit(solution)/shard_map/ppermute | solution.py:35
  141.5 2.7 %collective-permute-start.20 = (bf16[320,512]{1,0:T(8,128)(2,1)S(1)}, bf16[320,512]{1,0:T(8,128)(2,1)S(1)}, u32[]{:S(2)}, u32[]{:S(2)}) collective-permute-start(bf16[320,512]{1,0:T(8,128)(2,1)S(1)} %fusion.6), channel_id=1, source_target_pairs={{0,96},{16,112},{32,64},{48,80},{64,32},{80,48},{96,0},{112,16},{1... | collective-permute-start | bytes 983048 | tf_op jit(solution)/shard_map/ppermute | solution.py:39
  144.2 1.3 collective-permute-start.18
  145.5 1.3 copy_bitcast_fusion
  146.8 1.3 slice_bitcast_fusion.2
  148.6 1.5 copy.16
  150.1 0.7 collective-permute-done.19
  150.8 7.0 %collective-permute-done.18 = bf16[320,512]{1,0:T(8,128)(2,1)S(1)} collective-permute-done((bf16[320,512]{1,0:T(8,128)(2,1)S(1)}, bf16[320,512]{1,0:T(8,128)(2,1)S(1)}, u32[]{:S(2)}, u32[]{:S(2)}) %collective-permute-start.18) | collective-permute-done | bytes 327712 | tf_op jit(solution)/shard_map/ppermute | solution.py:39
  158.0 3.4 %collective-permute-start.21 = (f32[320,512]{1,0:T(8,128)S(1)}, f32[320,512]{1,0:T(8,128)S(1)}, u32[]{:S(2)}, u32[]{:S(2)}) collective-permute-start(f32[320,512]{1,0:T(8,128)S(1)} %add_multiply_fusion), channel_id=1, source_target_pairs={{0,16},{16,0},{32,48},{48,32},{64,80},{80,64},{96,112},{112,96},{1... | collective-permute-start | bytes 1966088 | tf_op jit(solution)/shard_map/ppermute | solution.py:43
  161.4 1.7 %collective-permute-done.21 = f32[320,512]{1,0:T(8,128)S(1)} collective-permute-done((f32[320,512]{1,0:T(8,128)S(1)}, f32[320,512]{1,0:T(8,128)S(1)}, u32[]{:S(2)}, u32[]{:S(2)}) %collective-permute-start.21) | collective-permute-done | bytes 655392 | tf_op jit(solution)/shard_map/ppermute | solution.py:43
  163.4 1.2 pad_maximum_fusion.3
  (56 shorter events, 3.6 us)
Async XLA Ops:
  2.8 7.4 %collective-permute-start.3 = (f32[1,128]{1,0:T(1,128)S(1)}, f32[1,128]{1,0:T(1,128)S(1)}, u32[]{:S(2)}, u32[]{:S(2)}) collective-permute-start(f32[1,128]{1,0:T(1,128)S(1)} %maximum_bitcast_fusion.2), channel_id=1, source_target_pairs={{0,12},{1,13},{2,14},{3,15},{4,8},{5,9},{6,10},{7,11},{8,4},{9,5},... | collective-permute-start | bytes 1544 | tf_op jit(solution)/shard_map/ppermute | solution.py:35
  7.4 3.9 %collective-permute-start.2 = (f32[1,128]{1,0:T(1,128)S(1)}, f32[1,128]{1,0:T(1,128)S(1)}, u32[]{:S(2)}, u32[]{:S(2)}) collective-permute-start(f32[1,128]{1,0:T(1,128)S(1)} %maximum_bitcast_fusion.2), channel_id=1, source_target_pairs={{0,8},{1,9},{2,10},{3,11},{4,12},{5,13},{6,14},{7,15},{8,0},{9,1},... | collective-permute-start | bytes 1544 | tf_op jit(solution)/shard_map/ppermute | solution.py:35
  7.4 3.9 %collective-permute-start.1 = (f32[1,128]{1,0:T(1,128)S(1)}, f32[1,128]{1,0:T(1,128)S(1)}, u32[]{:S(2)}, u32[]{:S(2)}) collective-permute-start(f32[1,128]{1,0:T(1,128)S(1)} %maximum_bitcast_fusion.2), channel_id=1, source_target_pairs={{0,4},{1,5},{2,6},{3,7},{4,0},{5,1},{6,2},{7,3},{8,12},{9,13},{10,... | collective-permute-start | bytes 1544 | tf_op jit(solution)/shard_map/ppermute | solution.py:35
  11.3 11.4 %collective-permute-start.6 = (bf16[336,512]{1,0:T(8,128)(2,1)S(1)}, bf16[336,512]{1,0:T(8,128)(2,1)S(1)}, u32[]{:S(2)}, u32[]{:S(2)}) collective-permute-start(bf16[336,512]{1,0:T(8,128)(2,1)S(1)} %fusion.8), channel_id=1, source_target_pairs={{0,3},{1,2},{2,1},{3,0},{4,7},{5,6},{6,5},{7,4},{8,11},{9,10},{10,... | collective-permute-start | bytes 1032200 | tf_op jit(solution)/shard_map/ppermute | solution.py:35
  14.1 8.7 %collective-permute-start.5 = (bf16[336,512]{1,0:T(8,128)(2,1)S(1)}, bf16[336,512]{1,0:T(8,128)(2,1)S(1)}, u32[]{:S(2)}, u32[]{:S(2)}) collective-permute-start(bf16[336,512]{1,0:T(8,128)(2,1)S(1)} %fusion.8), channel_id=1, source_target_pairs={{0,2},{1,3},{2,0},{3,1},{4,6},{5,7},{6,4},{7,5},{8,10},{9,11},{10,... | collective-permute-start | bytes 1032200 | tf_op jit(solution)/shard_map/ppermute | solution.py:35
  14.5 9.0 %collective-permute-start.4 = (bf16[336,512]{1,0:T(8,128)(2,1)S(1)}, bf16[336,512]{1,0:T(8,128)(2,1)S(1)}, u32[]{:S(2)}, u32[]{:S(2)}) collective-permute-start(bf16[336,512]{1,0:T(8,128)(2,1)S(1)} %fusion.8), channel_id=1, source_target_pairs={{0,1},{1,0},{2,3},{3,2},{4,5},{5,4},{6,7},{7,6},{8,9},{9,8},{10,11... | collective-permute-start | bytes 1032200 | tf_op jit(solution)/shard_map/ppermute | solution.py:35
  22.8 3.8 %copy-start.2 = (bf16[8,128,1024]{2,1,0:T(8,128)(2,1)S(1)}, bf16[8,128,1024]{2,1,0:T(8,128)(2,1)}, u32[]{:S(2)}) copy-start(bf16[8,128,1024]{2,1,0:T(8,128)(2,1)} %param.17) | copy-start | bytes 6291460
  23.6 27.1 %collective-permute-start.7 = (bf16[8,128,5120]{2,1,0:T(8,128)(2,1)}, bf16[8,128,5120]{2,1,0:T(8,128)(2,1)}, u32[]{:S(2)}, u32[]{:S(2)}) collective-permute-start(bf16[8,128,5120]{2,1,0:T(8,128)(2,1)} %own_ref.3), channel_id=1, source_target_pairs={{0,16},{16,0},{32,48},{48,32},{64,80},{80,64},{96,112},{112,96},{1... | collective-permute-start | bytes 31457288 | tf_op jit(solution)/shard_map/ppermute | solution.py:43
  29.0 9.0 %copy-start.3 = (s32[8]{0:T(128)S(1)}, s32[8]{0:T(128)}, u32[]{:S(2)}) copy-start(s32[8]{0:T(128)} %param.16) | copy-start | bytes 100
  29.0 9.0 %copy-start.4 = (s32[1,8]{1,0:T(1,128)S(1)}, s32[1,8]{1,0:T(1,128)}, u32[]{:S(2)}) copy-start(s32[1,8]{1,0:T(1,128)} %param.13) | copy-start | bytes 100
  29.0 9.0 %copy-start.5 = (s32[8]{0:T(128)S(1)}, s32[8]{0:T(128)}, u32[]{:S(2)}) copy-start(s32[8]{0:T(128)} %param.14) | copy-start | bytes 100
  29.0 9.0 %copy-start.6 = (s32[8]{0:T(128)S(1)}, s32[8]{0:T(128)}, u32[]{:S(2)}) copy-start(s32[8]{0:T(128)} %param.15) | copy-start | bytes 100
  29.0 38.1 %all-to-all-start = ((bf16[8,2,144,512]{3,2,1,0:T(8,128)(2,1)}), bf16[8,2,144,512]{3,2,1,0:T(8,128)(2,1)}, u32[]{:S(2)}, u32[]{:S(2)}) async-start(bf16[8,2,144,512]{3,2,1,0:T(8,128)(2,1)} %pad_maximum_fusion), calls=%async_computation | async-start | bytes 4718592 | tf_op jit(solution)/shard_map/all_to_all | solution.py:331
  33.9 16.9 %collective-permute-start.10 = (bf16[1280,512]{1,0:T(8,128)(2,1)S(1)}, bf16[1280,512]{1,0:T(8,128)(2,1)}, u32[]{:S(2)}, u32[]{:S(2)}) collective-permute-start(bf16[1280,512]{1,0:T(8,128)(2,1)S(1)} %pad_maximum_fusion.2.refs_8_), channel_id=1, source_target_pairs={{0,4},{1,5},{2,6},{3,7},{4,0},{5,1},{6,2},{7,3},{8,12},{9,13},{10,... | collective-permute-start | bytes 3932168 | tf_op jit(solution)/shard_map/ppermute | solution.py:35
  34.3 31.1 %collective-permute-start.9 = (bf16[1280,512]{1,0:T(8,128)(2,1)S(1)}, bf16[1280,512]{1,0:T(8,128)(2,1)S(1)}, u32[]{:S(2)}, u32[]{:S(2)}) collective-permute-start(bf16[1280,512]{1,0:T(8,128)(2,1)S(1)} %pad_maximum_fusion.2.refs_8_), channel_id=1, source_target_pairs={{0,12},{1,13},{2,14},{3,15},{4,8},{5,9},{6,10},{7,11},{8,4},{9,5},... | collective-permute-start | bytes 3932168 | tf_op jit(solution)/shard_map/ppermute | solution.py:35
  36.8 30.3 %collective-permute-start.8 = (bf16[1280,512]{1,0:T(8,128)(2,1)S(1)}, bf16[1280,512]{1,0:T(8,128)(2,1)}, u32[]{:S(2)}, u32[]{:S(2)}) collective-permute-start(bf16[1280,512]{1,0:T(8,128)(2,1)S(1)} %pad_maximum_fusion.2.refs_8_), channel_id=1, source_target_pairs={{0,8},{1,9},{2,10},{3,11},{4,12},{5,13},{6,14},{7,15},{8,0},{9,1},... | collective-permute-start | bytes 3932168 | tf_op jit(solution)/shard_map/ppermute | solution.py:35
  38.0 7.6 %collective-permute-start = (s32[4,8]{1,0:T(4,128)S(1)}, s32[4,8]{1,0:T(4,128)S(1)}, u32[]{:S(2)}, u32[]{:S(2)}) collective-permute-start(s32[4,8]{1,0:T(4,128)S(1)} %pad_add_fusion), channel_id=1, source_target_pairs={{0,16},{16,0},{32,48},{48,32},{64,80},{80,64},{96,112},{112,96},{1... | collective-permute-start | bytes 392 | tf_op jit(solution)/shard_map/ppermute | solution.py:43
  45.6 17.6 %collective-permute-start.11 = (f32[1024,128]{1,0:T(8,128)S(1)}, f32[1024,128]{1,0:T(8,128)}, u32[]{:S(2)}, u32[]{:S(2)}) collective-permute-start(f32[1024,128]{1,0:T(8,128)S(1)} %token_scale.1.refs_12_), channel_id=1, source_target_pairs={{0,16},{16,0},{32,48},{48,32},{64,80},{80,64},{96,112},{112,96},{1... | collective-permute-start | bytes 1572872 | tf_op jit(solution)/shard_map/ppermute | solution.py:43
  46.2 21.0 %copy-start.1 = (f32[128]{0:T(128)S(1)}, f32[128]{0:T(128)}, u32[]{:S(2)}) copy-start(f32[128]{0:T(128)} %param.12) | copy-start | bytes 1540
  82.8 1.6 copy-start
  94.4 18.6 %collective-permute-start.12 = (bf16[4,320,512]{2,1,0:T(8,128)(2,1)}, bf16[4,320,512]{2,1,0:T(8,128)(2,1)}, u32[]{:S(2)}, u32[]{:S(2)}) collective-permute-start(bf16[4,320,512]{2,1,0:T(8,128)(2,1)} %get-tuple-element.17), channel_id=1, source_target_pairs={{0,8},{1,9},{2,10},{3,11},{4,12},{5,13},{6,14},{7,15},{8,0},{9,1},... | collective-permute-start | bytes 3932168 | tf_op jit(solution)/shard_map/ppermute | solution.py:35
  96.2 30.9 %collective-permute-start.13 = (bf16[4,320,512]{2,1,0:T(8,128)(2,1)S(1)}, bf16[4,320,512]{2,1,0:T(8,128)(2,1)}, u32[]{:S(2)}, u32[]{:S(2)}) collective-permute-start(bf16[4,320,512]{2,1,0:T(8,128)(2,1)S(1)} %get-tuple-element.18), channel_id=1, source_target_pairs={{0,12},{1,13},{2,14},{3,15},{4,8},{5,9},{6,10},{7,11},{8,4},{9,5},... | collective-permute-start | bytes 3932168 | tf_op jit(solution)/shard_map/ppermute | solution.py:35
  106.7 20.4 %collective-permute-start.14 = (bf16[4,320,512]{2,1,0:T(8,128)(2,1)}, bf16[4,320,512]{2,1,0:T(8,128)(2,1)}, u32[]{:S(2)}, u32[]{:S(2)}) collective-permute-start(bf16[4,320,512]{2,1,0:T(8,128)(2,1)} %get-tuple-element.19), channel_id=1, source_target_pairs={{0,4},{1,5},{2,6},{3,7},{4,0},{5,1},{6,2},{7,3},{8,12},{9,13},{10,... | collective-permute-start | bytes 3932168 | tf_op jit(solution)/shard_map/ppermute | solution.py:35
  107.0 34.5 %all-to-all-start.1 = ((bf16[8,2,128,512]{3,2,1,0:T(8,128)(2,1)}), bf16[8,2,128,512]{3,2,1,0:T(8,128)(2,1)}, u32[]{:S(2)}, u32[]{:S(2)}) async-start(bf16[8,2,128,512]{3,2,1,0:T(8,128)(2,1)} %get-tuple-element.14), calls=%async_computation.1 | async-start | bytes 4194304 | tf_op jit(solution)/shard_map/all_to_all | solution.py:343
  130.0 8.0 %collective-permute-start.15 = (bf16[320,512]{1,0:T(8,128)(2,1)S(1)}, bf16[320,512]{1,0:T(8,128)(2,1)S(1)}, u32[]{:S(2)}, u32[]{:S(2)}) collective-permute-start(bf16[320,512]{1,0:T(8,128)(2,1)S(1)} %get-tuple-element.36), channel_id=1, source_target_pairs={{0,2},{1,3},{2,0},{3,1},{4,6},{5,7},{6,4},{7,5},{8,10},{9,11},{10,... | collective-permute-start | bytes 983048 | tf_op jit(solution)/shard_map/ppermute | solution.py:35
  131.8 9.5 %collective-permute-start.17 = (bf16[320,512]{1,0:T(8,128)(2,1)S(1)}, bf16[320,512]{1,0:T(8,128)(2,1)S(1)}, u32[]{:S(2)}, u32[]{:S(2)}) collective-permute-start(bf16[320,512]{1,0:T(8,128)(2,1)S(1)} %get-tuple-element.37), channel_id=1, source_target_pairs={{0,3},{1,2},{2,1},{3,0},{4,7},{5,6},{6,5},{7,4},{8,11},{9,10},{10,... | collective-permute-start | bytes 983048 | tf_op jit(solution)/shard_map/ppermute | solution.py:35
  132.3 9.0 %collective-permute-start.16 = (bf16[320,512]{1,0:T(8,128)(2,1)S(1)}, bf16[320,512]{1,0:T(8,128)(2,1)S(1)}, u32[]{:S(2)}, u32[]{:S(2)}) collective-permute-start(bf16[320,512]{1,0:T(8,128)(2,1)S(1)} %get-tuple-element.38), channel_id=1, source_target_pairs={{0,1},{1,0},{2,3},{3,2},{4,5},{5,4},{6,7},{7,6},{8,9},{9,8},{10,11... | collective-permute-start | bytes 983048 | tf_op jit(solution)/shard_map/ppermute | solution.py:35
  141.5 8.6 %collective-permute-start.20 = (bf16[320,512]{1,0:T(8,128)(2,1)S(1)}, bf16[320,512]{1,0:T(8,128)(2,1)S(1)}, u32[]{:S(2)}, u32[]{:S(2)}) collective-permute-start(bf16[320,512]{1,0:T(8,128)(2,1)S(1)} %fusion.6), channel_id=1, source_target_pairs={{0,96},{16,112},{32,64},{48,80},{64,32},{80,48},{96,0},{112,16},{1... | collective-permute-start | bytes 983048 | tf_op jit(solution)/shard_map/ppermute | solution.py:39
  144.2 6.6 %collective-permute-start.19 = (bf16[320,512]{1,0:T(8,128)(2,1)S(1)}, bf16[320,512]{1,0:T(8,128)(2,1)S(1)}, u32[]{:S(2)}, u32[]{:S(2)}) collective-permute-start(bf16[320,512]{1,0:T(8,128)(2,1)S(1)} %fusion.6), channel_id=1, source_target_pairs={{0,32},{16,48},{32,0},{48,16},{64,96},{80,112},{96,64},{112,80},{1... | collective-permute-start | bytes 983048 | tf_op jit(solution)/shard_map/ppermute | solution.py:39
  144.2 13.6 %collective-permute-start.18 = (bf16[320,512]{1,0:T(8,128)(2,1)S(1)}, bf16[320,512]{1,0:T(8,128)(2,1)S(1)}, u32[]{:S(2)}, u32[]{:S(2)}) collective-permute-start(bf16[320,512]{1,0:T(8,128)(2,1)S(1)} %fusion.6), channel_id=1, source_target_pairs={{0,64},{16,80},{32,96},{48,112},{64,0},{80,16},{96,32},{112,48},{1... | collective-permute-start | bytes 983048 | tf_op jit(solution)/shard_map/ppermute | solution.py:39
  158.0 5.2 %collective-permute-start.21 = (f32[320,512]{1,0:T(8,128)S(1)}, f32[320,512]{1,0:T(8,128)S(1)}, u32[]{:S(2)}, u32[]{:S(2)}) collective-permute-start(f32[320,512]{1,0:T(8,128)S(1)} %add_multiply_fusion), channel_id=1, source_target_pairs={{0,16},{16,0},{32,48},{48,32},{64,80},{80,64},{96,112},{112,96},{1... | collective-permute-start | bytes 1966088 | tf_op jit(solution)/shard_map/ppermute | solution.py:43

commit v4 on v3

--- a/solution.py
+++ b/solution.py
@@ -79,7 +79,7 @@
     )(hidden)
 
 
-SEQ_STEP = 4
+SEQ_STEP = 2
 STEP = SEQ_STEP * ROWS
 
 
@@ -273,12 +273,25 @@
     )(place, own, partner, scaled)
 
 
+def sums_kernel(rewards_ref, groups_ref, sums_ref):
+    lane = lax.broadcasted_iota(jnp.int32, (1, 2 * GROUPS), 1)
+    total = jnp.zeros((1, 2 * GROUPS), jnp.int32)
+    for n in range(SEQS):
+        reward, group = rewards_ref[n], groups_ref[n]
+        total += jnp.where(lane == group, reward, 0)
+        total += jnp.where(lane == group + GROUPS, reward * reward, 0)
+    sums_ref[...] = total.astype(f32)
+
+
 def group_sums(rewards, group_ids):
-    scores = rewards.astype(f32)
-    member = (group_ids[:, None] == jnp.arange(GROUPS, dtype=jnp.int32)[None, :]).astype(f32)
-    return jnp.concatenate(
-        [jnp.sum(member * scores[:, None], 0), jnp.sum(member * (scores * scores)[:, None], 0)]
-    ).reshape(1, 2 * GROUPS)
+    return pl.pallas_call(
+        sums_kernel,
+        in_specs=[pl.BlockSpec(memory_space=pltpu.SMEM)] * 2,
+        out_specs=pl.BlockSpec(memory_space=pltpu.VMEM),
+        out_shape=jax.ShapeDtypeStruct((1, 2 * GROUPS), f32),
+        cost_estimate=COST,
+        name="group_sums",
+    )(rewards, group_ids)
 
 
 def as_rows(sums):
@@ -344,13 +357,14 @@
 
     two, three = gradient_call(other_pair, place, hidden_in, partner, scaled)
     here, one = gradient_call(own_pair, place, hidden_in, partner, scaled)
-    total = (
-        here.astype(f32)
-        + along(two, True, 2).astype(f32)
-        + along(three, True, 3).astype(f32)
-        + along(one, True, 1).astype(f32)
-    )
-    total = sum(along(total[n].astype(bf16), False, n).astype(f32) for n in (2, 1, 3)) + total[0]
+    received = [here, along(two, True, 2), along(three, True, 3), along(one, True, 1)]
+    total = None
+    for n in (2, 1, 3, 0):
+        block = sum(part[n].astype(f32) for part in received)
+        if n:
+            received = lax.optimization_barrier(received)
+            block = along(block.astype(bf16), False, n).astype(f32)
+        total = block if total is None else total + block
     rows = total.astype(bf16)
     kv, rows = lax.optimization_barrier((kv, rows))
     kv = kv.reshape(4, 2, 2, ROWS, COLS)

time: 165 us -> 164 us (level)
  waiting for transfers between devices: 50.9 us -> 47.9 us
    add x0 -> x3, other arithmetic: none -> 4.1 us  [on_device(): block = sum((part[n].astype(f32) for part in received))]
    another operation x1 -> x0, other arithmetic: 2.88 us -> none
    ppermute x15, waiting for transfers between devices: 41.4 us -> 39.2 us  [along(): return lax.ppermute(value, BOTH, pairs)]
  transfers between devices with their start and end apart: 24 -> 24, of which waited for: 13 -> 14; matrix products, arithmetic and copies ran while one was open for 7% -> 9% of each run, Pallas kernels for 18% -> 18%
where the time goes in v4:
time: 164 us; the launch traced here: 163 us
  Pallas kernels  55 us (34%)
  waiting for transfers between devices  47.9 us (29%)
  starting transfers between devices  40.7 us (25%)
  other arithmetic  9.91 us (6%)
  local copies, waits for them, and re-layouts  8.21 us (5%)
    ppermute x15, waiting for transfers between devices, along(): return lax.ppermute(value, BOTH, pairs)  39.2 us
    pallas_call x2, Pallas kernels, gradient_call(): pl.pallas_call(gradient_kernel, grid_spec=pltpu.PrefetchScalarGridSpec(nu...  20 us
    ppermute x15, starting transfers between devices, along(): return lax.ppermute(value, BOTH, pairs)  18.5 us
    pallas_call x1, Pallas kernels, second_call(): pl.pallas_call(second_kernel, grid_spec=pltpu.PrefetchScalarGridSpec(num_...  14.4 us
    pallas_call x1, Pallas kernels, first_call(): pl.pallas_call(first_kernel, grid_spec=pltpu.PrefetchScalarGridSpec(num_s...  12 us
    ppermute x4, starting transfers between devices, to_partner(): return lax.ppermute(value, 'dp', [(i, i ^ 1) for i in range(8)])  8.01 us
    pallas_call x1, Pallas kernels, scale_call(): pl.pallas_call(scale_kernel, grid=(SEQS,), in_specs=[pl.BlockSpec((1, ROW...  7.35 us
    ppermute x3, waiting for transfers between devices, along_x(): return lax.ppermute(value, 'dp', [(i, i ^ 2 * flip) for i in range(8)])  6.89 us
  transfers between devices with their start and end apart: 24, of which 14 were waited for; matrix products, arithmetic and copies ran while one was open for 9% of the time, Pallas kernels for 18%

profile of v4, /device:TPU:1, one launch (start us, length us, event | category | flops | bytes accessed | tf_op | source)
XLA Modules:
  0.0 162.6 jit_solution(14995267987566573272)
XLA Ops:
  0.6 1.2 group_sums.1
  1.8 4.6 %collective-permute-start.3 = (f32[1,128]{1,0:T(1,128)}, f32[1,128]{1,0:T(1,128)S(1)}, u32[]{:S(2)}, u32[]{:S(2)}) collective-permute-start(f32[1,128]{1,0:T(1,128)} %group_sums.1), channel_id=1, source_target_pairs={{0,12},{1,13},{2,14},{3,15},{4,8},{5,9},{6,10},{7,11},{8,4},{9,5},... | collective-permute-start | bytes 1544 | tf_op jit(solution)/shard_map/ppermute | solution.py:35
  6.4 0.6 collective-permute-start.1
  7.0 1.2 fusion.19
  8.2 0.8 dynamic_slice.3
  9.1 1.3 collective-permute-done.2
  10.5 2.8 %collective-permute-start.6 = (bf16[336,512]{1,0:T(8,128)(2,1)S(1)}, bf16[336,512]{1,0:T(8,128)(2,1)S(1)}, u32[]{:S(2)}, u32[]{:S(2)}) collective-permute-start(bf16[336,512]{1,0:T(8,128)(2,1)S(1)} %fusion.7), channel_id=1, source_target_pairs={{0,3},{1,2},{2,1},{3,0},{4,7},{5,6},{6,5},{7,4},{8,11},{9,10},{10,... | collective-permute-start | bytes 1032200 | tf_op jit(solution)/shard_map/ppermute | solution.py:35
  14.0 8.0 %collective-permute-done.6 = bf16[336,512]{1,0:T(8,128)(2,1)S(1)} collective-permute-done((bf16[336,512]{1,0:T(8,128)(2,1)S(1)}, bf16[336,512]{1,0:T(8,128)(2,1)S(1)}, u32[]{:S(2)}, u32[]{:S(2)}) %collective-permute-start.6) | collective-permute-done | bytes 344096 | tf_op jit(solution)/shard_map/ppermute | solution.py:35
  22.0 0.6 collective-permute-done.4
  22.8 3.0 %collective-permute-start.7 = (bf16[8,128,5120]{2,1,0:T(8,128)(2,1)}, bf16[8,128,5120]{2,1,0:T(8,128)(2,1)}, u32[]{:S(2)}, u32[]{:S(2)}) collective-permute-start(bf16[8,128,5120]{2,1,0:T(8,128)(2,1)} %own_ref.3), channel_id=1, source_target_pairs={{0,16},{16,0},{32,48},{48,32},{64,80},{80,64},{96,112},{112,96},{1... | collective-permute-start | bytes 31457288 | tf_op jit(solution)/shard_map/ppermute | solution.py:43
  26.5 1.6 %pad_maximum_fusion = bf16[8,2,144,512]{3,2,1,0:T(8,128)(2,1)} fusion(bf16[8,2,16,512]{3,2,1,0:T(8,128)(2,1)S(1)} %broadcast_in_dim.4, bf16[8,2,128,512]{3,2,1,0:T(8,128)(2,1)S(1)} %bitcast.37), kind=kLoop, calls=%fused_computation.3 | loop fusion | flops 4718592 | bytes 4718592 | tf_op jit(solution)/shard_map/concatenate | solution.py:343
  28.2 4.9 %all-to-all-start = ((bf16[8,2,144,512]{3,2,1,0:T(8,128)(2,1)}), bf16[8,2,144,512]{3,2,1,0:T(8,128)(2,1)}, u32[]{:S(2)}, u32[]{:S(2)}) async-start(bf16[8,2,144,512]{3,2,1,0:T(8,128)(2,1)} %pad_maximum_fusion), calls=%async_computation | async-start | bytes 4718592 | tf_op jit(solution)/shard_map/all_to_all | solution.py:344
  33.0 0.5 collective-permute-start.10
  33.5 2.5 %collective-permute-start.9 = (bf16[1280,512]{1,0:T(8,128)(2,1)S(1)}, bf16[1280,512]{1,0:T(8,128)(2,1)S(1)}, u32[]{:S(2)}, u32[]{:S(2)}) collective-permute-start(bf16[1280,512]{1,0:T(8,128)(2,1)S(1)} %pad_maximum_fusion.2.refs_8_), channel_id=1, source_target_pairs={{0,12},{1,13},{2,14},{3,15},{4,8},{5,9},{6,10},{7,11},{8,4},{9,5},... | collective-permute-start | bytes 3932168 | tf_op jit(solution)/shard_map/ppermute | solution.py:35
  36.0 1.2 collective-permute-start.8
  37.4 7.3 %token_scale.1.refs_12_ = f32[1024,128]{1,0:T(8,128)S(1)} custom-call(bf16[8,128,5120]{2,1,0:T(8,128)(2,1)} %own_ref.3), custom_call_target="tpu_custom_call" | custom-call | flops 1 | bytes 1 | tf_op jit(solution)/shard_map/token_scale/pallas_call | solution.py:70
  44.8 0.5 collective-permute-start.11
  45.4 4.6 %collective-permute-done.10.refs_9_ = bf16[1280,512]{1,0:T(8,128)(2,1)} collective-permute-done((bf16[1280,512]{1,0:T(8,128)(2,1)S(1)}, bf16[1280,512]{1,0:T(8,128)(2,1)}, u32[]{:S(2)}, u32[]{:S(2)}) %collective-permute-start.10) | collective-permute-done | bytes 1310752 | tf_op jit(solution)/shard_map/ppermute | solution.py:35
  49.9 12.0 %project_first.1.refs_10_ = f32[2,1024,512]{2,1,0:T(8,128)} custom-call(s32[3]{0:T(128)S(1)} %pad_add_fusion.1.place, bf16[8,128,5120]{2,1,0:T(8,128)(2,1)} %own_ref.3, bf16[8,128,5120]{2,1,0:T(8,128)(2,1)} %own_ref.3, bf16[8,128,5120]{2,1,0:T(8,128)(2,1)} %own_ref.3, bf16[8,128,5120]{2,1,0:T(8,128)(2,1)} %own_ref.3, ...), custom_call_target="tpu_custom_call" | custom-call | flops 1 | bytes 1 | tf_op jit(solution)/shard_map/project_first/pallas_call | solution.py:184
  62.0 2.6 %collective-permute-done.9.refs_9_ = bf16[1280,512]{1,0:T(8,128)(2,1)S(1)} collective-permute-done((bf16[1280,512]{1,0:T(8,128)(2,1)S(1)}, bf16[1280,512]{1,0:T(8,128)(2,1)S(1)}, u32[]{:S(2)}, u32[]{:S(2)}) %collective-permute-start.9) | collective-permute-done | bytes 1310752 | tf_op jit(solution)/shard_map/ppermute | solution.py:35
  64.6 1.7 %collective-permute-done.8.refs_8_ = bf16[1280,512]{1,0:T(8,128)(2,1)} collective-permute-done((bf16[1280,512]{1,0:T(8,128)(2,1)S(1)}, bf16[1280,512]{1,0:T(8,128)(2,1)}, u32[]{:S(2)}, u32[]{:S(2)}) %collective-permute-start.8) | collective-permute-done | bytes 1310752 | tf_op jit(solution)/shard_map/ppermute | solution.py:35
  66.3 14.4 %project_second.1 = (bf16[8,2,128,512]{3,2,1,0:T(8,128)(2,1)}, bf16[2,1024,512]{2,1,0:T(8,128)(2,1)}) custom-call(s32[3]{0:T(128)S(1)} %pad_add_fusion.1.place, s32[8,8]{1,0:T(8,128)S(1)} %concatenate.31.facts, bf16[8,128,5120]{2,1,0:T(8,128)(2,1)} %own_ref.3, bf16[8,128,5120]{2,1,0:T(8,128)(2,1)} %own_ref.3, bf16[8,128,5120]{2,1,0:T(8,128)(2,1)} %own_ref.3, ...), custom_call_target="tpu_custom_call" | custom-call | flops 1 | bytes 1 | tf_op jit(solution)/shard_map/project_second/pallas_call | solution.py:204
  80.8 1.6 copy-done
  82.4 10.0 %weight_gradient.3 = (bf16[4,320,512]{2,1,0:T(8,128)(2,1)}, bf16[4,320,512]{2,1,0:T(8,128)(2,1)S(1)}) custom-call(s32[3]{0:T(128)S(1)} %pad_add_fusion.1.place, bf16[8,128,5120]{2,1,0:T(8,128)(2,1)} %own_ref.3, bf16[8,128,5120]{2,1,0:T(8,128)(2,1)} %collective-permute-done.7.refs_4_.refs_5_.refs_6_.refs_7_.partner_ref, bf16[2,1024,512]{2,1,0:T(8,128)(2,1)S(1)} %copy-done), custom_call_target="tpu_custom_call" | custom-call | flops 1 | bytes 1 | tf_op jit(solution)/shard_map/weight_gradient/pallas_call | solution.py:261
  92.3 1.7 %collective-permute-start.12 = (bf16[4,320,512]{2,1,0:T(8,128)(2,1)}, bf16[4,320,512]{2,1,0:T(8,128)(2,1)}, u32[]{:S(2)}, u32[]{:S(2)}) collective-permute-start(bf16[4,320,512]{2,1,0:T(8,128)(2,1)} %get-tuple-element.29), channel_id=1, source_target_pairs={{0,8},{1,9},{2,10},{3,11},{4,12},{5,13},{6,14},{7,15},{8,0},{9,1},... | collective-permute-start | bytes 3932168 | tf_op jit(solution)/shard_map/ppermute | solution.py:35
  94.0 0.6 collective-permute-start.13
  94.6 10.0 %weight_gradient.2 = (bf16[4,320,512]{2,1,0:T(8,128)(2,1)S(1)}, bf16[4,320,512]{2,1,0:T(8,128)(2,1)}) custom-call(s32[3]{0:T(128)S(1)} %pad_add_fusion.1.place, bf16[8,128,5120]{2,1,0:T(8,128)(2,1)} %own_ref.3, bf16[8,128,5120]{2,1,0:T(8,128)(2,1)} %collective-permute-done.7.refs_4_.refs_5_.refs_6_.refs_7_.partner_ref, bf16[2,1024,512]{2,1,0:T(8,128)(2,1)S(1)} %copy-done), custom_call_target="tpu_custom_call" | custom-call | flops 1 | bytes 1 | tf_op jit(solution)/shard_map/weight_gradient/pallas_call | solution.py:261
  105.0 5.4 %all-to-all-start.1 = ((bf16[8,2,128,512]{3,2,1,0:T(8,128)(2,1)}), bf16[8,2,128,512]{3,2,1,0:T(8,128)(2,1)}, u32[]{:S(2)}, u32[]{:S(2)}) async-start(bf16[8,2,128,512]{3,2,1,0:T(8,128)(2,1)} %get-tuple-element.26), calls=%async_computation.1 | async-start | bytes 4194304 | tf_op jit(solution)/shard_map/all_to_all | solution.py:356
  110.4 0.6 collective-permute-done.12
  111.0 14.0 %collective-permute-done.13 = bf16[4,320,512]{2,1,0:T(8,128)(2,1)} collective-permute-done((bf16[4,320,512]{2,1,0:T(8,128)(2,1)S(1)}, bf16[4,320,512]{2,1,0:T(8,128)(2,1)}, u32[]{:S(2)}, u32[]{:S(2)}) %collective-permute-start.13) | collective-permute-done | bytes 1310752 | tf_op jit(solution)/shard_map/ppermute | solution.py:35
  125.0 1.4 fusion.8
  126.3 2.0 %collective-permute-start.15 = (bf16[320,512]{1,0:T(8,128)(2,1)S(1)}, bf16[320,512]{1,0:T(8,128)(2,1)S(1)}, u32[]{:S(2)}, u32[]{:S(2)}) collective-permute-start(bf16[320,512]{1,0:T(8,128)(2,1)S(1)} %fusion.8), channel_id=1, source_target_pairs={{0,2},{1,3},{2,0},{3,1},{4,6},{5,7},{6,4},{7,5},{8,10},{9,11},{10,... | collective-permute-start | bytes 983048 | tf_op jit(solution)/shard_map/ppermute | solution.py:35
  128.3 1.4 fusion.10
  129.7 0.6 collective-permute-start.17
  130.3 1.4 fusion.9
  131.7 0.5 collective-permute-start.16
  132.1 2.3 %collective-permute-done.15 = bf16[320,512]{1,0:T(8,128)(2,1)S(1)} collective-permute-done((bf16[320,512]{1,0:T(8,128)(2,1)S(1)}, bf16[320,512]{1,0:T(8,128)(2,1)S(1)}, u32[]{:S(2)}, u32[]{:S(2)}) %collective-permute-start.15) | collective-permute-done | bytes 327712 | tf_op jit(solution)/shard_map/ppermute | solution.py:35
  134.4 3.4 %collective-permute-done.17 = bf16[320,512]{1,0:T(8,128)(2,1)S(1)} collective-permute-done((bf16[320,512]{1,0:T(8,128)(2,1)S(1)}, bf16[320,512]{1,0:T(8,128)(2,1)S(1)}, u32[]{:S(2)}, u32[]{:S(2)}) %collective-permute-start.17) | collective-permute-done | bytes 327712 | tf_op jit(solution)/shard_map/ppermute | solution.py:35
  138.0 1.5 fusion.5
  139.5 2.7 %collective-permute-start.20 = (bf16[320,512]{1,0:T(8,128)(2,1)S(1)}, bf16[320,512]{1,0:T(8,128)(2,1)S(1)}, u32[]{:S(2)}, u32[]{:S(2)}) collective-permute-start(bf16[320,512]{1,0:T(8,128)(2,1)S(1)} %fusion.5), channel_id=1, source_target_pairs={{0,96},{16,112},{32,64},{48,80},{64,32},{80,48},{96,0},{112,16},{1... | collective-permute-start | bytes 983048 | tf_op jit(solution)/shard_map/ppermute | solution.py:39
  142.2 1.3 collective-permute-start.18
  143.5 1.3 copy_bitcast_fusion
  144.8 1.3 slice_bitcast_fusion.1
  146.5 1.5 copy.13
  148.4 6.5 %collective-permute-done.18 = bf16[320,512]{1,0:T(8,128)(2,1)S(1)} collective-permute-done((bf16[320,512]{1,0:T(8,128)(2,1)S(1)}, bf16[320,512]{1,0:T(8,128)(2,1)S(1)}, u32[]{:S(2)}, u32[]{:S(2)}) %collective-permute-start.18) | collective-permute-done | bytes 327712 | tf_op jit(solution)/shard_map/ppermute | solution.py:39
  155.1 4.3 %collective-permute-start.21 = (f32[320,512]{1,0:T(8,128)S(1)}, f32[320,512]{1,0:T(8,128)S(1)}, u32[]{:S(2)}, u32[]{:S(2)}) collective-permute-start(f32[320,512]{1,0:T(8,128)S(1)} %add_multiply_fusion), channel_id=1, source_target_pairs={{0,16},{16,0},{32,48},{48,32},{64,80},{80,64},{96,112},{112,96},{1... | collective-permute-start | bytes 1966088 | tf_op jit(solution)/shard_map/ppermute | solution.py:43
  159.4 1.7 %collective-permute-done.21 = f32[320,512]{1,0:T(8,128)S(1)} collective-permute-done((f32[320,512]{1,0:T(8,128)S(1)}, f32[320,512]{1,0:T(8,128)S(1)}, u32[]{:S(2)}, u32[]{:S(2)}) %collective-permute-start.21) | collective-permute-done | bytes 655392 | tf_op jit(solution)/shard_map/ppermute | solution.py:43
  161.4 1.2 pad_maximum_fusion.3
  (56 shorter events, 3.8 us)
Async XLA Ops:
  1.8 8.6 %copy-start.7 = (f32[1,128]{1,0:T(1,128)S(1)}, f32[1,128]{1,0:T(1,128)}, u32[]{:S(2)}) copy-start(f32[1,128]{1,0:T(1,128)} %group_sums.1) | copy-start | bytes 1540
  1.8 7.3 %collective-permute-start.3 = (f32[1,128]{1,0:T(1,128)}, f32[1,128]{1,0:T(1,128)S(1)}, u32[]{:S(2)}, u32[]{:S(2)}) collective-permute-start(f32[1,128]{1,0:T(1,128)} %group_sums.1), channel_id=1, source_target_pairs={{0,12},{1,13},{2,14},{3,15},{4,8},{5,9},{6,10},{7,11},{8,4},{9,5},... | collective-permute-start | bytes 1544 | tf_op jit(solution)/shard_map/ppermute | solution.py:35
  6.4 4.0 %collective-permute-start.2 = (f32[1,128]{1,0:T(1,128)}, f32[1,128]{1,0:T(1,128)S(1)}, u32[]{:S(2)}, u32[]{:S(2)}) collective-permute-start(f32[1,128]{1,0:T(1,128)} %group_sums.1), channel_id=1, source_target_pairs={{0,8},{1,9},{2,10},{3,11},{4,12},{5,13},{6,14},{7,15},{8,0},{9,1},... | collective-permute-start | bytes 1544 | tf_op jit(solution)/shard_map/ppermute | solution.py:35
  6.4 4.0 %collective-permute-start.1 = (f32[1,128]{1,0:T(1,128)}, f32[1,128]{1,0:T(1,128)S(1)}, u32[]{:S(2)}, u32[]{:S(2)}) collective-permute-start(f32[1,128]{1,0:T(1,128)} %group_sums.1), channel_id=1, source_target_pairs={{0,4},{1,5},{2,6},{3,7},{4,0},{5,1},{6,2},{7,3},{8,12},{9,13},{10,... | collective-permute-start | bytes 1544 | tf_op jit(solution)/shard_map/ppermute | solution.py:35
  10.5 11.4 %collective-permute-start.6 = (bf16[336,512]{1,0:T(8,128)(2,1)S(1)}, bf16[336,512]{1,0:T(8,128)(2,1)S(1)}, u32[]{:S(2)}, u32[]{:S(2)}) collective-permute-start(bf16[336,512]{1,0:T(8,128)(2,1)S(1)} %fusion.7), channel_id=1, source_target_pairs={{0,3},{1,2},{2,1},{3,0},{4,7},{5,6},{6,5},{7,4},{8,11},{9,10},{10,... | collective-permute-start | bytes 1032200 | tf_op jit(solution)/shard_map/ppermute | solution.py:35
  13.3 8.7 %collective-permute-start.5 = (bf16[336,512]{1,0:T(8,128)(2,1)S(1)}, bf16[336,512]{1,0:T(8,128)(2,1)S(1)}, u32[]{:S(2)}, u32[]{:S(2)}) collective-permute-start(bf16[336,512]{1,0:T(8,128)(2,1)S(1)} %fusion.7), channel_id=1, source_target_pairs={{0,2},{1,3},{2,0},{3,1},{4,6},{5,7},{6,4},{7,5},{8,10},{9,11},{10,... | collective-permute-start | bytes 1032200 | tf_op jit(solution)/shard_map/ppermute | solution.py:35
  13.7 9.0 %collective-permute-start.4 = (bf16[336,512]{1,0:T(8,128)(2,1)S(1)}, bf16[336,512]{1,0:T(8,128)(2,1)S(1)}, u32[]{:S(2)}, u32[]{:S(2)}) collective-permute-start(bf16[336,512]{1,0:T(8,128)(2,1)S(1)} %fusion.7), channel_id=1, source_target_pairs={{0,1},{1,0},{2,3},{3,2},{4,5},{5,4},{6,7},{7,6},{8,9},{9,8},{10,11... | collective-permute-start | bytes 1032200 | tf_op jit(solution)/shard_map/ppermute | solution.py:35
  22.0 3.8 %copy-start.2 = (bf16[8,128,1024]{2,1,0:T(8,128)(2,1)S(1)}, bf16[8,128,1024]{2,1,0:T(8,128)(2,1)}, u32[]{:S(2)}) copy-start(bf16[8,128,1024]{2,1,0:T(8,128)(2,1)} %param.17) | copy-start | bytes 6291460
  22.8 27.1 %collective-permute-start.7 = (bf16[8,128,5120]{2,1,0:T(8,128)(2,1)}, bf16[8,128,5120]{2,1,0:T(8,128)(2,1)}, u32[]{:S(2)}, u32[]{:S(2)}) collective-permute-start(bf16[8,128,5120]{2,1,0:T(8,128)(2,1)} %own_ref.3), channel_id=1, source_target_pairs={{0,16},{16,0},{32,48},{48,32},{64,80},{80,64},{96,112},{112,96},{1... | collective-permute-start | bytes 31457288 | tf_op jit(solution)/shard_map/ppermute | solution.py:43
  28.2 9.0 %copy-start.3 = (s32[1,8]{1,0:T(1,128)S(1)}, s32[1,8]{1,0:T(1,128)}, u32[]{:S(2)}) copy-start(s32[1,8]{1,0:T(1,128)} %param.13) | copy-start | bytes 100
  28.2 9.0 %copy-start.4 = (s32[8]{0:T(128)S(1)}, s32[8]{0:T(128)}, u32[]{:S(2)}) copy-start(s32[8]{0:T(128)} %param.14) | copy-start | bytes 100
  28.2 9.0 %copy-start.5 = (s32[8]{0:T(128)S(1)}, s32[8]{0:T(128)}, u32[]{:S(2)}) copy-start(s32[8]{0:T(128)} %rewards_ref.1) | copy-start | bytes 100
  28.2 9.0 %copy-start.6 = (s32[8]{0:T(128)S(1)}, s32[8]{0:T(128)}, u32[]{:S(2)}) copy-start(s32[8]{0:T(128)} %groups_ref.1) | copy-start | bytes 100
  28.2 38.1 %all-to-all-start = ((bf16[8,2,144,512]{3,2,1,0:T(8,128)(2,1)}), bf16[8,2,144,512]{3,2,1,0:T(8,128)(2,1)}, u32[]{:S(2)}, u32[]{:S(2)}) async-start(bf16[8,2,144,512]{3,2,1,0:T(8,128)(2,1)} %pad_maximum_fusion), calls=%async_computation | async-start | bytes 4718592 | tf_op jit(solution)/shard_map/all_to_all | solution.py:344
  33.0 16.9 %collective-permute-start.10 = (bf16[1280,512]{1,0:T(8,128)(2,1)S(1)}, bf16[1280,512]{1,0:T(8,128)(2,1)}, u32[]{:S(2)}, u32[]{:S(2)}) collective-permute-start(bf16[1280,512]{1,0:T(8,128)(2,1)S(1)} %pad_maximum_fusion.2.refs_8_), channel_id=1, source_target_pairs={{0,4},{1,5},{2,6},{3,7},{4,0},{5,1},{6,2},{7,3},{8,12},{9,13},{10,... | collective-permute-start | bytes 3932168 | tf_op jit(solution)/shard_map/ppermute | solution.py:35
  33.5 31.1 %collective-permute-start.9 = (bf16[1280,512]{1,0:T(8,128)(2,1)S(1)}, bf16[1280,512]{1,0:T(8,128)(2,1)S(1)}, u32[]{:S(2)}, u32[]{:S(2)}) collective-permute-start(bf16[1280,512]{1,0:T(8,128)(2,1)S(1)} %pad_maximum_fusion.2.refs_8_), channel_id=1, source_target_pairs={{0,12},{1,13},{2,14},{3,15},{4,8},{5,9},{6,10},{7,11},{8,4},{9,5},... | collective-permute-start | bytes 3932168 | tf_op jit(solution)/shard_map/ppermute | solution.py:35
  36.0 30.3 %collective-permute-start.8 = (bf16[1280,512]{1,0:T(8,128)(2,1)S(1)}, bf16[1280,512]{1,0:T(8,128)(2,1)}, u32[]{:S(2)}, u32[]{:S(2)}) collective-permute-start(bf16[1280,512]{1,0:T(8,128)(2,1)S(1)} %pad_maximum_fusion.2.refs_8_), channel_id=1, source_target_pairs={{0,8},{1,9},{2,10},{3,11},{4,12},{5,13},{6,14},{7,15},{8,0},{9,1},... | collective-permute-start | bytes 3932168 | tf_op jit(solution)/shard_map/ppermute | solution.py:35
  37.2 7.6 %collective-permute-start = (s32[4,8]{1,0:T(4,128)S(1)}, s32[4,8]{1,0:T(4,128)S(1)}, u32[]{:S(2)}, u32[]{:S(2)}) collective-permute-start(s32[4,8]{1,0:T(4,128)S(1)} %pad_add_fusion), channel_id=1, source_target_pairs={{0,16},{16,0},{32,48},{48,32},{64,80},{80,64},{96,112},{112,96},{1... | collective-permute-start | bytes 392 | tf_op jit(solution)/shard_map/ppermute | solution.py:43
  44.8 17.2 %collective-permute-start.11 = (f32[1024,128]{1,0:T(8,128)S(1)}, f32[1024,128]{1,0:T(8,128)}, u32[]{:S(2)}, u32[]{:S(2)}) collective-permute-start(f32[1024,128]{1,0:T(8,128)S(1)} %token_scale.1.refs_12_), channel_id=1, source_target_pairs={{0,16},{16,0},{32,48},{48,32},{64,80},{80,64},{96,112},{112,96},{1... | collective-permute-start | bytes 1572872 | tf_op jit(solution)/shard_map/ppermute | solution.py:43
  45.3 21.0 %copy-start.1 = (f32[128]{0:T(128)S(1)}, f32[128]{0:T(128)}, u32[]{:S(2)}) copy-start(f32[128]{0:T(128)} %param.12) | copy-start | bytes 1540
  80.8 1.6 copy-start
  92.3 18.6 %collective-permute-start.12 = (bf16[4,320,512]{2,1,0:T(8,128)(2,1)}, bf16[4,320,512]{2,1,0:T(8,128)(2,1)}, u32[]{:S(2)}, u32[]{:S(2)}) collective-permute-start(bf16[4,320,512]{2,1,0:T(8,128)(2,1)} %get-tuple-element.29), channel_id=1, source_target_pairs={{0,8},{1,9},{2,10},{3,11},{4,12},{5,13},{6,14},{7,15},{8,0},{9,1},... | collective-permute-start | bytes 3932168 | tf_op jit(solution)/shard_map/ppermute | solution.py:35
  94.0 30.9 %collective-permute-start.13 = (bf16[4,320,512]{2,1,0:T(8,128)(2,1)S(1)}, bf16[4,320,512]{2,1,0:T(8,128)(2,1)}, u32[]{:S(2)}, u32[]{:S(2)}) collective-permute-start(bf16[4,320,512]{2,1,0:T(8,128)(2,1)S(1)} %get-tuple-element.30), channel_id=1, source_target_pairs={{0,12},{1,13},{2,14},{3,15},{4,8},{5,9},{6,10},{7,11},{8,4},{9,5},... | collective-permute-start | bytes 3932168 | tf_op jit(solution)/shard_map/ppermute | solution.py:35
  104.6 20.3 %collective-permute-start.14 = (bf16[4,320,512]{2,1,0:T(8,128)(2,1)}, bf16[4,320,512]{2,1,0:T(8,128)(2,1)}, u32[]{:S(2)}, u32[]{:S(2)}) collective-permute-start(bf16[4,320,512]{2,1,0:T(8,128)(2,1)} %get-tuple-element.31), channel_id=1, source_target_pairs={{0,4},{1,5},{2,6},{3,7},{4,0},{5,1},{6,2},{7,3},{8,12},{9,13},{10,... | collective-permute-start | bytes 3932168 | tf_op jit(solution)/shard_map/ppermute | solution.py:35
  105.0 34.5 %all-to-all-start.1 = ((bf16[8,2,128,512]{3,2,1,0:T(8,128)(2,1)}), bf16[8,2,128,512]{3,2,1,0:T(8,128)(2,1)}, u32[]{:S(2)}, u32[]{:S(2)}) async-start(bf16[8,2,128,512]{3,2,1,0:T(8,128)(2,1)} %get-tuple-element.26), calls=%async_computation.1 | async-start | bytes 4194304 | tf_op jit(solution)/shard_map/all_to_all | solution.py:356
  126.3 8.1 %collective-permute-start.15 = (bf16[320,512]{1,0:T(8,128)(2,1)S(1)}, bf16[320,512]{1,0:T(8,128)(2,1)S(1)}, u32[]{:S(2)}, u32[]{:S(2)}) collective-permute-start(bf16[320,512]{1,0:T(8,128)(2,1)S(1)} %fusion.8), channel_id=1, source_target_pairs={{0,2},{1,3},{2,0},{3,1},{4,6},{5,7},{6,4},{7,5},{8,10},{9,11},{10,... | collective-permute-start | bytes 983048 | tf_op jit(solution)/shard_map/ppermute | solution.py:35
  129.7 8.1 %collective-permute-start.17 = (bf16[320,512]{1,0:T(8,128)(2,1)S(1)}, bf16[320,512]{1,0:T(8,128)(2,1)S(1)}, u32[]{:S(2)}, u32[]{:S(2)}) collective-permute-start(bf16[320,512]{1,0:T(8,128)(2,1)S(1)} %fusion.10), channel_id=1, source_target_pairs={{0,3},{1,2},{2,1},{3,0},{4,7},{5,6},{6,5},{7,4},{8,11},{9,10},{10,... | collective-permute-start | bytes 983048 | tf_op jit(solution)/shard_map/ppermute | solution.py:35
  131.7 6.3 %collective-permute-start.16 = (bf16[320,512]{1,0:T(8,128)(2,1)S(1)}, bf16[320,512]{1,0:T(8,128)(2,1)S(1)}, u32[]{:S(2)}, u32[]{:S(2)}) collective-permute-start(bf16[320,512]{1,0:T(8,128)(2,1)S(1)} %fusion.9), channel_id=1, source_target_pairs={{0,1},{1,0},{2,3},{3,2},{4,5},{5,4},{6,7},{7,6},{8,9},{9,8},{10,11... | collective-permute-start | bytes 983048 | tf_op jit(solution)/shard_map/ppermute | solution.py:35
  139.5 8.5 %collective-permute-start.20 = (bf16[320,512]{1,0:T(8,128)(2,1)S(1)}, bf16[320,512]{1,0:T(8,128)(2,1)S(1)}, u32[]{:S(2)}, u32[]{:S(2)}) collective-permute-start(bf16[320,512]{1,0:T(8,128)(2,1)S(1)} %fusion.5), channel_id=1, source_target_pairs={{0,96},{16,112},{32,64},{48,80},{64,32},{80,48},{96,0},{112,16},{1... | collective-permute-start | bytes 983048 | tf_op jit(solution)/shard_map/ppermute | solution.py:39
  142.2 6.2 %collective-permute-start.19 = (bf16[320,512]{1,0:T(8,128)(2,1)S(1)}, bf16[320,512]{1,0:T(8,128)(2,1)S(1)}, u32[]{:S(2)}, u32[]{:S(2)}) collective-permute-start(bf16[320,512]{1,0:T(8,128)(2,1)S(1)} %fusion.5), channel_id=1, source_target_pairs={{0,32},{16,48},{32,0},{48,16},{64,96},{80,112},{96,64},{112,80},{1... | collective-permute-start | bytes 983048 | tf_op jit(solution)/shard_map/ppermute | solution.py:39
  142.2 12.7 %collective-permute-start.18 = (bf16[320,512]{1,0:T(8,128)(2,1)S(1)}, bf16[320,512]{1,0:T(8,128)(2,1)S(1)}, u32[]{:S(2)}, u32[]{:S(2)}) collective-permute-start(bf16[320,512]{1,0:T(8,128)(2,1)S(1)} %fusion.5), channel_id=1, source_target_pairs={{0,64},{16,80},{32,96},{48,112},{64,0},{80,16},{96,32},{112,48},{1... | collective-permute-start | bytes 983048 | tf_op jit(solution)/shard_map/ppermute | solution.py:39
  155.1 6.0 %collective-permute-start.21 = (f32[320,512]{1,0:T(8,128)S(1)}, f32[320,512]{1,0:T(8,128)S(1)}, u32[]{:S(2)}, u32[]{:S(2)}) collective-permute-start(f32[320,512]{1,0:T(8,128)S(1)} %add_multiply_fusion), channel_id=1, source_target_pairs={{0,16},{16,0},{32,48},{48,32},{64,80},{80,64},{96,112},{112,96},{1... | collective-permute-start | bytes 1966088 | tf_op jit(solution)/shard_map/ppermute | solution.py:43

commit v5 on v4

--- a/solution.py
+++ b/solution.py
@@ -43,8 +43,8 @@
     return lax.ppermute(value, "dp", [(i, i ^ 1) for i in range(8)])
 
 
-def params():
-    return pltpu.CompilerParams(vmem_limit_bytes=48 * MIB)
+def params(mib=48):
+    return pltpu.CompilerParams(vmem_limit_bytes=mib * MIB)
 
 
 def window(pair_of, j, place):
@@ -217,7 +217,7 @@
             jax.ShapeDtypeStruct((SEQS, 2, ROWS, COLS), bf16),
             jax.ShapeDtypeStruct((2, TOKENS, COLS), bf16),
         ],
-        compiler_params=params(),
+        compiler_params=params(45),
         cost_estimate=COST,
         name="project_second",
     )(

time: 164 us -> 162 us (0.988)
  no operation moved by 1% of the time
where the time goes in v5:
time: 162 us; the launch traced here: 161 us
  Pallas kernels  54.8 us (34%)
  waiting for transfers between devices  47.9 us (30%)
  starting transfers between devices  40.7 us (25%)
  other arithmetic  9.9 us (6%)
  local copies, waits for them, and re-layouts  6.63 us (4%)
    ppermute x15, waiting for transfers between devices, along(): return lax.ppermute(value, BOTH, pairs)  39.3 us
    pallas_call x2, Pallas kernels, gradient_call(): pl.pallas_call(gradient_kernel, grid_spec=pltpu.PrefetchScalarGridSpec(nu...  20 us
    ppermute x15, starting transfers between devices, along(): return lax.ppermute(value, BOTH, pairs)  18.5 us
    pallas_call x1, Pallas kernels, second_call(): pl.pallas_call(second_kernel, grid_spec=pltpu.PrefetchScalarGridSpec(num_...  14.2 us
    pallas_call x1, Pallas kernels, first_call(): pl.pallas_call(first_kernel, grid_spec=pltpu.PrefetchScalarGridSpec(num_s...  12 us
    ppermute x4, starting transfers between devices, to_partner(): return lax.ppermute(value, 'dp', [(i, i ^ 1) for i in range(8)])  8.02 us
    pallas_call x1, Pallas kernels, scale_call(): pl.pallas_call(scale_kernel, grid=(SEQS,), in_specs=[pl.BlockSpec((1, ROW...  7.35 us
    ppermute x3, waiting for transfers between devices, along_x(): return lax.ppermute(value, 'dp', [(i, i ^ 2 * flip) for i in range(8)])  6.89 us
  transfers between devices with their start and end apart: 24, of which 14 were waited for; matrix products, arithmetic and copies ran while one was open for 9% of the time, Pallas kernels for 18%

profile of v5, /device:TPU:1, one launch (start us, length us, event | category | flops | bytes accessed | tf_op | source)
XLA Modules:
  0.0 160.8 jit_solution(5193000785931882775)
XLA Ops:
  0.6 1.2 group_sums.1
  1.8 4.6 %collective-permute-start.3 = (f32[1,128]{1,0:T(1,128)}, f32[1,128]{1,0:T(1,128)S(1)}, u32[]{:S(2)}, u32[]{:S(2)}) collective-permute-start(f32[1,128]{1,0:T(1,128)} %group_sums.1), channel_id=1, source_target_pairs={{0,12},{1,13},{2,14},{3,15},{4,8},{5,9},{6,10},{7,11},{8,4},{9,5},... | collective-permute-start | bytes 1544 | tf_op jit(solution)/shard_map/ppermute | solution.py:35
  6.4 0.6 collective-permute-start.1
  7.0 1.2 fusion.19
  8.2 0.8 dynamic_slice.3
  9.1 1.3 collective-permute-done.2
  10.5 2.8 %collective-permute-start.6 = (bf16[336,512]{1,0:T(8,128)(2,1)S(1)}, bf16[336,512]{1,0:T(8,128)(2,1)S(1)}, u32[]{:S(2)}, u32[]{:S(2)}) collective-permute-start(bf16[336,512]{1,0:T(8,128)(2,1)S(1)} %fusion.7), channel_id=1, source_target_pairs={{0,3},{1,2},{2,1},{3,0},{4,7},{5,6},{6,5},{7,4},{8,11},{9,10},{10,... | collective-permute-start | bytes 1032200 | tf_op jit(solution)/shard_map/ppermute | solution.py:35
  14.0 8.0 %collective-permute-done.6 = bf16[336,512]{1,0:T(8,128)(2,1)S(1)} collective-permute-done((bf16[336,512]{1,0:T(8,128)(2,1)S(1)}, bf16[336,512]{1,0:T(8,128)(2,1)S(1)}, u32[]{:S(2)}, u32[]{:S(2)}) %collective-permute-start.6) | collective-permute-done | bytes 344096 | tf_op jit(solution)/shard_map/ppermute | solution.py:35
  22.0 0.6 collective-permute-done.4
  22.8 3.0 %collective-permute-start.7 = (bf16[8,128,5120]{2,1,0:T(8,128)(2,1)}, bf16[8,128,5120]{2,1,0:T(8,128)(2,1)}, u32[]{:S(2)}, u32[]{:S(2)}) collective-permute-start(bf16[8,128,5120]{2,1,0:T(8,128)(2,1)} %own_ref.3), channel_id=1, source_target_pairs={{0,16},{16,0},{32,48},{48,32},{64,80},{80,64},{96,112},{112,96},{1... | collective-permute-start | bytes 31457288 | tf_op jit(solution)/shard_map/ppermute | solution.py:43
  26.5 1.6 %pad_maximum_fusion = bf16[8,2,144,512]{3,2,1,0:T(8,128)(2,1)} fusion(bf16[8,2,16,512]{3,2,1,0:T(8,128)(2,1)S(1)} %broadcast_in_dim.4, bf16[8,2,128,512]{3,2,1,0:T(8,128)(2,1)S(1)} %bitcast.37), kind=kLoop, calls=%fused_computation.3 | loop fusion | flops 4718592 | bytes 4718592 | tf_op jit(solution)/shard_map/concatenate | solution.py:343
  28.2 4.9 %all-to-all-start = ((bf16[8,2,144,512]{3,2,1,0:T(8,128)(2,1)}), bf16[8,2,144,512]{3,2,1,0:T(8,128)(2,1)}, u32[]{:S(2)}, u32[]{:S(2)}) async-start(bf16[8,2,144,512]{3,2,1,0:T(8,128)(2,1)} %pad_maximum_fusion), calls=%async_computation | async-start | bytes 4718592 | tf_op jit(solution)/shard_map/all_to_all | solution.py:344
  33.0 0.5 collective-permute-start.10
  33.5 2.5 %collective-permute-start.9 = (bf16[1280,512]{1,0:T(8,128)(2,1)S(1)}, bf16[1280,512]{1,0:T(8,128)(2,1)S(1)}, u32[]{:S(2)}, u32[]{:S(2)}) collective-permute-start(bf16[1280,512]{1,0:T(8,128)(2,1)S(1)} %pad_maximum_fusion.2.refs_8_), channel_id=1, source_target_pairs={{0,12},{1,13},{2,14},{3,15},{4,8},{5,9},{6,10},{7,11},{8,4},{9,5},... | collective-permute-start | bytes 3932168 | tf_op jit(solution)/shard_map/ppermute | solution.py:35
  36.0 1.2 collective-permute-start.8
  37.4 7.3 %token_scale.1.refs_12_ = f32[1024,128]{1,0:T(8,128)S(1)} custom-call(bf16[8,128,5120]{2,1,0:T(8,128)(2,1)} %own_ref.3), custom_call_target="tpu_custom_call" | custom-call | flops 1 | bytes 1 | tf_op jit(solution)/shard_map/token_scale/pallas_call | solution.py:70
  44.8 0.5 collective-permute-start.11
  45.3 4.6 %collective-permute-done.10.refs_9_ = bf16[1280,512]{1,0:T(8,128)(2,1)} collective-permute-done((bf16[1280,512]{1,0:T(8,128)(2,1)S(1)}, bf16[1280,512]{1,0:T(8,128)(2,1)}, u32[]{:S(2)}, u32[]{:S(2)}) %collective-permute-start.10) | collective-permute-done | bytes 1310752 | tf_op jit(solution)/shard_map/ppermute | solution.py:35
  49.9 12.0 %project_first.1.refs_10_ = f32[2,1024,512]{2,1,0:T(8,128)} custom-call(s32[3]{0:T(128)S(1)} %pad_add_fusion.1.place, bf16[8,128,5120]{2,1,0:T(8,128)(2,1)} %own_ref.3, bf16[8,128,5120]{2,1,0:T(8,128)(2,1)} %own_ref.3, bf16[8,128,5120]{2,1,0:T(8,128)(2,1)} %own_ref.3, bf16[8,128,5120]{2,1,0:T(8,128)(2,1)} %own_ref.3, ...), custom_call_target="tpu_custom_call" | custom-call | flops 1 | bytes 1 | tf_op jit(solution)/shard_map/project_first/pallas_call | solution.py:184
  61.9 2.6 %collective-permute-done.9.refs_9_ = bf16[1280,512]{1,0:T(8,128)(2,1)S(1)} collective-permute-done((bf16[1280,512]{1,0:T(8,128)(2,1)S(1)}, bf16[1280,512]{1,0:T(8,128)(2,1)S(1)}, u32[]{:S(2)}, u32[]{:S(2)}) %collective-permute-start.9) | collective-permute-done | bytes 1310752 | tf_op jit(solution)/shard_map/ppermute | solution.py:35
  64.6 1.7 %collective-permute-done.8.refs_8_ = bf16[1280,512]{1,0:T(8,128)(2,1)} collective-permute-done((bf16[1280,512]{1,0:T(8,128)(2,1)S(1)}, bf16[1280,512]{1,0:T(8,128)(2,1)}, u32[]{:S(2)}, u32[]{:S(2)}) %collective-permute-start.8) | collective-permute-done | bytes 1310752 | tf_op jit(solution)/shard_map/ppermute | solution.py:35
  66.3 14.2 %project_second.1 = (bf16[8,2,128,512]{3,2,1,0:T(8,128)(2,1)}, bf16[2,1024,512]{2,1,0:T(8,128)(2,1)S(1)}) custom-call(s32[3]{0:T(128)S(1)} %pad_add_fusion.1.place, s32[8,8]{1,0:T(8,128)S(1)} %concatenate.31.facts, bf16[8,128,5120]{2,1,0:T(8,128)(2,1)} %own_ref.3, bf16[8,128,5120]{2,1,0:T(8,128)(2,1)} %own_ref.3, bf16[8,128,5120]{2,1,0:T(8,128)(2,1)} %own_ref.3, ...), custom_call_target="tpu_custom_call" | custom-call | flops 1 | bytes 1 | tf_op jit(solution)/shard_map/project_second/pallas_call | solution.py:204
  80.6 10.0 %weight_gradient.3 = (bf16[4,320,512]{2,1,0:T(8,128)(2,1)}, bf16[4,320,512]{2,1,0:T(8,128)(2,1)S(1)}) custom-call(s32[3]{0:T(128)S(1)} %pad_add_fusion.1.place, bf16[8,128,5120]{2,1,0:T(8,128)(2,1)} %own_ref.3, bf16[8,128,5120]{2,1,0:T(8,128)(2,1)} %collective-permute-done.7.refs_4_.refs_5_.refs_6_.refs_7_.partner_ref, ...), custom_call_target="tpu_custom_call" | custom-call | flops 1 | bytes 1 | tf_op jit(solution)/shard_map/weight_gradient/pallas_call | solution.py:261
  90.6 1.7 %collective-permute-start.12 = (bf16[4,320,512]{2,1,0:T(8,128)(2,1)}, bf16[4,320,512]{2,1,0:T(8,128)(2,1)}, u32[]{:S(2)}, u32[]{:S(2)}) collective-permute-start(bf16[4,320,512]{2,1,0:T(8,128)(2,1)} %get-tuple-element.29), channel_id=1, source_target_pairs={{0,8},{1,9},{2,10},{3,11},{4,12},{5,13},{6,14},{7,15},{8,0},{9,1},... | collective-permute-start | bytes 3932168 | tf_op jit(solution)/shard_map/ppermute | solution.py:35
  92.2 0.6 collective-permute-start.13
  92.9 10.0 %weight_gradient.2 = (bf16[4,320,512]{2,1,0:T(8,128)(2,1)S(1)}, bf16[4,320,512]{2,1,0:T(8,128)(2,1)}) custom-call(s32[3]{0:T(128)S(1)} %pad_add_fusion.1.place, bf16[8,128,5120]{2,1,0:T(8,128)(2,1)} %own_ref.3, bf16[8,128,5120]{2,1,0:T(8,128)(2,1)} %collective-permute-done.7.refs_4_.refs_5_.refs_6_.refs_7_.partner_ref, ...), custom_call_target="tpu_custom_call" | custom-call | flops 1 | bytes 1 | tf_op jit(solution)/shard_map/weight_gradient/pallas_call | solution.py:261
  103.2 5.4 %all-to-all-start.1 = ((bf16[8,2,128,512]{3,2,1,0:T(8,128)(2,1)}), bf16[8,2,128,512]{3,2,1,0:T(8,128)(2,1)}, u32[]{:S(2)}, u32[]{:S(2)}) async-start(bf16[8,2,128,512]{3,2,1,0:T(8,128)(2,1)} %get-tuple-element.26), calls=%async_computation.1 | async-start | bytes 4194304 | tf_op jit(solution)/shard_map/all_to_all | solution.py:356
  108.6 0.6 collective-permute-done.12
  109.2 14.0 %collective-permute-done.13 = bf16[4,320,512]{2,1,0:T(8,128)(2,1)} collective-permute-done((bf16[4,320,512]{2,1,0:T(8,128)(2,1)S(1)}, bf16[4,320,512]{2,1,0:T(8,128)(2,1)}, u32[]{:S(2)}, u32[]{:S(2)}) %collective-permute-start.13) | collective-permute-done | bytes 1310752 | tf_op jit(solution)/shard_map/ppermute | solution.py:35
  123.2 1.4 fusion.8
  124.6 2.0 %collective-permute-start.15 = (bf16[320,512]{1,0:T(8,128)(2,1)S(1)}, bf16[320,512]{1,0:T(8,128)(2,1)S(1)}, u32[]{:S(2)}, u32[]{:S(2)}) collective-permute-start(bf16[320,512]{1,0:T(8,128)(2,1)S(1)} %fusion.8), channel_id=1, source_target_pairs={{0,2},{1,3},{2,0},{3,1},{4,6},{5,7},{6,4},{7,5},{8,10},{9,11},{10,... | collective-permute-start | bytes 983048 | tf_op jit(solution)/shard_map/ppermute | solution.py:35
  126.6 1.4 fusion.10
  127.9 0.6 collective-permute-start.17
  128.5 1.4 fusion.9
  129.9 0.5 collective-permute-start.16
  130.4 2.3 %collective-permute-done.15 = bf16[320,512]{1,0:T(8,128)(2,1)S(1)} collective-permute-done((bf16[320,512]{1,0:T(8,128)(2,1)S(1)}, bf16[320,512]{1,0:T(8,128)(2,1)S(1)}, u32[]{:S(2)}, u32[]{:S(2)}) %collective-permute-start.15) | collective-permute-done | bytes 327712 | tf_op jit(solution)/shard_map/ppermute | solution.py:35
  132.6 3.4 %collective-permute-done.17 = bf16[320,512]{1,0:T(8,128)(2,1)S(1)} collective-permute-done((bf16[320,512]{1,0:T(8,128)(2,1)S(1)}, bf16[320,512]{1,0:T(8,128)(2,1)S(1)}, u32[]{:S(2)}, u32[]{:S(2)}) %collective-permute-start.17) | collective-permute-done | bytes 327712 | tf_op jit(solution)/shard_map/ppermute | solution.py:35
  136.2 1.5 fusion.5
  137.7 2.7 %collective-permute-start.20 = (bf16[320,512]{1,0:T(8,128)(2,1)S(1)}, bf16[320,512]{1,0:T(8,128)(2,1)S(1)}, u32[]{:S(2)}, u32[]{:S(2)}) collective-permute-start(bf16[320,512]{1,0:T(8,128)(2,1)S(1)} %fusion.5), channel_id=1, source_target_pairs={{0,96},{16,112},{32,64},{48,80},{64,32},{80,48},{96,0},{112,16},{1... | collective-permute-start | bytes 983048 | tf_op jit(solution)/shard_map/ppermute | solution.py:39
  140.4 1.3 collective-permute-start.18
  141.7 1.3 copy_bitcast_fusion
  143.0 1.3 slice_bitcast_fusion.1
  144.8 1.5 copy.13
  146.3 0.4 collective-permute-done.19
  146.6 6.5 %collective-permute-done.18 = bf16[320,512]{1,0:T(8,128)(2,1)S(1)} collective-permute-done((bf16[320,512]{1,0:T(8,128)(2,1)S(1)}, bf16[320,512]{1,0:T(8,128)(2,1)S(1)}, u32[]{:S(2)}, u32[]{:S(2)}) %collective-permute-start.18) | collective-permute-done | bytes 327712 | tf_op jit(solution)/shard_map/ppermute | solution.py:39
  153.3 4.3 %collective-permute-start.21 = (f32[320,512]{1,0:T(8,128)S(1)}, f32[320,512]{1,0:T(8,128)S(1)}, u32[]{:S(2)}, u32[]{:S(2)}) collective-permute-start(f32[320,512]{1,0:T(8,128)S(1)} %add_multiply_fusion), channel_id=1, source_target_pairs={{0,16},{16,0},{32,48},{48,32},{64,80},{80,64},{96,112},{112,96},{1... | collective-permute-start | bytes 1966088 | tf_op jit(solution)/shard_map/ppermute | solution.py:43
  157.6 1.7 %collective-permute-done.21 = f32[320,512]{1,0:T(8,128)S(1)} collective-permute-done((f32[320,512]{1,0:T(8,128)S(1)}, f32[320,512]{1,0:T(8,128)S(1)}, u32[]{:S(2)}, u32[]{:S(2)}) %collective-permute-start.21) | collective-permute-done | bytes 655392 | tf_op jit(solution)/shard_map/ppermute | solution.py:43
  159.6 1.2 pad_maximum_fusion.3
  (54 shorter events, 3.4 us)
Async XLA Ops:
  1.8 8.6 %copy-start.6 = (f32[1,128]{1,0:T(1,128)S(1)}, f32[1,128]{1,0:T(1,128)}, u32[]{:S(2)}) copy-start(f32[1,128]{1,0:T(1,128)} %group_sums.1) | copy-start | bytes 1540
  1.8 7.3 %collective-permute-start.3 = (f32[1,128]{1,0:T(1,128)}, f32[1,128]{1,0:T(1,128)S(1)}, u32[]{:S(2)}, u32[]{:S(2)}) collective-permute-start(f32[1,128]{1,0:T(1,128)} %group_sums.1), channel_id=1, source_target_pairs={{0,12},{1,13},{2,14},{3,15},{4,8},{5,9},{6,10},{7,11},{8,4},{9,5},... | collective-permute-start | bytes 1544 | tf_op jit(solution)/shard_map/ppermute | solution.py:35
  6.4 4.0 %collective-permute-start.2 = (f32[1,128]{1,0:T(1,128)}, f32[1,128]{1,0:T(1,128)S(1)}, u32[]{:S(2)}, u32[]{:S(2)}) collective-permute-start(f32[1,128]{1,0:T(1,128)} %group_sums.1), channel_id=1, source_target_pairs={{0,8},{1,9},{2,10},{3,11},{4,12},{5,13},{6,14},{7,15},{8,0},{9,1},... | collective-permute-start | bytes 1544 | tf_op jit(solution)/shard_map/ppermute | solution.py:35
  6.4 4.0 %collective-permute-start.1 = (f32[1,128]{1,0:T(1,128)}, f32[1,128]{1,0:T(1,128)S(1)}, u32[]{:S(2)}, u32[]{:S(2)}) collective-permute-start(f32[1,128]{1,0:T(1,128)} %group_sums.1), channel_id=1, source_target_pairs={{0,4},{1,5},{2,6},{3,7},{4,0},{5,1},{6,2},{7,3},{8,12},{9,13},{10,... | collective-permute-start | bytes 1544 | tf_op jit(solution)/shard_map/ppermute | solution.py:35
  10.5 11.4 %collective-permute-start.6 = (bf16[336,512]{1,0:T(8,128)(2,1)S(1)}, bf16[336,512]{1,0:T(8,128)(2,1)S(1)}, u32[]{:S(2)}, u32[]{:S(2)}) collective-permute-start(bf16[336,512]{1,0:T(8,128)(2,1)S(1)} %fusion.7), channel_id=1, source_target_pairs={{0,3},{1,2},{2,1},{3,0},{4,7},{5,6},{6,5},{7,4},{8,11},{9,10},{10,... | collective-permute-start | bytes 1032200 | tf_op jit(solution)/shard_map/ppermute | solution.py:35
  13.3 8.7 %collective-permute-start.5 = (bf16[336,512]{1,0:T(8,128)(2,1)S(1)}, bf16[336,512]{1,0:T(8,128)(2,1)S(1)}, u32[]{:S(2)}, u32[]{:S(2)}) collective-permute-start(bf16[336,512]{1,0:T(8,128)(2,1)S(1)} %fusion.7), channel_id=1, source_target_pairs={{0,2},{1,3},{2,0},{3,1},{4,6},{5,7},{6,4},{7,5},{8,10},{9,11},{10,... | collective-permute-start | bytes 1032200 | tf_op jit(solution)/shard_map/ppermute | solution.py:35
  13.7 9.0 %collective-permute-start.4 = (bf16[336,512]{1,0:T(8,128)(2,1)S(1)}, bf16[336,512]{1,0:T(8,128)(2,1)S(1)}, u32[]{:S(2)}, u32[]{:S(2)}) collective-permute-start(bf16[336,512]{1,0:T(8,128)(2,1)S(1)} %fusion.7), channel_id=1, source_target_pairs={{0,1},{1,0},{2,3},{3,2},{4,5},{5,4},{6,7},{7,6},{8,9},{9,8},{10,11... | collective-permute-start | bytes 1032200 | tf_op jit(solution)/shard_map/ppermute | solution.py:35
  22.0 3.8 %copy-start.1 = (bf16[8,128,1024]{2,1,0:T(8,128)(2,1)S(1)}, bf16[8,128,1024]{2,1,0:T(8,128)(2,1)}, u32[]{:S(2)}) copy-start(bf16[8,128,1024]{2,1,0:T(8,128)(2,1)} %param.17) | copy-start | bytes 6291460
  22.8 27.1 %collective-permute-start.7 = (bf16[8,128,5120]{2,1,0:T(8,128)(2,1)}, bf16[8,128,5120]{2,1,0:T(8,128)(2,1)}, u32[]{:S(2)}, u32[]{:S(2)}) collective-permute-start(bf16[8,128,5120]{2,1,0:T(8,128)(2,1)} %own_ref.3), channel_id=1, source_target_pairs={{0,16},{16,0},{32,48},{48,32},{64,80},{80,64},{96,112},{112,96},{1... | collective-permute-start | bytes 31457288 | tf_op jit(solution)/shard_map/ppermute | solution.py:43
  28.2 9.0 %copy-start.2 = (s32[1,8]{1,0:T(1,128)S(1)}, s32[1,8]{1,0:T(1,128)}, u32[]{:S(2)}) copy-start(s32[1,8]{1,0:T(1,128)} %param.13) | copy-start | bytes 100
  28.2 9.0 %copy-start.3 = (s32[8]{0:T(128)S(1)}, s32[8]{0:T(128)}, u32[]{:S(2)}) copy-start(s32[8]{0:T(128)} %param.14) | copy-start | bytes 100
  28.2 9.0 %copy-start.4 = (s32[8]{0:T(128)S(1)}, s32[8]{0:T(128)}, u32[]{:S(2)}) copy-start(s32[8]{0:T(128)} %rewards_ref.1) | copy-start | bytes 100
  28.2 9.0 %copy-start.5 = (s32[8]{0:T(128)S(1)}, s32[8]{0:T(128)}, u32[]{:S(2)}) copy-start(s32[8]{0:T(128)} %groups_ref.1) | copy-start | bytes 100
  28.2 38.1 %all-to-all-start = ((bf16[8,2,144,512]{3,2,1,0:T(8,128)(2,1)}), bf16[8,2,144,512]{3,2,1,0:T(8,128)(2,1)}, u32[]{:S(2)}, u32[]{:S(2)}) async-start(bf16[8,2,144,512]{3,2,1,0:T(8,128)(2,1)} %pad_maximum_fusion), calls=%async_computation | async-start | bytes 4718592 | tf_op jit(solution)/shard_map/all_to_all | solution.py:344
  33.0 16.9 %collective-permute-start.10 = (bf16[1280,512]{1,0:T(8,128)(2,1)S(1)}, bf16[1280,512]{1,0:T(8,128)(2,1)}, u32[]{:S(2)}, u32[]{:S(2)}) collective-permute-start(bf16[1280,512]{1,0:T(8,128)(2,1)S(1)} %pad_maximum_fusion.2.refs_8_), channel_id=1, source_target_pairs={{0,4},{1,5},{2,6},{3,7},{4,0},{5,1},{6,2},{7,3},{8,12},{9,13},{10,... | collective-permute-start | bytes 3932168 | tf_op jit(solution)/shard_map/ppermute | solution.py:35
  33.5 31.1 %collective-permute-start.9 = (bf16[1280,512]{1,0:T(8,128)(2,1)S(1)}, bf16[1280,512]{1,0:T(8,128)(2,1)S(1)}, u32[]{:S(2)}, u32[]{:S(2)}) collective-permute-start(bf16[1280,512]{1,0:T(8,128)(2,1)S(1)} %pad_maximum_fusion.2.refs_8_), channel_id=1, source_target_pairs={{0,12},{1,13},{2,14},{3,15},{4,8},{5,9},{6,10},{7,11},{8,4},{9,5},... | collective-permute-start | bytes 3932168 | tf_op jit(solution)/shard_map/ppermute | solution.py:35
  36.0 30.3 %collective-permute-start.8 = (bf16[1280,512]{1,0:T(8,128)(2,1)S(1)}, bf16[1280,512]{1,0:T(8,128)(2,1)}, u32[]{:S(2)}, u32[]{:S(2)}) collective-permute-start(bf16[1280,512]{1,0:T(8,128)(2,1)S(1)} %pad_maximum_fusion.2.refs_8_), channel_id=1, source_target_pairs={{0,8},{1,9},{2,10},{3,11},{4,12},{5,13},{6,14},{7,15},{8,0},{9,1},... | collective-permute-start | bytes 3932168 | tf_op jit(solution)/shard_map/ppermute | solution.py:35
  37.2 7.6 %collective-permute-start = (s32[4,8]{1,0:T(4,128)S(1)}, s32[4,8]{1,0:T(4,128)S(1)}, u32[]{:S(2)}, u32[]{:S(2)}) collective-permute-start(s32[4,8]{1,0:T(4,128)S(1)} %pad_add_fusion), channel_id=1, source_target_pairs={{0,16},{16,0},{32,48},{48,32},{64,80},{80,64},{96,112},{112,96},{1... | collective-permute-start | bytes 392 | tf_op jit(solution)/shard_map/ppermute | solution.py:43
  44.8 17.2 %collective-permute-start.11 = (f32[1024,128]{1,0:T(8,128)S(1)}, f32[1024,128]{1,0:T(8,128)}, u32[]{:S(2)}, u32[]{:S(2)}) collective-permute-start(f32[1024,128]{1,0:T(8,128)S(1)} %token_scale.1.refs_12_), channel_id=1, source_target_pairs={{0,16},{16,0},{32,48},{48,32},{64,80},{80,64},{96,112},{112,96},{1... | collective-permute-start | bytes 1572872 | tf_op jit(solution)/shard_map/ppermute | solution.py:43
  45.3 21.0 %copy-start = (f32[128]{0:T(128)S(1)}, f32[128]{0:T(128)}, u32[]{:S(2)}) copy-start(f32[128]{0:T(128)} %param.12) | copy-start | bytes 1540
  90.6 18.6 %collective-permute-start.12 = (bf16[4,320,512]{2,1,0:T(8,128)(2,1)}, bf16[4,320,512]{2,1,0:T(8,128)(2,1)}, u32[]{:S(2)}, u32[]{:S(2)}) collective-permute-start(bf16[4,320,512]{2,1,0:T(8,128)(2,1)} %get-tuple-element.29), channel_id=1, source_target_pairs={{0,8},{1,9},{2,10},{3,11},{4,12},{5,13},{6,14},{7,15},{8,0},{9,1},... | collective-permute-start | bytes 3932168 | tf_op jit(solution)/shard_map/ppermute | solution.py:35
  92.2 30.9 %collective-permute-start.13 = (bf16[4,320,512]{2,1,0:T(8,128)(2,1)S(1)}, bf16[4,320,512]{2,1,0:T(8,128)(2,1)}, u32[]{:S(2)}, u32[]{:S(2)}) collective-permute-start(bf16[4,320,512]{2,1,0:T(8,128)(2,1)S(1)} %get-tuple-element.30), channel_id=1, source_target_pairs={{0,12},{1,13},{2,14},{3,15},{4,8},{5,9},{6,10},{7,11},{8,4},{9,5},... | collective-permute-start | bytes 3932168 | tf_op jit(solution)/shard_map/ppermute | solution.py:35
  102.8 20.3 %collective-permute-start.14 = (bf16[4,320,512]{2,1,0:T(8,128)(2,1)}, bf16[4,320,512]{2,1,0:T(8,128)(2,1)}, u32[]{:S(2)}, u32[]{:S(2)}) collective-permute-start(bf16[4,320,512]{2,1,0:T(8,128)(2,1)} %get-tuple-element.31), channel_id=1, source_target_pairs={{0,4},{1,5},{2,6},{3,7},{4,0},{5,1},{6,2},{7,3},{8,12},{9,13},{10,... | collective-permute-start | bytes 3932168 | tf_op jit(solution)/shard_map/ppermute | solution.py:35
  103.2 34.5 %all-to-all-start.1 = ((bf16[8,2,128,512]{3,2,1,0:T(8,128)(2,1)}), bf16[8,2,128,512]{3,2,1,0:T(8,128)(2,1)}, u32[]{:S(2)}, u32[]{:S(2)}) async-start(bf16[8,2,128,512]{3,2,1,0:T(8,128)(2,1)} %get-tuple-element.26), calls=%async_computation.1 | async-start | bytes 4194304 | tf_op jit(solution)/shard_map/all_to_all | solution.py:356
  124.6 8.1 %collective-permute-start.15 = (bf16[320,512]{1,0:T(8,128)(2,1)S(1)}, bf16[320,512]{1,0:T(8,128)(2,1)S(1)}, u32[]{:S(2)}, u32[]{:S(2)}) collective-permute-start(bf16[320,512]{1,0:T(8,128)(2,1)S(1)} %fusion.8), channel_id=1, source_target_pairs={{0,2},{1,3},{2,0},{3,1},{4,6},{5,7},{6,4},{7,5},{8,10},{9,11},{10,... | collective-permute-start | bytes 983048 | tf_op jit(solution)/shard_map/ppermute | solution.py:35
  127.9 8.1 %collective-permute-start.17 = (bf16[320,512]{1,0:T(8,128)(2,1)S(1)}, bf16[320,512]{1,0:T(8,128)(2,1)S(1)}, u32[]{:S(2)}, u32[]{:S(2)}) collective-permute-start(bf16[320,512]{1,0:T(8,128)(2,1)S(1)} %fusion.10), channel_id=1, source_target_pairs={{0,3},{1,2},{2,1},{3,0},{4,7},{5,6},{6,5},{7,4},{8,11},{9,10},{10,... | collective-permute-start | bytes 983048 | tf_op jit(solution)/shard_map/ppermute | solution.py:35
  129.9 6.3 %collective-permute-start.16 = (bf16[320,512]{1,0:T(8,128)(2,1)S(1)}, bf16[320,512]{1,0:T(8,128)(2,1)S(1)}, u32[]{:S(2)}, u32[]{:S(2)}) collective-permute-start(bf16[320,512]{1,0:T(8,128)(2,1)S(1)} %fusion.9), channel_id=1, source_target_pairs={{0,1},{1,0},{2,3},{3,2},{4,5},{5,4},{6,7},{7,6},{8,9},{9,8},{10,11... | collective-permute-start | bytes 983048 | tf_op jit(solution)/shard_map/ppermute | solution.py:35
  137.7 8.5 %collective-permute-start.20 = (bf16[320,512]{1,0:T(8,128)(2,1)S(1)}, bf16[320,512]{1,0:T(8,128)(2,1)S(1)}, u32[]{:S(2)}, u32[]{:S(2)}) collective-permute-start(bf16[320,512]{1,0:T(8,128)(2,1)S(1)} %fusion.5), channel_id=1, source_target_pairs={{0,96},{16,112},{32,64},{48,80},{64,32},{80,48},{96,0},{112,16},{1... | collective-permute-start | bytes 983048 | tf_op jit(solution)/shard_map/ppermute | solution.py:39
  140.4 6.2 %collective-permute-start.19 = (bf16[320,512]{1,0:T(8,128)(2,1)S(1)}, bf16[320,512]{1,0:T(8,128)(2,1)S(1)}, u32[]{:S(2)}, u32[]{:S(2)}) collective-permute-start(bf16[320,512]{1,0:T(8,128)(2,1)S(1)} %fusion.5), channel_id=1, source_target_pairs={{0,32},{16,48},{32,0},{48,16},{64,96},{80,112},{96,64},{112,80},{1... | collective-permute-start | bytes 983048 | tf_op jit(solution)/shard_map/ppermute | solution.py:39
  140.4 12.7 %collective-permute-start.18 = (bf16[320,512]{1,0:T(8,128)(2,1)S(1)}, bf16[320,512]{1,0:T(8,128)(2,1)S(1)}, u32[]{:S(2)}, u32[]{:S(2)}) collective-permute-start(bf16[320,512]{1,0:T(8,128)(2,1)S(1)} %fusion.5), channel_id=1, source_target_pairs={{0,64},{16,80},{32,96},{48,112},{64,0},{80,16},{96,32},{112,48},{1... | collective-permute-start | bytes 983048 | tf_op jit(solution)/shard_map/ppermute | solution.py:39
  153.3 6.0 %collective-permute-start.21 = (f32[320,512]{1,0:T(8,128)S(1)}, f32[320,512]{1,0:T(8,128)S(1)}, u32[]{:S(2)}, u32[]{:S(2)}) collective-permute-start(f32[320,512]{1,0:T(8,128)S(1)} %add_multiply_fusion), channel_id=1, source_target_pairs={{0,16},{16,0},{32,48},{48,32},{64,80},{80,64},{96,112},{112,96},{1... | collective-permute-start | bytes 1966088 | tf_op jit(solution)/shard_map/ppermute | solution.py:43
